TPU v7x, 128 devices: a whole 4x4x4 slice. The times are simulated.
128 devices in a mesh: replica: 4 (over z), fsdp: 32 (over x, y, core).
Axes of the slice: x: 4, y: 4, z: 4, core: 2. Of those that a mesh axis runs over, the one named last changes fastest.
Arguments:
- weight: float32 [4096, 128, 128], P('fsdp'), may hold values from -6 to 6
- moment: float32 [4096, 128, 128], P('fsdp'), may hold values from -6 to 6
- base_codes: int32 [4096, 128, 128], P('fsdp'), may hold values from -8 to 7
- base_scale: float32 [4096], P('fsdp'), may hold values from 0.05 to 0.2
- weight_mask: int32 [4096], P('fsdp'), may hold values 0 or 1
- moment_mask: int32 [4096], P('fsdp'), may hold values 0 or 1
- writer: int32 [4096, 1], P('fsdp'), may hold values from 0 to 31; in each aligned block of 128 rows (0 to 127, 128 to 255, ...) at most 8 rows name the same one
Outputs:
- written_weight: bfloat16 [1024, 8, 128, 128], P('fsdp')
- written_moment: bfloat16 [1024, 8, 128, 128], P('fsdp')
- written_scales: bfloat16 [2, 1024, 8], P(None, 'fsdp')
- refreshed: bfloat16 [4096, 128, 128], P('fsdp')
Inputs may be any that keep to these rules, and one draw needn't show every extreme that they name: No writer is named by more than 8 blocks of one fsdp shard.
All inputs are finite; a program needn't handle non-finite values. Where the computation divides by a largest or mean magnitude, that divisor is 1e-20 or more. No bound on the sum of `weight_mask` or of `moment_mask` on one device may be relied on, other than what follows from the above.
Results may differ from a plain program's by a relative error of at most 0.013.
Values may be sent and summed in bfloat16 or wider, within the bound.
No kernel may reach another device: no remote copies, remote signals or barrier semaphores. Data moves between devices by JAX's collectives and lax.ppermute only.
A program may use at most 192 MiB of HBM per device.

v0:
```python
import jax
import jax.numpy as jnp
from jax import lax
from jax.sharding import PartitionSpec as P

EPSILON = 1e-06


def compress(weights_in, moment_in, codes_in, scale_in, wmask_in, mmask_in):
    base_value = codes_in.astype(jnp.float32) * scale_in[:, None, None]
    residual = weights_in - base_value
    keep_weight = wmask_in.astype(jnp.float32)
    keep_moment = (wmask_in * mmask_in).astype(jnp.float32)
    scale_weight = (jnp.max(jnp.abs(residual), axis=(1, 2)) + EPSILON).astype(jnp.bfloat16)
    scale_moment = (jnp.max(jnp.abs(moment_in), axis=(1, 2)) + EPSILON).astype(jnp.bfloat16)
    coded_weight = (
        residual / scale_weight.astype(jnp.float32)[:, None, None] * keep_weight[:, None, None]
    ).astype(jnp.bfloat16)
    coded_moment = (
        moment_in / scale_moment.astype(jnp.float32)[:, None, None] * keep_moment[:, None, None]
    ).astype(jnp.bfloat16)
    refreshed = (
        base_value
        + coded_weight.astype(jnp.float32) * scale_weight.astype(jnp.float32)[:, None, None]
    ).astype(jnp.bfloat16)
    return (coded_weight, coded_moment, scale_weight, scale_moment, refreshed)


def on_device(weight, moment, base_codes, base_scale, weight_mask, moment_mask, writer):
    writers = lax.axis_size("fsdp")
    copies = lax.axis_size("replica")
    blocks_here = weight.shape[0]
    width = weight.shape[1]
    capacity = copies * max(1, 2 * blocks_here // (writers * copies))
    target = writer[:, 0]
    onehot = (target[:, None] == jnp.arange(writers, dtype=jnp.int32)[None, :]).astype(jnp.int32)
    before = jnp.cumsum(onehot, axis=0) - onehot
    slot_rank = jnp.sum(before * onehot, axis=1)
    position = target * capacity + slot_rank

    def blank(values, filled):
        shape = (filled.shape[0],) + (1,) * (values.ndim - 1)
        return jnp.where(filled.reshape(shape), values, jnp.zeros_like(values))

    coded_weight, coded_moment, scale_weight, scale_moment, refreshed = compress(
        weight, moment, base_codes, base_scale, weight_mask, moment_mask
    )
    wanted = (
        jnp.arange(writers, dtype=jnp.int32)[:, None] * capacity
        + jnp.arange(capacity, dtype=jnp.int32)[None, :]
    )
    matches = (position[:, None] == wanted.reshape(-1)[None, :]).astype(jnp.int32)
    source_block = jnp.sum(jnp.arange(blocks_here, dtype=jnp.int32)[:, None] * matches, axis=0)
    filled = jnp.sum(matches, axis=0) > 0
    source_block, filled = (source_block, filled)
    send_weight = blank(coded_weight[source_block], filled).reshape(writers, capacity, width, width)
    send_moment = blank(coded_moment[source_block], filled).reshape(writers, capacity, width, width)
    send_sw = blank(scale_weight[source_block], filled).reshape(writers, capacity)
    send_sm = blank(scale_moment[source_block], filled).reshape(writers, capacity)
    got_weight, got_moment, got_sw, got_sm = (
        lax.all_to_all(send_weight, "fsdp", split_axis=0, concat_axis=0, tiled=True),
        lax.all_to_all(send_moment, "fsdp", split_axis=0, concat_axis=0, tiled=True),
        lax.all_to_all(send_sw, "fsdp", split_axis=0, concat_axis=0, tiled=True),
        lax.all_to_all(send_sm, "fsdp", split_axis=0, concat_axis=0, tiled=True),
    )
    written_scales = jnp.stack([got_sw, got_sm], axis=0)
    return (got_weight, got_moment, written_scales, refreshed)


def solution(mesh):
    placed = (
        P("fsdp", None, None),
        P("fsdp", None, None),
        P("fsdp", None, None),
        P("fsdp"),
        P("fsdp"),
        P("fsdp"),
        P("fsdp", None),
    )
    return jax.shard_map(
        on_device,
        mesh=mesh,
        in_specs=placed,
        out_specs=(
            P("fsdp", None, None, None),
            P("fsdp", None, None, None),
            P(None, "fsdp", None),
            P("fsdp", None, None),
        ),
        check_vma=False,
    )
```

profile of v0, /device:TPU:44, one launch (start us, length us, event | category | flops | bytes accessed | tf_op | source)
XLA Modules:
  0.0 334.5 jit_solution(9005255124326231272)
XLA Ops:
  0.6 0.0 copy-start
  0.7 4.6 %abs_reduce_fusion = f32[128]{0:T(128)S(1)} fusion(f32[128,128,128]{2,1,0:T(8,128)} %param.8), kind=kLoop, calls=%fused_computation.6 | loop fusion | flops 4194176 | bytes 8389120 | tf_op jit(solution)/shard_map/reduce_max | solution.py:15
  5.2 1.2 copy-done
  6.4 5.4 %abs_reduce_fusion.1 = f32[128]{0:T(128)S(1)} fusion(f32[128,128,128]{2,1,0:T(8,128)S(1)} %copy-done, f32[128]{0:T(128)S(1)} %copy-done.2, s32[128,128,128]{2,1,0:T(8,128)} %param.9), kind=kLoop, calls=%fused_computation.8 | loop fusion | flops 10485632 | bytes 16778240 | tf_op jit(solution)/shard_map/reduce_max | solution.py:14
  11.8 0.1 iota_add_fusion
  11.9 0.1 add.58
  12.0 0.1 fusion.3
  12.1 0.2 reduce_window_sum.11
  12.3 0.2 select_reduce_fusion
  12.5 0.1 fusion.1
  12.6 1.9 gather_fusion.3
  14.5 1.9 gather_fusion.2
  16.4 0.7 select_n.59
  17.1 7.5 %all-to-all-start.3 = ((bf16[32,1,8]{2,1,0:T(2,128)(2,1)}), bf16[32,1,8]{2,1,0:T(2,128)(2,1)S(1)}, u32[]{:S(2)}, u32[]{:S(2)}) async-start(bf16[32,1,8]{2,1,0:T(2,128)(2,1)} %select_n.59), calls=%async_computation.3 | async-start | bytes 32768 | tf_op jit(solution)/shard_map/all_to_all | solution.py:64
  24.6 9.7 %add_convert_fusion = (bf16[128,128,128]{2,1,0:T(8,128)(2,1)}, bf16[128,128,128]{2,1,0:T(8,128)(2,1)}) fusion(s32[128,128,128]{2,1,0:T(8,128)} %param.9, f32[128]{0:T(128)S(1)} %get-tuple-element.21, f32[128]{0:T(128)S(1)} %copy-done.2, f32[128]{0:T(128)S(1)} %get-tuple-element.19, f32[128,128,128]{2,1,0:T(8,128)} %param.7), kind=kLoop, calls=%fused_computation.4 | loop fusion | flops 20971520 | bytes 25167360 | tf_op jit(solution)/shard_map/convert_element_type | solution.py:25
  34.4 5.3 %multiply_convert_fusion = bf16[128,128,128]{2,1,0:T(8,128)(2,1)} fusion(f32[128,128,128]{2,1,0:T(8,128)} %param.8, f32[128]{0:T(128)S(1)} %get-tuple-element.18, f32[128]{0:T(128)S(1)} %get-tuple-element.17), kind=kLoop, calls=%fused_computation.5 | loop fusion | flops 6291456 | bytes 12583936 | tf_op jit(solution)/shard_map/convert_element_type | solution.py:21
  39.7 0.1 gt.25
  39.8 0.7 select_n.58
  40.5 10.8 %gather_fusion.1 = bf16[256,128,128]{2,1,0:T(8,128)(2,1)} fusion(bf16[128,128,128]{2,1,0:T(8,128)(2,1)} %multiply_convert_fusion, s32[1024]{0:T(1024)S(1)} %pad_clamp_fusion), kind=kCustom, calls=%fused_computation.1 | custom fusion | bytes 16778240 | tf_op jit(solution)/shard_map/gather | solution.py:57
  51.3 10.8 %gather_fusion = bf16[256,128,128]{2,1,0:T(8,128)(2,1)} fusion(bf16[128,128,128]{2,1,0:T(8,128)(2,1)} %get-tuple-element.11, s32[1024]{0:T(1024)S(1)} %pad_clamp_fusion), kind=kCustom, calls=%fused_computation | custom fusion | bytes 16778240 | tf_op jit(solution)/shard_map/gather | solution.py:56
  62.2 0.0 all-to-all-done.3
  62.2 7.5 %all-to-all-start.2 = ((bf16[32,1,8]{2,1,0:T(2,128)(2,1)}), bf16[32,1,8]{2,1,0:T(2,128)(2,1)S(1)}, u32[]{:S(2)}, u32[]{:S(2)}) async-start(bf16[32,1,8]{2,1,0:T(2,128)(2,1)} %select_n.58), calls=%async_computation.2 | async-start | bytes 32768 | tf_op jit(solution)/shard_map/all_to_all | solution.py:63
  69.7 11.6 %broadcast_select_fusion = (bf16[32,8,128,128]{3,2,1,0:T(8,128)(2,1)}, bf16[32,8,128,128]{3,2,1,0:T(8,128)(2,1)}) fusion(bf16[32,8,128,128]{3,2,1,0:T(8,128)(2,1)} %bitcast.13, pred[32,8]{1,0:T(8,128)(4,1)S(1)} %gt.25, bf16[32,8,128,128]{3,2,1,0:T(8,128)(2,1)} %bitcast.14), kind=kLoop, calls=%fused_computation.10 | loop fusion | flops 8388608 | bytes 33554688 | tf_op jit(solution)/shard_map/jit(_where)/select_n | solution.py:43
  81.3 0.0 all-to-all-done.2
  81.3 99.9 %all_to_all.22 = bf16[32,8,128,128]{3,2,1,0:T(8,128)(2,1)} all-to-all(bf16[32,8,128,128]{3,2,1,0:T(8,128)(2,1)} %get-tuple-element.14), channel_id=1, replica_groups=mesh['replica'=4,'fsdp'=32] {'fsdp'}, dimensions={0} | all-to-all | bytes 16777216 | tf_op jit(solution)/shard_map/all_to_all | solution.py:62
  181.2 8.0 %all-to-all-start = ((bf16[32,8,128,128]{3,2,1,0:T(8,128)(2,1)}), bf16[32,8,128,128]{3,2,1,0:T(8,128)(2,1)}, u32[]{:S(2)}, u32[]{:S(2)}) async-start(bf16[32,8,128,128]{3,2,1,0:T(8,128)(2,1)} %get-tuple-element.15), calls=%async_computation | async-start | bytes 16777216 | tf_op jit(solution)/shard_map/all_to_all | solution.py:61
  189.2 0.1 copy.23
  189.3 0.1 copy.21
  189.3 0.6 pad_maximum_fusion
  190.0 123.5 %all-to-all-done = bf16[32,8,128,128]{3,2,1,0:T(8,128)(2,1)} async-done(((bf16[32,8,128,128]{3,2,1,0:T(8,128)(2,1)}), bf16[32,8,128,128]{3,2,1,0:T(8,128)(2,1)}, u32[]{:S(2)}, u32[]{:S(2)}) %all-to-all-start) | async-done | bytes 8388640 | tf_op jit(solution)/shard_map/all_to_all | solution.py:61
  313.5 10.5 %copy.26 = bf16[32,8,128,128]{3,2,1,0:T(8,128)(2,1)} copy(bf16[32,8,128,128]{3,2,1,0:T(8,128)(2,1)} %all-to-all-done) | data formatting | bytes 16777216
  324.0 10.5 %copy.27 = bf16[32,8,128,128]{3,2,1,0:T(8,128)(2,1)} copy(bf16[32,8,128,128]{3,2,1,0:T(8,128)(2,1)} %all_to_all.22) | data formatting | bytes 16777216
  (17 shorter events, 0.1 us)
Async XLA Ops:
  0.6 4.6 %copy-start.2 = (f32[128]{0:T(128)S(1)}, f32[128]{0:T(128)}, u32[]{:S(2)}) copy-start(f32[128]{0:T(128)} %param.10) | copy-start | bytes 1540
  0.6 5.8 %copy-start = (f32[128,128,128]{2,1,0:T(8,128)S(1)}, f32[128,128,128]{2,1,0:T(8,128)}, u32[]{:S(2)}) copy-start(f32[128,128,128]{2,1,0:T(8,128)} %param.7) | copy-start | bytes 25165828
  6.4 5.6 %copy-start.1 = (s32[128,1]{0,1:T(1,128)S(1)}, s32[128,1]{0,1:T(1,128)}, u32[]{:S(2)}) copy-start(s32[128,1]{0,1:T(1,128)} %param.13) | copy-start | bytes 1540
  6.4 18.2 %copy-start.3 = (s32[128]{0:T(128)S(1)}, s32[128]{0:T(128)}, u32[]{:S(2)}) copy-start(s32[128]{0:T(128)} %param.11) | copy-start | bytes 1540
  6.4 18.2 %copy-start.4 = (s32[128]{0:T(128)S(1)}, s32[128]{0:T(128)}, u32[]{:S(2)}) copy-start(s32[128]{0:T(128)} %param.12) | copy-start | bytes 1540
  17.1 45.1 %all-to-all-start.3 = ((bf16[32,1,8]{2,1,0:T(2,128)(2,1)}), bf16[32,1,8]{2,1,0:T(2,128)(2,1)S(1)}, u32[]{:S(2)}, u32[]{:S(2)}) async-start(bf16[32,1,8]{2,1,0:T(2,128)(2,1)} %select_n.59), calls=%async_computation.3 | async-start | bytes 32768 | tf_op jit(solution)/shard_map/all_to_all | solution.py:64
  62.2 19.1 %all-to-all-start.2 = ((bf16[32,1,8]{2,1,0:T(2,128)(2,1)}), bf16[32,1,8]{2,1,0:T(2,128)(2,1)S(1)}, u32[]{:S(2)}, u32[]{:S(2)}) async-start(bf16[32,1,8]{2,1,0:T(2,128)(2,1)} %select_n.58), calls=%async_computation.2 | async-start | bytes 32768 | tf_op jit(solution)/shard_map/all_to_all | solution.py:63
  181.2 132.3 %all-to-all-start = ((bf16[32,8,128,128]{3,2,1,0:T(8,128)(2,1)}), bf16[32,8,128,128]{3,2,1,0:T(8,128)(2,1)}, u32[]{:S(2)}, u32[]{:S(2)}) async-start(bf16[32,8,128,128]{3,2,1,0:T(8,128)(2,1)} %get-tuple-element.15), calls=%async_computation | async-start | bytes 16777216 | tf_op jit(solution)/shard_map/all_to_all | solution.py:61
where the time goes:
time: 335 us
  waiting for transfers between devices  124 us (37%)
  blocking collectives  99.9 us (30%)
  local copies, waits for them, and re-layouts  49.4 us (15%)
  other arithmetic  37.9 us (11%)
  starting transfers between devices  23 us (7%)
    all_to_all x1, waiting for transfers between devices, on_device(): lax.all_to_all(send_weight, 'fsdp', split_axis=0, concat_axis=0, tiled=True)  124 us
    all_to_all x1, blocking collectives, on_device(): lax.all_to_all(send_moment, 'fsdp', split_axis=0, concat_axis=0, tiled=True)  99.9 us
    unnamed x12, local copies, waits for them, and re-layouts  22.2 us
    select_n x3, other arithmetic, blank(): return jnp.where(filled.reshape(shape), values, jnp.zeros_like(values))  11.6 us
    gather x1, local copies, waits for them, and re-layouts, on_device(): coded_moment[source_block]  10.8 us
    gather x1, local copies, waits for them, and re-layouts, on_device(): coded_weight[source_block]  10.8 us
    convert_element_type x1, other arithmetic, compress(): refreshed = (base_value + coded_weight.astype(jnp.float32) * scale_weight...  9.75 us
    all_to_all x1, starting transfers between devices, on_device(): lax.all_to_all(send_weight, 'fsdp', split_axis=0, concat_axis=0, tiled=True)  7.96 us
  transfers between devices with their start and end apart: 3, of which 1 were waited for; matrix products, arithmetic and copies ran while one was open for 15% of the time, Pallas kernels for 0%

commit v1 on v0

v1 whole, which is shorter than its diff:
```python
import functools

import jax
import jax.numpy as jnp
from jax import lax
from jax.experimental import pallas as pl
from jax.experimental.pallas import tpu as pltpu
from jax.sharding import PartitionSpec as P

EPSILON = 1e-06
WRITERS = 32
CAP = 8
GROUP = 8
ROWS = 32
VMEM = 60 * 1024 * 1024

SLOTS_MOMENT = (3, 3, 2)
SLOTS_WEIGHT = (3, 2, 3)


def start_map(step, blocks, slot_of, count, coded):
    @pl.when(step == 0)
    def _():
        def clear(i, carry):
            slot_of[i] = blocks
            return carry

        def clear_count(i, carry):
            count[i] = 0
            return carry

        lax.fori_loop(0, WRITERS * CAP, clear, 0, unroll=8)
        lax.fori_loop(0, WRITERS, clear_count, 0, unroll=8)
        coded[blocks] = jnp.zeros(coded.shape[1:], coded.dtype)


def note_block(block, writer, slot_of, count):
    target = writer[block]
    rank = count[target]
    count[target] = rank + 1
    slot_of[target * CAP + rank] = block


def scale_of(values):
    top = jnp.max(jnp.max(jnp.abs(values), axis=0, keepdims=True), axis=1, keepdims=True)
    top = jnp.broadcast_to(top + EPSILON, (8, 128))
    return top.astype(jnp.bfloat16).astype(jnp.float32)


def place(step, steps, replica, slots, slot_of, coded, first, second, whole):
    @pl.when(step == steps - 1)
    def _():
        rows = pl.ds(pl.multiple_of(replica[0] * ROWS, ROWS), ROWS)
        n_first, n_second, n_whole = slots

        def one(w, carry):
            for k in range(n_first):
                first[w * n_first + k] = coded[slot_of[w * CAP + k], rows, :]
            for k in range(n_second):
                second[w * n_second + k] = coded[slot_of[w * CAP + n_first + k], rows, :]
            for k in range(n_whole):
                whole[w * n_whole + k] = coded[slot_of[w * CAP + n_first + n_second + k]]
            return carry

        lax.fori_loop(0, WRITERS, one, 0, unroll=2)


def moment_kernel(blocks, slots, replica, writer, weight_mask, moment_mask, moment, first, second, whole, scales, coded, slot_of, count):
    step = pl.program_id(0)
    start_map(step, blocks, slot_of, count, coded)
    for i in range(GROUP):
        block = step * GROUP + i
        note_block(block, writer, slot_of, count)
        keep = (weight_mask[block] * moment_mask[block]).astype(jnp.float32)
        values = moment[i]
        scale = scale_of(values)
        scales[pl.ds(i, 1), :] = scale[0:1, :]
        coded[block] = (values * (keep / scale)[0:1, :]).astype(jnp.bfloat16)
    place(step, blocks // GROUP, replica, slots, slot_of, coded, first, second, whole)


def weight_kernel(
    blocks, slots, replica, writer, weight_mask, base_scale, weight, codes, first, second, whole, scales, refreshed, coded, slot_of, count
):
    step = pl.program_id(0)
    start_map(step, blocks, slot_of, count, coded)
    for i in range(GROUP):
        block = step * GROUP + i
        note_block(block, writer, slot_of, count)
        keep = weight_mask[block].astype(jnp.float32)
        base = codes[i].astype(jnp.float32) * base_scale[block]
        values = weight[i] - base
        scale = scale_of(values)
        scales[pl.ds(i, 1), :] = scale[0:1, :]
        rounded = (values * (keep / scale)[0:1, :]).astype(jnp.bfloat16)
        coded[block] = rounded
        refreshed[i] = (base + rounded.astype(jnp.float32) * scale[0:1, :]).astype(jnp.bfloat16)
    place(step, blocks // GROUP, replica, slots, slot_of, coded, first, second, whole)


def compress_call(kernel, slots, scalars, arrays, refresh, cost):
    blocks, width = arrays[0].shape[0], arrays[0].shape[1]
    steps = blocks // GROUP
    bf16 = jnp.bfloat16
    shapes = [
        jax.ShapeDtypeStruct((WRITERS * slots[0], ROWS, width), bf16),
        jax.ShapeDtypeStruct((WRITERS * slots[1], ROWS, width), bf16),
        jax.ShapeDtypeStruct((WRITERS * slots[2], width, width), bf16),
        jax.ShapeDtypeStruct((blocks, 128), jnp.float32),
    ]
    specs = [pl.BlockSpec(s.shape, lambda i, *_: (0, 0, 0)) for s in shapes[:3]]
    specs.append(pl.BlockSpec((GROUP, 128), lambda i, *_: (i, 0)))
    moving = pl.BlockSpec((GROUP, width, width), lambda i, *_: (i, 0, 0))
    if refresh:
        shapes.append(jax.ShapeDtypeStruct((blocks, width, width), bf16))
        specs.append(moving)
    return pl.pallas_call(
        functools.partial(kernel, blocks, slots),
        grid_spec=pltpu.PrefetchScalarGridSpec(
            num_scalar_prefetch=len(scalars),
            grid=(steps,),
            in_specs=[moving] * len(arrays),
            out_specs=specs,
            scratch_shapes=[
                pltpu.VMEM((blocks + 1, width, width), bf16),
                pltpu.SMEM((WRITERS * CAP,), jnp.int32),
                pltpu.SMEM((WRITERS,), jnp.int32),
            ],
        ),
        out_shape=shapes,
        compiler_params=pltpu.CompilerParams(dimension_semantics=("arbitrary",), vmem_limit_bytes=VMEM),
        cost_estimate=pl.CostEstimate(flops=cost[0], bytes_accessed=cost[1], transcendentals=0),
    )(*scalars, *arrays)


SOURCES = 4


def unpack_kernel(slots, replica, *refs):
    quarters, whole, out = (refs[0:4], refs[4:8]), refs[8], refs[9]
    for turn in range(4):
        rows = pl.ds(pl.multiple_of(lax.rem(replica[0] + turn, 4) * ROWS, ROWS), ROWS)
        for s in range(SOURCES):
            for k in range(slots[0]):
                out[s * CAP + k, rows, :] = quarters[0][turn][s * slots[0] + k]
            for k in range(slots[1]):
                out[s * CAP + slots[0] + k, rows, :] = quarters[1][turn][s * slots[1] + k]
    for s in range(SOURCES):
        for k in range(slots[2]):
            out[s * CAP + slots[0] + slots[1] + k] = whole[s * slots[2] + k]


def unpack_call(slots, replica, first, second, whole):
    width = whole.shape[-1]

    def spec(n, rows):
        return pl.BlockSpec((SOURCES * n, rows, width), lambda i, *_: (i, 0, 0))

    return pl.pallas_call(
        functools.partial(unpack_kernel, slots),
        grid_spec=pltpu.PrefetchScalarGridSpec(
            num_scalar_prefetch=1,
            grid=(WRITERS // SOURCES,),
            in_specs=[spec(slots[0], ROWS)] * 4 + [spec(slots[1], ROWS)] * 4 + [spec(slots[2], width)],
            out_specs=spec(CAP, width),
        ),
        out_shape=jax.ShapeDtypeStruct((WRITERS * CAP, width, width), jnp.bfloat16),
        compiler_params=pltpu.CompilerParams(dimension_semantics=("arbitrary",), vmem_limit_bytes=VMEM),
        cost_estimate=pl.CostEstimate(flops=0, bytes_accessed=1 << 24, transcendentals=0),
    )(replica, *first, *second, whole)


def regroup(values):
    return lax.all_to_all(values, "fsdp", split_axis=0, concat_axis=0, tiled=True)


def upward(values):
    return lax.ppermute(values, "replica", [(i, (i + 1) % 4) for i in range(4)])


def downward(values):
    return lax.ppermute(values, "replica", [(i, (i - 1) % 4) for i in range(4)])


def gather_rows(first, second):
    first_up, first_down = upward(first), downward(first)
    second_up, second_down = upward(second), downward(second)
    return (
        (first, first_down, upward(first_up), first_up),
        (second, second_down, downward(second_down), second_up),
    )


def on_device(weight, moment, base_codes, base_scale, weight_mask, moment_mask, writer):
    blocks, width = weight.shape[0], weight.shape[1]
    target = writer[:, 0]
    replica = lax.axis_index("replica").astype(jnp.int32).reshape(1)
    m_first, m_second, m_whole, m_scales = compress_call(
        moment_kernel, SLOTS_MOMENT, (replica, target, weight_mask, moment_mask), (moment,), False, (10 << 20, 12 << 20)
    )
    w_first, w_second, w_whole, w_scales, refreshed = compress_call(
        weight_kernel, SLOTS_WEIGHT, (replica, target, weight_mask, base_scale), (weight, base_codes), True, (20 << 20, 24 << 20)
    )
    m_first, m_second = regroup(m_first), regroup(m_second)
    w_first, w_second = regroup(w_first), regroup(w_second)
    m_whole, w_whole = regroup(m_whole), regroup(w_whole)
    m_parts = gather_rows(m_first, m_second)
    w_parts = gather_rows(w_first, w_second)

    onehot = (target[:, None] == jnp.arange(WRITERS, dtype=jnp.int32)[None, :]).astype(jnp.int32)
    rank = jnp.sum((jnp.cumsum(onehot, axis=0) - onehot) * onehot, axis=1)
    slot = target * CAP + rank
    matches = slot[:, None] == jnp.arange(WRITERS * CAP, dtype=jnp.int32)[None, :]
    by_slot = [jnp.sum(jnp.where(matches, s[:, 0:1], 0.0), axis=0).reshape(WRITERS, CAP) for s in (w_scales, m_scales)]
    got_scales = regroup(jnp.concatenate(by_slot, axis=1).astype(jnp.bfloat16))
    written_scales = jnp.transpose(got_scales.reshape(WRITERS, 2, CAP), (1, 0, 2))

    written_moment = unpack_call(SLOTS_MOMENT, replica, *m_parts, m_whole)
    written_weight = unpack_call(SLOTS_WEIGHT, replica, *w_parts, w_whole)
    shape = (WRITERS, CAP, width, width)
    return written_weight.reshape(shape), written_moment.reshape(shape), written_scales, refreshed


def solution(mesh):
    placed = (
        P("fsdp", None, None),
        P("fsdp", None, None),
        P("fsdp", None, None),
        P("fsdp"),
        P("fsdp"),
        P("fsdp"),
        P("fsdp", None),
    )
    return jax.shard_map(
        on_device,
        mesh=mesh,
        in_specs=placed,
        out_specs=(
            P("fsdp", None, None, None),
            P("fsdp", None, None, None),
            P(None, "fsdp", None),
            P("fsdp", None, None),
        ),
        check_vma=False,
    )
```

time: 335 us -> 274 us (0.82)
  the two profiles are of different devices: /device:TPU:44 before, /device:TPU:2 now
where the time goes in v1:
time: 274 us; the launch traced here: 272 us
  blocking collectives  115 us (42%)
  waiting for transfers between devices  76.2 us (28%)
  Pallas kernels  48.5 us (18%)
  starting transfers between devices  22.5 us (8%)
  local copies, waits for them, and re-layouts  6.29 us (2%)
    all_to_all x6, blocking collectives, regroup(): lax.all_to_all(values, 'fsdp', split_axis=0, concat_axis=0, tiled=True)  115 us
    ppermute x6, waiting for transfers between devices, upward(): return lax.ppermute(values, 'replica', [(i, (i + 1) % 4) for i in range(4)])  38.7 us
    ppermute x6, waiting for transfers between devices, downward(): return lax.ppermute(values, 'replica', [(i, (i - 1) % 4) for i in range(4)])  37.4 us
    pallas_call x2, Pallas kernels, compress_call(): pl.pallas_call(functools.partial(kernel, blocks, slots), grid_spec=pltpu....  30.6 us
    pallas_call x2, Pallas kernels, unpack_call(): pl.pallas_call(functools.partial(unpack_kernel, slots), grid_spec=pltpu.P...  17.9 us
    ppermute x6, starting transfers between devices, downward(): return lax.ppermute(values, 'replica', [(i, (i - 1) % 4) for i in range(4)])  11.9 us
    all_to_all x1, starting transfers between devices, regroup(): lax.all_to_all(values, 'fsdp', split_axis=0, concat_axis=0, tiled=True)  6.43 us
  transfers between devices with their start and end apart: 13, of which 6 were waited for; matrix products, arithmetic and copies ran while one was open for 0% of the time, Pallas kernels for 3%

profile of v1, /device:TPU:2, one launch (start us, length us, event | category | flops | bytes accessed | tf_op | source)
XLA Modules:
  0.0 271.9 jit_solution(2154884818186269626)
XLA Ops:
  0.6 0.7 fusion
  1.6 0.8 select_reduce_fusion.2
  2.4 0.7 fusion.1
  3.1 13.5 %shard_map.104 = (bf16[96,32,128]{2,1,0:T(8,128)(2,1)}, bf16[96,32,128]{2,1,0:T(8,128)(2,1)}, bf16[64,128,128]{2,1,0:T(8,128)(2,1)}, f32[128,128]{1,0:T(8,128)}) custom-call(s32[1]{0:T(128)} %bitcast.replica, s32[128]{0:T(128)} %bitcast.17, s32[128]{0:T(128)} %weight_mask.3, s32[128]{0:T(128)} %moment_mask.1, f32[128,128,128]{2,1,0:T(8,128)} %moment.1), custom_call_target="tpu_custom_call" | custom-call | flops 10485760 | bytes 12582912 | tf_op jit(solution)/shard_map/pallas_call | solution.py:117
  16.6 0.9 slice_reduce_fusion
  17.5 17.1 %shard_map.102 = (bf16[96,32,128]{2,1,0:T(8,128)(2,1)}, bf16[64,32,128]{2,1,0:T(8,128)(2,1)}, bf16[96,128,128]{2,1,0:T(8,128)(2,1)}, f32[128,128]{1,0:T(8,128)}, bf16[128,128,128]{2,1,0:T(8,128)(2,1)}) custom-call(s32[1]{0:T(128)} %bitcast.replica, s32[128]{0:T(128)} %bitcast.18, s32[128]{0:T(128)} %weight_mask.3, f32[128]{0:T(128)} %base_scale.1, ...), custom_call_target="tpu_custom_call" | custom-call | flops 20971520 | bytes 25165824 | tf_op jit(solution)/shard_map/pallas_call | solution.py:117
  34.6 0.9 slice_reduce_fusion.1
  36.0 13.6 %all_to_all.36 = bf16[32,1,16]{2,1,0:T(2,128)(2,1)S(1)} all-to-all(bf16[32,1,16]{2,1,0:T(2,128)(2,1)S(1)} %copy.15), channel_id=1, replica_groups=mesh['replica'=4,'fsdp'=32] {'fsdp'}, dimensions={0} | all-to-all | bytes 2048 | tf_op jit(solution)/shard_map/all_to_all | solution.py:174
  49.6 15.5 %all_to_all.37.refs_4_ = bf16[64,32,128]{2,1,0:T(8,128)(2,1)} all-to-all(bf16[64,32,128]{2,1,0:T(8,128)(2,1)} %get-tuple-element.14), channel_id=1, replica_groups=mesh['replica'=4,'fsdp'=32] {'fsdp'}, dimensions={0} | all-to-all | bytes 1048576 | tf_op jit(solution)/shard_map/all_to_all | solution.py:174
  65.1 18.2 %all_to_all.38.refs_0_ = bf16[96,32,128]{2,1,0:T(8,128)(2,1)} all-to-all(bf16[96,32,128]{2,1,0:T(8,128)(2,1)} %get-tuple-element.16), channel_id=1, replica_groups=mesh['replica'=4,'fsdp'=32] {'fsdp'}, dimensions={0} | all-to-all | bytes 1572864 | tf_op jit(solution)/shard_map/all_to_all | solution.py:174
  83.2 17.9 %all_to_all.39.refs_4_ = bf16[96,32,128]{2,1,0:T(8,128)(2,1)} all-to-all(bf16[96,32,128]{2,1,0:T(8,128)(2,1)S(1)} %copy-done.6), channel_id=1, replica_groups=mesh['replica'=4,'fsdp'=32] {'fsdp'}, dimensions={0} | all-to-all | bytes 1572864 | tf_op jit(solution)/shard_map/all_to_all | solution.py:174
  101.1 18.5 %all_to_all.40.refs_0_ = bf16[96,32,128]{2,1,0:T(8,128)(2,1)} all-to-all(bf16[96,32,128]{2,1,0:T(8,128)(2,1)} %get-tuple-element.13), channel_id=1, replica_groups=mesh['replica'=4,'fsdp'=32] {'fsdp'}, dimensions={0} | all-to-all | bytes 1572864 | tf_op jit(solution)/shard_map/all_to_all | solution.py:174
  119.6 31.5 %all_to_all.41.refs_8_ = bf16[64,128,128]{2,1,0:T(8,128)(2,1)} all-to-all(bf16[64,128,128]{2,1,0:T(8,128)(2,1)S(1)} %copy-done.1), channel_id=1, replica_groups=mesh['replica'=4,'fsdp'=32] {'fsdp'}, dimensions={0} | all-to-all | bytes 4194304 | tf_op jit(solution)/shard_map/all_to_all | solution.py:174
  151.1 6.4 %all-to-all-start.2 = ((bf16[96,128,128]{2,1,0:T(8,128)(2,1)}), bf16[96,128,128]{2,1,0:T(8,128)(2,1)S(1)}, u32[]{:S(2)}, u32[]{:S(2)}) async-start(bf16[96,128,128]{2,1,0:T(8,128)(2,1)} %get-tuple-element.15), calls=%async_computation.2 | async-start | bytes 6291456 | tf_op jit(solution)/shard_map/all_to_all | solution.py:174
  157.5 4.1 %collective-permute-start.9 = (bf16[96,32,128]{2,1,0:T(8,128)(2,1)}, bf16[96,32,128]{2,1,0:T(8,128)(2,1)S(1)}, u32[]{:S(2)}, u32[]{:S(2)}) collective-permute-start(bf16[96,32,128]{2,1,0:T(8,128)(2,1)} %all_to_all.39.refs_4_), channel_id=1, source_target_pairs={{0,96},{32,0},{64,32},{96,64},{1,97},{33,1},{65,33},{97,65},{2,98}... | collective-permute-start | bytes 2359304 | tf_op jit(solution)/shard_map/ppermute | solution.py:182
  161.6 0.4 collective-permute-start.3
  162.0 1.6 collective-permute-start.7
  163.7 26.6 %collective-permute-done.3.refs_5_ = bf16[64,32,128]{2,1,0:T(8,128)(2,1)} collective-permute-done((bf16[64,32,128]{2,1,0:T(8,128)(2,1)}, bf16[64,32,128]{2,1,0:T(8,128)(2,1)}, u32[]{:S(2)}, u32[]{:S(2)}) %collective-permute-start.3) | collective-permute-done | bytes 524320 | tf_op jit(solution)/shard_map/ppermute | solution.py:182
  190.3 3.7 %collective-permute-start.6 = (bf16[96,32,128]{2,1,0:T(8,128)(2,1)}, bf16[96,32,128]{2,1,0:T(8,128)(2,1)S(1)}, u32[]{:S(2)}, u32[]{:S(2)}) collective-permute-start(bf16[96,32,128]{2,1,0:T(8,128)(2,1)} %all_to_all.38.refs_0_), channel_id=1, source_target_pairs={{0,96},{32,0},{64,32},{96,64},{1,97},{33,1},{65,33},{97,65},{2,98}... | collective-permute-start | bytes 2359304 | tf_op jit(solution)/shard_map/ppermute | solution.py:182
  194.0 0.9 copy-done.2
  194.9 2.0 collective-permute-start.8
  196.9 3.9 %collective-permute-done.11.refs_7_ = bf16[96,32,128]{2,1,0:T(8,128)(2,1)S(1)} collective-permute-done((bf16[96,32,128]{2,1,0:T(8,128)(2,1)}, bf16[96,32,128]{2,1,0:T(8,128)(2,1)S(1)}, u32[]{:S(2)}, u32[]{:S(2)}) %collective-permute-start.11) | collective-permute-done | bytes 786464 | tf_op jit(solution)/shard_map/ppermute | solution.py:178
  200.8 17.0 %collective-permute-done.1.refs_3_ = bf16[96,32,128]{2,1,0:T(8,128)(2,1)} collective-permute-done((bf16[96,32,128]{2,1,0:T(8,128)(2,1)}, bf16[96,32,128]{2,1,0:T(8,128)(2,1)}, u32[]{:S(2)}, u32[]{:S(2)}) %collective-permute-start.1) | collective-permute-done | bytes 786464 | tf_op jit(solution)/shard_map/ppermute | solution.py:178
  217.7 0.4 collective-permute-start.2
  218.2 10.8 %collective-permute-done.10.refs_6_ = bf16[96,32,128]{2,1,0:T(8,128)(2,1)S(1)} collective-permute-done((bf16[96,32,128]{2,1,0:T(8,128)(2,1)S(1)}, bf16[96,32,128]{2,1,0:T(8,128)(2,1)S(1)}, u32[]{:S(2)}, u32[]{:S(2)}) %collective-permute-start.10) | collective-permute-done | bytes 786464 | tf_op jit(solution)/shard_map/ppermute | solution.py:182
  229.1 0.9 copy-done.5
  230.0 3.7 %collective-permute-start.4 = (bf16[64,32,128]{2,1,0:T(8,128)(2,1)}, bf16[64,32,128]{2,1,0:T(8,128)(2,1)}, u32[]{:S(2)}, u32[]{:S(2)}) collective-permute-start(bf16[64,32,128]{2,1,0:T(8,128)(2,1)} %collective-permute-done.3.refs_5_), channel_id=1, source_target_pairs={{0,96},{32,0},{64,32},{96,64},{1,97},{33,1},{65,33},{97,65},{2,98}... | collective-permute-start | bytes 1572872 | tf_op jit(solution)/shard_map/ppermute | solution.py:182
  233.7 0.7 copy.16
  234.6 9.0 %shard_map.105 = bf16[256,128,128]{2,1,0:T(8,128)(2,1)} custom-call(s32[1]{0:T(128)} %bitcast.replica, bf16[96,32,128]{2,1,0:T(8,128)(2,1)} %all_to_all.38.refs_0_, bf16[96,32,128]{2,1,0:T(8,128)(2,1)} %copy-done.4, bf16[96,32,128]{2,1,0:T(8,128)(2,1)} %collective-permute-done.8.refs_2_, bf16[96,32,128]{2,1,0:T(8,128)(2,1)} %collective-permute-done.7.refs_3_, ...), custom_call_target="tpu_custom_call" | custom-call | bytes 16777216 | tf_op jit(solution)/shard_map/pallas_call | solution.py:159
  243.5 17.7 %collective-permute-done.5.refs_7_ = bf16[64,32,128]{2,1,0:T(8,128)(2,1)} collective-permute-done((bf16[64,32,128]{2,1,0:T(8,128)(2,1)}, bf16[64,32,128]{2,1,0:T(8,128)(2,1)}, u32[]{:S(2)}, u32[]{:S(2)}) %collective-permute-start.5) | collective-permute-done | bytes 524320 | tf_op jit(solution)/shard_map/ppermute | solution.py:178
  261.3 1.7 copy-done
  263.0 9.0 %shard_map.103 = bf16[256,128,128]{2,1,0:T(8,128)(2,1)} custom-call(s32[1]{0:T(128)} %bitcast.replica, bf16[96,32,128]{2,1,0:T(8,128)(2,1)} %all_to_all.40.refs_0_, bf16[96,32,128]{2,1,0:T(8,128)(2,1)} %collective-permute-done.refs_1_, bf16[96,32,128]{2,1,0:T(8,128)(2,1)} %collective-permute-done.2.refs_2_, ...), custom_call_target="tpu_custom_call" | custom-call | bytes 16777216 | tf_op jit(solution)/shard_map/pallas_call | solution.py:159
  (30 shorter events, 1.0 us)
Async XLA Ops:
  17.5 65.7 %copy-start.6 = (bf16[96,32,128]{2,1,0:T(8,128)(2,1)S(1)}, bf16[96,32,128]{2,1,0:T(8,128)(2,1)}, u32[]{:S(2)}) copy-start(bf16[96,32,128]{2,1,0:T(8,128)(2,1)} %get-tuple-element.17) | copy-start | bytes 2359300
  17.5 102.1 %copy-start.1 = (bf16[64,128,128]{2,1,0:T(8,128)(2,1)S(1)}, bf16[64,128,128]{2,1,0:T(8,128)(2,1)}, u32[]{:S(2)}) copy-start(bf16[64,128,128]{2,1,0:T(8,128)(2,1)} %get-tuple-element.18) | copy-start | bytes 6291460
  151.1 110.2 %all-to-all-start.2 = ((bf16[96,128,128]{2,1,0:T(8,128)(2,1)}), bf16[96,128,128]{2,1,0:T(8,128)(2,1)S(1)}, u32[]{:S(2)}, u32[]{:S(2)}) async-start(bf16[96,128,128]{2,1,0:T(8,128)(2,1)} %get-tuple-element.15), calls=%async_computation.2 | async-start | bytes 6291456 | tf_op jit(solution)/shard_map/all_to_all | solution.py:174
  157.5 36.5 %collective-permute-start.9 = (bf16[96,32,128]{2,1,0:T(8,128)(2,1)}, bf16[96,32,128]{2,1,0:T(8,128)(2,1)S(1)}, u32[]{:S(2)}, u32[]{:S(2)}) collective-permute-start(bf16[96,32,128]{2,1,0:T(8,128)(2,1)} %all_to_all.39.refs_4_), channel_id=1, source_target_pairs={{0,96},{32,0},{64,32},{96,64},{1,97},{33,1},{65,33},{97,65},{2,98}... | collective-permute-start | bytes 2359304 | tf_op jit(solution)/shard_map/ppermute | solution.py:182
  161.6 28.7 %collective-permute-start.3 = (bf16[64,32,128]{2,1,0:T(8,128)(2,1)}, bf16[64,32,128]{2,1,0:T(8,128)(2,1)}, u32[]{:S(2)}, u32[]{:S(2)}) collective-permute-start(bf16[64,32,128]{2,1,0:T(8,128)(2,1)} %all_to_all.37.refs_4_), channel_id=1, source_target_pairs={{0,96},{32,0},{64,32},{96,64},{1,97},{33,1},{65,33},{97,65},{2,98}... | collective-permute-start | bytes 1572872 | tf_op jit(solution)/shard_map/ppermute | solution.py:182
  162.0 32.8 %collective-permute-start.7 = (bf16[96,32,128]{2,1,0:T(8,128)(2,1)}, bf16[96,32,128]{2,1,0:T(8,128)(2,1)}, u32[]{:S(2)}, u32[]{:S(2)}) collective-permute-start(bf16[96,32,128]{2,1,0:T(8,128)(2,1)} %all_to_all.38.refs_0_), channel_id=1, source_target_pairs={{0,32},{32,64},{64,96},{96,0},{1,33},{33,65},{65,97},{97,1},{2,34}... | collective-permute-start | bytes 2359304 | tf_op jit(solution)/shard_map/ppermute | solution.py:178
  163.7 37.1 %collective-permute-start.11 = (bf16[96,32,128]{2,1,0:T(8,128)(2,1)}, bf16[96,32,128]{2,1,0:T(8,128)(2,1)S(1)}, u32[]{:S(2)}, u32[]{:S(2)}) collective-permute-start(bf16[96,32,128]{2,1,0:T(8,128)(2,1)} %all_to_all.39.refs_4_), channel_id=1, source_target_pairs={{0,32},{32,64},{64,96},{96,0},{1,33},{33,65},{65,97},{97,1},{2,34}... | collective-permute-start | bytes 2359304 | tf_op jit(solution)/shard_map/ppermute | solution.py:178
  163.7 54.0 %collective-permute-start.1 = (bf16[96,32,128]{2,1,0:T(8,128)(2,1)}, bf16[96,32,128]{2,1,0:T(8,128)(2,1)}, u32[]{:S(2)}, u32[]{:S(2)}) collective-permute-start(bf16[96,32,128]{2,1,0:T(8,128)(2,1)} %all_to_all.40.refs_0_), channel_id=1, source_target_pairs={{0,32},{32,64},{64,96},{96,0},{1,33},{33,65},{65,97},{97,1},{2,34}... | collective-permute-start | bytes 2359304 | tf_op jit(solution)/shard_map/ppermute | solution.py:178
  190.3 27.8 %collective-permute-start.6 = (bf16[96,32,128]{2,1,0:T(8,128)(2,1)}, bf16[96,32,128]{2,1,0:T(8,128)(2,1)S(1)}, u32[]{:S(2)}, u32[]{:S(2)}) collective-permute-start(bf16[96,32,128]{2,1,0:T(8,128)(2,1)} %all_to_all.38.refs_0_), channel_id=1, source_target_pairs={{0,96},{32,0},{64,32},{96,64},{1,97},{33,1},{65,33},{97,65},{2,98}... | collective-permute-start | bytes 2359304 | tf_op jit(solution)/shard_map/ppermute | solution.py:182
  194.0 0.9 copy-start.2
  194.9 34.2 %collective-permute-start.10 = (bf16[96,32,128]{2,1,0:T(8,128)(2,1)S(1)}, bf16[96,32,128]{2,1,0:T(8,128)(2,1)S(1)}, u32[]{:S(2)}, u32[]{:S(2)}) collective-permute-start(bf16[96,32,128]{2,1,0:T(8,128)(2,1)S(1)} %collective-permute-done.9.refs_5_), channel_id=1, source_target_pairs={{0,96},{32,0},{64,32},{96,64},{1,97},{33,1},{65,33},{97,65},{2,98}... | collective-permute-start | bytes 2359304 | tf_op jit(solution)/shard_map/ppermute | solution.py:182
  194.9 39.7 %collective-permute-start.8 = (bf16[96,32,128]{2,1,0:T(8,128)(2,1)}, bf16[96,32,128]{2,1,0:T(8,128)(2,1)}, u32[]{:S(2)}, u32[]{:S(2)}) collective-permute-start(bf16[96,32,128]{2,1,0:T(8,128)(2,1)} %collective-permute-done.7.refs_3_), channel_id=1, source_target_pairs={{0,32},{32,64},{64,96},{96,0},{1,33},{33,65},{65,97},{97,1},{2,34}... | collective-permute-start | bytes 2359304 | tf_op jit(solution)/shard_map/ppermute | solution.py:178
  200.8 28.3 %copy-start.3 = (bf16[96,32,128]{2,1,0:T(8,128)(2,1)}, bf16[96,32,128]{2,1,0:T(8,128)(2,1)S(1)}, u32[]{:S(2)}) copy-start(bf16[96,32,128]{2,1,0:T(8,128)(2,1)S(1)} %collective-permute-done.11.refs_7_) | copy-start | bytes 2359300
  200.8 60.5 %collective-permute-start = (bf16[96,32,128]{2,1,0:T(8,128)(2,1)}, bf16[96,32,128]{2,1,0:T(8,128)(2,1)}, u32[]{:S(2)}, u32[]{:S(2)}) collective-permute-start(bf16[96,32,128]{2,1,0:T(8,128)(2,1)} %all_to_all.40.refs_0_), channel_id=1, source_target_pairs={{0,96},{32,0},{64,32},{96,64},{1,97},{33,1},{65,33},{97,65},{2,98}... | collective-permute-start | bytes 2359304 | tf_op jit(solution)/shard_map/ppermute | solution.py:182
  217.7 43.5 %collective-permute-start.2 = (bf16[96,32,128]{2,1,0:T(8,128)(2,1)}, bf16[96,32,128]{2,1,0:T(8,128)(2,1)}, u32[]{:S(2)}, u32[]{:S(2)}) collective-permute-start(bf16[96,32,128]{2,1,0:T(8,128)(2,1)} %collective-permute-done.1.refs_3_), channel_id=1, source_target_pairs={{0,32},{32,64},{64,96},{96,0},{1,33},{33,65},{65,97},{97,1},{2,34}... | collective-permute-start | bytes 2359304 | tf_op jit(solution)/shard_map/ppermute | solution.py:178
  218.1 10.9 %copy-start.4 = (bf16[96,32,128]{2,1,0:T(8,128)(2,1)}, bf16[96,32,128]{2,1,0:T(8,128)(2,1)S(1)}, u32[]{:S(2)}) copy-start(bf16[96,32,128]{2,1,0:T(8,128)(2,1)S(1)} %collective-permute-done.6.refs_1_) | copy-start | bytes 2359300
  218.1 43.1 %collective-permute-start.5 = (bf16[64,32,128]{2,1,0:T(8,128)(2,1)}, bf16[64,32,128]{2,1,0:T(8,128)(2,1)}, u32[]{:S(2)}, u32[]{:S(2)}) collective-permute-start(bf16[64,32,128]{2,1,0:T(8,128)(2,1)} %all_to_all.37.refs_4_), channel_id=1, source_target_pairs={{0,32},{32,64},{64,96},{96,0},{1,33},{33,65},{65,97},{97,1},{2,34}... | collective-permute-start | bytes 1572872 | tf_op jit(solution)/shard_map/ppermute | solution.py:178
  229.1 0.9 copy-start.5
  230.0 31.3 %collective-permute-start.4 = (bf16[64,32,128]{2,1,0:T(8,128)(2,1)}, bf16[64,32,128]{2,1,0:T(8,128)(2,1)}, u32[]{:S(2)}, u32[]{:S(2)}) collective-permute-start(bf16[64,32,128]{2,1,0:T(8,128)(2,1)} %collective-permute-done.3.refs_5_), channel_id=1, source_target_pairs={{0,96},{32,0},{64,32},{96,64},{1,97},{33,1},{65,33},{97,65},{2,98}... | collective-permute-start | bytes 1572872 | tf_op jit(solution)/shard_map/ppermute | solution.py:182
  261.3 1.7 copy-start

commit v2 on v0

v2 whole, which is shorter than its diff:
```python
import functools

import jax
import jax.numpy as jnp
from jax import lax
from jax.experimental import pallas as pl
from jax.experimental.pallas import tpu as pltpu
from jax.sharding import PartitionSpec as P

EPSILON = 1e-06
WRITERS = 32
CAP = 8
GROUP = 8
ROWS = 32
TILE = 16
SLOTS = WRITERS * CAP
VMEM = 60 * 1024 * 1024

BY_ROWS_MOMENT = 8
BY_ROWS_WEIGHT = 6
USUAL = (128, 128)
FULL = (WRITERS * BY_ROWS_MOMENT + 8, WRITERS * BY_ROWS_WEIGHT + 8)


def clear(ref, length, value):
    def one(i, carry):
        ref[i] = value
        return carry

    lax.fori_loop(0, length, one, 0, unroll=8)


def scale_of(values):
    top = jnp.max(jnp.max(jnp.abs(values), axis=0, keepdims=True), axis=1, keepdims=True)
    top = jnp.broadcast_to(top + EPSILON, (8, 128))
    return top.astype(jnp.bfloat16).astype(jnp.float32)


def row_quarter(replica):
    return pl.ds(pl.multiple_of(replica[0] * ROWS, ROWS), ROWS)


def payload_rows(by_rows):
    return by_rows * ROWS + TILE


def tile_rows(writer, by_rows):
    return pl.ds(pl.multiple_of(writer * payload_rows(by_rows) + by_rows * ROWS, TILE), TILE)


def slot_rows(writer, k, by_rows):
    return pl.ds(pl.multiple_of(writer * payload_rows(by_rows) + k * ROWS, TILE), ROWS)


def moment_kernel(blocks, replica, writer, weight_mask, moment_mask, moment, payload, coded, scales, slot_of, kept_w, kept_m, count, count_w, count_m):
    step = pl.program_id(0)
    rows = row_quarter(replica)

    @pl.when(step == 0)
    def _():
        clear(slot_of, SLOTS, blocks)
        clear(kept_w, SLOTS, 0)
        clear(kept_m, SLOTS, 0)
        clear(count, WRITERS, 0)
        clear(count_w, WRITERS, 0)
        clear(count_m, WRITERS, 0)
        coded[blocks] = jnp.zeros(coded.shape[1:], coded.dtype)
        scales[pl.ds(blocks, 8), :] = jnp.zeros((8, 128), jnp.float32)

    for i in range(GROUP):
        block = step * GROUP + i
        target = writer[block]
        rank = count[target]
        count[target] = rank + 1
        slot = target * CAP + rank
        slot_of[slot] = block
        keep_w = weight_mask[block]
        keep_m = keep_w * moment_mask[block]
        kept_w[slot] = keep_w
        kept_m[slot] = keep_m
        count_w[target] = count_w[target] + jnp.where(rank < BY_ROWS_WEIGHT, keep_w, 0)
        count_m[target] = count_m[target] + jnp.where(rank < BY_ROWS_MOMENT, keep_m, 0)
        scale = scale_of(moment[i])
        scales[pl.ds(block, 1), :] = scale[0:1, :]
        coded[block] = (moment[i, rows, :] * (keep_m.astype(jnp.float32) / scale)[0:1, :]).astype(jnp.bfloat16)

    @pl.when(step == blocks // GROUP - 1)
    def _():
        lane = lax.broadcasted_iota(jnp.int32, (TILE, 128), 1)
        line = lax.broadcasted_iota(jnp.int32, (TILE, 128), 0)

        def counts(w, tile):
            both = jnp.where(line == 3, count_w[w].astype(jnp.float32), jnp.where(line == 4, count_m[w].astype(jnp.float32), 0.0))
            return jnp.where(lane == w, both, tile)

        common = lax.fori_loop(0, WRITERS, counts, jnp.zeros((TILE, 128), jnp.float32))

        def one(w, carry):
            tile = common
            for k in range(CAP):
                slot = w * CAP + k
                block = slot_of[slot]
                if k < BY_ROWS_MOMENT:
                    payload[slot_rows(w, k, BY_ROWS_MOMENT), :] = coded[block]
                scale = jnp.broadcast_to(scales[pl.ds(block, 1), :], (TILE, 128))
                kept = jnp.where(line == 1, kept_w[slot].astype(jnp.float32), kept_m[slot].astype(jnp.float32))
                tile = jnp.where((lane == k) & (line <= 2), jnp.where(line == 0, scale, kept), tile)
            payload[tile_rows(w, BY_ROWS_MOMENT), :] = tile.astype(jnp.bfloat16)
            return carry

        lax.fori_loop(0, WRITERS, one, 0)


def weight_kernel(blocks, replica, writer, weight_mask, base_scale, weight, codes, payload, whole, refreshed, coded, scales, slot_of, count):
    step = pl.program_id(0)

    @pl.when(step == 0)
    def _():
        clear(slot_of, SLOTS, blocks)
        clear(count, WRITERS, 0)
        coded[blocks] = jnp.zeros(coded.shape[1:], coded.dtype)
        scales[pl.ds(blocks, 8), :] = jnp.zeros((8, 128), jnp.float32)

    for i in range(GROUP):
        block = step * GROUP + i
        target = writer[block]
        rank = count[target]
        count[target] = rank + 1
        slot_of[target * CAP + rank] = block
        keep = weight_mask[block].astype(jnp.float32)
        base = codes[i].astype(jnp.float32) * base_scale[block]
        values = weight[i] - base
        scale = scale_of(values)
        scales[pl.ds(block, 1), :] = scale[0:1, :]
        rounded = (values * (keep / scale)[0:1, :]).astype(jnp.bfloat16)
        coded[block] = rounded
        refreshed[i] = (base + rounded.astype(jnp.float32) * scale[0:1, :]).astype(jnp.bfloat16)

    @pl.when(step == blocks // GROUP - 1)
    def _():
        rows = row_quarter(replica)
        lane = lax.broadcasted_iota(jnp.int32, (TILE, 128), 1)

        def one(w, carry):
            tile = jnp.zeros((TILE, 128), jnp.float32)
            for k in range(CAP):
                block = slot_of[w * CAP + k]
                if k < BY_ROWS_WEIGHT:
                    payload[slot_rows(w, k, BY_ROWS_WEIGHT), :] = coded[block, rows, :]
                else:
                    whole[w * (CAP - BY_ROWS_WEIGHT) + k - BY_ROWS_WEIGHT] = coded[block]
                tile = jnp.where(lane == k, jnp.broadcast_to(scales[pl.ds(block, 1), :], (TILE, 128)), tile)
            payload[tile_rows(w, BY_ROWS_WEIGHT), :] = tile.astype(jnp.bfloat16)
            return carry

        lax.fori_loop(0, WRITERS, one, 0)


def cost(flops, moved):
    return pl.CostEstimate(flops=flops, bytes_accessed=moved, transcendentals=0)


def params():
    return pltpu.CompilerParams(dimension_semantics=("arbitrary",), vmem_limit_bytes=VMEM)


def moment_call(replica, writer, weight_mask, moment_mask, moment):
    blocks, width = moment.shape[0], moment.shape[1]
    shape = (WRITERS * payload_rows(BY_ROWS_MOMENT), width)
    return pl.pallas_call(
        functools.partial(moment_kernel, blocks),
        grid_spec=pltpu.PrefetchScalarGridSpec(
            num_scalar_prefetch=4,
            grid=(blocks // GROUP,),
            in_specs=[pl.BlockSpec((GROUP, width, width), lambda i, *_: (i, 0, 0))],
            out_specs=pl.BlockSpec(shape, lambda i, *_: (0, 0)),
            scratch_shapes=[
                pltpu.VMEM((blocks + 1, ROWS, width), jnp.bfloat16),
                pltpu.VMEM((blocks + 8, 128), jnp.float32),
                pltpu.SMEM((SLOTS,), jnp.int32),
                pltpu.SMEM((SLOTS,), jnp.int32),
                pltpu.SMEM((SLOTS,), jnp.int32),
                pltpu.SMEM((WRITERS,), jnp.int32),
                pltpu.SMEM((WRITERS,), jnp.int32),
                pltpu.SMEM((WRITERS,), jnp.int32),
            ],
        ),
        out_shape=jax.ShapeDtypeStruct(shape, jnp.bfloat16),
        compiler_params=params(),
        cost_estimate=cost(10 << 20, 12 << 20),
    )(replica, writer, weight_mask, moment_mask, moment)


def weight_call(replica, writer, weight_mask, base_scale, weight, codes):
    blocks, width = weight.shape[0], weight.shape[1]
    moving = pl.BlockSpec((GROUP, width, width), lambda i, *_: (i, 0, 0))
    payload = (WRITERS * payload_rows(BY_ROWS_WEIGHT), width)
    whole = (WRITERS * (CAP - BY_ROWS_WEIGHT), width, width)
    return pl.pallas_call(
        functools.partial(weight_kernel, blocks),
        grid_spec=pltpu.PrefetchScalarGridSpec(
            num_scalar_prefetch=4,
            grid=(blocks // GROUP,),
            in_specs=[moving, moving],
            out_specs=[pl.BlockSpec(payload, lambda i, *_: (0, 0)), pl.BlockSpec(whole, lambda i, *_: (0, 0, 0)), moving],
            scratch_shapes=[
                pltpu.VMEM((blocks + 1, width, width), jnp.bfloat16),
                pltpu.VMEM((blocks + 8, 128), jnp.float32),
                pltpu.SMEM((SLOTS,), jnp.int32),
                pltpu.SMEM((WRITERS,), jnp.int32),
            ],
        ),
        out_shape=[
            jax.ShapeDtypeStruct(payload, jnp.bfloat16),
            jax.ShapeDtypeStruct(whole, jnp.bfloat16),
            jax.ShapeDtypeStruct((blocks, width, width), jnp.bfloat16),
        ],
        compiler_params=params(),
        cost_estimate=cost(20 << 20, 28 << 20),
    )(replica, writer, weight_mask, base_scale, weight, codes)


def pack_kernel(by_rows, half, kept, payload, _, first, second, passed, packed):
    def one(s, place):
        for k in range(by_rows):
            packed[place] = payload[slot_rows(s, k, by_rows), :]
            place = place + kept[s * CAP + k]
        return place

    lax.fori_loop(0, WRITERS, one, 0)
    first[...] = packed[0:half]
    second[...] = packed[half : 2 * half]


def pack_call(by_rows, capacity, kept, payload, later):
    width = payload.shape[-1]
    half = capacity // 2
    part = (half, ROWS, width)
    return pl.pallas_call(
        functools.partial(pack_kernel, by_rows, half),
        grid_spec=pltpu.PrefetchScalarGridSpec(
            num_scalar_prefetch=1,
            grid=(1,),
            in_specs=[pl.BlockSpec(payload.shape, lambda i, *_: (0, 0)), pl.BlockSpec(memory_space=pl.ANY)],
            out_specs=[pl.BlockSpec(part, lambda i, *_: (0, 0, 0))] * 2 + [pl.BlockSpec(memory_space=pl.ANY)],
            scratch_shapes=[pltpu.VMEM((capacity, ROWS, width), jnp.bfloat16)],
        ),
        out_shape=[jax.ShapeDtypeStruct(part, jnp.bfloat16)] * 2 + [jax.ShapeDtypeStruct(later.shape, later.dtype)],
        input_output_aliases={2: 2},
        compiler_params=params(),
        cost_estimate=cost(0, 4 << 20),
    )(kept, payload, later)


SOURCES = 4


def unpack_kernel(by_rows, half, replica, kept, *refs):
    parts, refs = refs[:8], refs[8:]
    if by_rows < CAP:
        whole, refs = refs[0], refs[1:]
    out, held, sems, place_ref = refs
    step = pl.program_id(0)

    @pl.when(step == 0)
    def _():
        place_ref[0] = 0
        copies = [
            pltpu.make_async_copy(part, held.at[i // 2, pl.ds((i % 2) * half, half)], sems.at[i]) for i, part in enumerate(parts)
        ]
        for copy in copies:
            copy.start()
        for copy in copies:
            copy.wait()

    rows = [pl.ds(pl.multiple_of(lax.rem(replica[0] + turn, 4) * ROWS, ROWS), ROWS) for turn in range(4)]
    place = place_ref[0]
    for s in range(SOURCES):
        for k in range(by_rows):
            flag = kept[(step * SOURCES + s) * CAP + k]
            for turn in range(4):
                values = held[turn, place]
                out[s * CAP + k, rows[turn], :] = jnp.where(flag > 0, values, jnp.zeros_like(values))
            place = place + flag
        for k in range(by_rows, CAP):
            out[s * CAP + k] = whole[s * (CAP - by_rows) + k - by_rows]
    place_ref[0] = place


def unpack_call(by_rows, capacity, replica, kept, parts, whole):
    width = parts[0].shape[-1]
    half = capacity // 2
    specs = [pl.BlockSpec(memory_space=pl.ANY)] * 8
    if whole is not None:
        specs.append(pl.BlockSpec((SOURCES * (CAP - by_rows), width, width), lambda i, *_: (i, 0, 0)))
        parts = (*parts, whole)
    return pl.pallas_call(
        functools.partial(unpack_kernel, by_rows, half),
        grid_spec=pltpu.PrefetchScalarGridSpec(
            num_scalar_prefetch=2,
            grid=(WRITERS // SOURCES,),
            in_specs=specs,
            out_specs=pl.BlockSpec((SOURCES * CAP, width, width), lambda i, *_: (i, 0, 0)),
            scratch_shapes=[
                pltpu.VMEM((4, capacity, ROWS, width), jnp.bfloat16),
                pltpu.SemaphoreType.DMA((8,)),
                pltpu.SMEM((1,), jnp.int32),
            ],
        ),
        out_shape=jax.ShapeDtypeStruct((SLOTS, width, width), jnp.bfloat16),
        compiler_params=params(),
        cost_estimate=cost(0, 14 << 20),
    )(replica, kept, *parts)


def regroup(values):
    return lax.all_to_all(values, "fsdp", split_axis=0, concat_axis=0, tiled=True)


def upward(values):
    return lax.ppermute(values, "replica", [(i, (i + 1) % 4) for i in range(4)])


def downward(values):
    return lax.ppermute(values, "replica", [(i, (i - 1) % 4) for i in range(4)])


def gather_rows(first, second):
    first_up, first_down = upward(first), downward(first)
    second_up, second_down = upward(second), downward(second)
    return (first, second, first_down, second_down, upward(first_up), downward(second_down), first_up, second_up)


def exchange(capacities, replica, kept_w, kept_m, m_payload, w_payload, w_whole):
    m_first, m_second, w_payload = pack_call(BY_ROWS_MOMENT, capacities[0], kept_m, m_payload, w_payload)
    m_parts = gather_rows(m_first, m_second)
    w_payload = regroup(w_payload)
    w_first, w_second, w_whole = pack_call(BY_ROWS_WEIGHT, capacities[1], kept_w, w_payload, w_whole)
    w_parts = gather_rows(w_first, w_second)
    w_whole = regroup(w_whole)
    written_moment = unpack_call(BY_ROWS_MOMENT, capacities[0], replica, kept_m, m_parts, None)
    written_weight = unpack_call(BY_ROWS_WEIGHT, capacities[1], replica, kept_w, w_parts, w_whole)
    w_tile = w_payload.reshape(WRITERS, payload_rows(BY_ROWS_WEIGHT), -1)[:, BY_ROWS_WEIGHT * ROWS, :CAP]
    return written_weight, written_moment, w_tile


def on_device(weight, moment, base_codes, base_scale, weight_mask, moment_mask, writer):
    width = weight.shape[1]
    target = writer[:, 0]
    replica = lax.axis_index("replica").astype(jnp.int32).reshape(1)
    m_payload = regroup(moment_call(replica, target, weight_mask, moment_mask, moment))
    w_payload, w_whole, refreshed = weight_call(replica, target, weight_mask, base_scale, weight, base_codes)

    tile = m_payload.reshape(WRITERS, payload_rows(BY_ROWS_MOMENT), width)[:, BY_ROWS_MOMENT * ROWS :, :]
    kept_w, kept_m = (tile[:, line, :CAP].astype(jnp.int32).reshape(SLOTS) for line in (1, 2))
    totals = jnp.sum(tile[:, 3:5, :WRITERS].astype(jnp.int32), axis=0)
    fits = jnp.all(totals < jnp.array([[USUAL[1]], [USUAL[0]]], jnp.int32))
    written_weight, written_moment, w_scales = lax.cond(
        fits,
        functools.partial(exchange, USUAL),
        functools.partial(exchange, FULL),
        replica, kept_w, kept_m, m_payload, w_payload, w_whole,
    )
    written_scales = jnp.stack([w_scales, tile[:, 0, :CAP]], axis=0)
    shape = (WRITERS, CAP, width, width)
    return written_weight.reshape(shape), written_moment.reshape(shape), written_scales, refreshed


def solution(mesh):
    placed = (
        P("fsdp", None, None),
        P("fsdp", None, None),
        P("fsdp", None, None),
        P("fsdp"),
        P("fsdp"),
        P("fsdp"),
        P("fsdp", None),
    )
    return jax.shard_map(
        on_device,
        mesh=mesh,
        in_specs=placed,
        out_specs=(
            P("fsdp", None, None, None),
            P("fsdp", None, None, None),
            P(None, "fsdp", None),
            P("fsdp", None, None),
        ),
        check_vma=False,
    )
```

time: 335 us -> 182 us (0.54)
  the two profiles are of different devices: /device:TPU:44 before, /device:TPU:2 now
where the time goes in v2:
time: 182 us; the launch traced here: 180 us
  waiting for transfers between devices  76.8 us (42%)
  Pallas kernels  55.4 us (30%)
  starting transfers between devices  38.6 us (21%)
  local copies, waits for them, and re-layouts  6.25 us (3%)
    ppermute x6, waiting for transfers between devices, upward(): return lax.ppermute(values, 'replica', [(i, (i + 1) % 4) for i in range(4)])  37.7 us
    all_to_all x3, waiting for transfers between devices, regroup(): lax.all_to_all(values, 'fsdp', split_axis=0, concat_axis=0, tiled=True)  31.2 us
    all_to_all x3, starting transfers between devices, regroup(): lax.all_to_all(values, 'fsdp', split_axis=0, concat_axis=0, tiled=True)  21.6 us
    pallas_call x2, Pallas kernels, unpack_call(): pl.pallas_call(functools.partial(unpack_kernel, by_rows, half), grid_spec...  18.8 us
    pallas_call x1, Pallas kernels, weight_call(): pl.pallas_call(functools.partial(weight_kernel, blocks), grid_spec=pltpu....  17.1 us
    pallas_call x1, Pallas kernels, moment_call(): pl.pallas_call(functools.partial(moment_kernel, blocks), grid_spec=pltpu....  13.3 us
    ppermute x6, starting transfers between devices, downward(): return lax.ppermute(values, 'replica', [(i, (i - 1) % 4) for i in range(4)])  13.1 us
    ppermute x6, waiting for transfers between devices, downward(): return lax.ppermute(values, 'replica', [(i, (i - 1) % 4) for i in range(4)])  7.81 us
  transfers between devices with their start and end apart: 15, of which 7 were waited for; matrix products, arithmetic and copies ran while one was open for 1% of the time, Pallas kernels for 14%

profile of v2, /device:TPU:2, one launch (start us, length us, event | category | flops | bytes accessed | tf_op | source)
XLA Modules:
  0.0 180.0 jit_solution(11217063495727998875)
XLA Ops:
  0.6 13.3 %shard_map.111 = bf16[8704,128]{1,0:T(8,128)(2,1)} custom-call(s32[1]{0:T(128)} %bitcast.12.replica, s32[128]{0:T(128)} %bitcast.38, s32[128]{0:T(128)} %weight_mask.3, s32[128]{0:T(128)} %moment_mask.1, f32[128,128,128]{2,1,0:T(8,128)} %moment.1), custom_call_target="tpu_custom_call" | custom-call | flops 10485760 | bytes 12582912 | tf_op jit(solution)/shard_map/pallas_call | solution.py:170
  13.9 7.6 %all-to-all-start.4 = ((bf16[32,272,128]{2,1,0:T(8,128)(2,1)}), bf16[32,272,128]{2,1,0:T(8,128)(2,1)S(1)}, u32[]{:S(2)}, u32[]{:S(2)}) async-start(bf16[32,272,128]{2,1,0:T(8,128)(2,1)} %bitcast.28), calls=%async_computation.4 | async-start | bytes 4456448 | tf_op jit(solution)/shard_map/all_to_all | solution.py:317
  21.5 17.1 %shard_map.112 = (bf16[6656,128]{1,0:T(8,128)(2,1)}, bf16[64,128,128]{2,1,0:T(8,128)(2,1)}, bf16[128,128,128]{2,1,0:T(8,128)(2,1)}) custom-call(s32[1]{0:T(128)} %bitcast.12.replica, s32[128]{0:T(128)} %bitcast.39, s32[128]{0:T(128)} %weight_mask.3, f32[128]{0:T(128)} %base_scale.1, f32[128,128,128]{2,1,0:T(8,128)} %weight.1, s32[128,128,128]{2,1,0:T(8,128)} %codes.1), custom_call_target="tpu_custom_call" | custom-call | flops 20971520 | bytes 29360128 | tf_op jit(solution)/shard_map/pallas_call | solution.py:199
  38.6 10.3 %all-to-all-done.4 = bf16[32,272,128]{2,1,0:T(8,128)(2,1)S(1)} async-done(((bf16[32,272,128]{2,1,0:T(8,128)(2,1)}), bf16[32,272,128]{2,1,0:T(8,128)(2,1)S(1)}, u32[]{:S(2)}, u32[]{:S(2)}) %all-to-all-start.4) | async-done | bytes 2228256 | tf_op jit(solution)/shard_map/all_to_all | solution.py:317
  48.9 0.6 compare_reduce_fusion
  50.3 129.1 %conditional.1 = (bf16[32,8,128,128]{3,2,1,0:T(8,128)(2,1)}, bf16[32,8,128,128]{3,2,1,0:T(8,128)(2,1)}, bf16[1,32,8]{1,2,0:T(8,128)(2,1)S(1)}) conditional(s32[]{:T(128)} %convert_element_type.35, (bf16[32,272,128]{2,1,0:T(8,128)(2,1)S(1)}, bf16[6656,128]{1,0:T(8,128)(2,1)}, bf16[64,128,128]{2,1,0:T(8,128)(2,1)}, s32[1]{0:T(128)}) %tuple.22, ...), branch_computations={%region_2.0_spmd, %region_3.0_spmd} | conditional | flops 512 | bytes 126363320 | solution.py:358
  50.9 0.7 reshape.61.kept
  51.6 2.5 %branch_1_fun.4 = (bf16[64,32,128]{2,1,0:T(8,128)(2,1)}, bf16[64,32,128]{2,1,0:T(8,128)(2,1)}, bf16[6656,128]{1,0:T(8,128)(2,1)}) custom-call(s32[256]{0:T(256)} %reshape.61.kept, bf16[8704,128]{1,0:T(8,128)(2,1)S(1)} %bitcast.25, bf16[6656,128]{1,0:T(8,128)(2,1)} %get-tuple-element.49._), custom_call_target="tpu_custom_call", output_to_operand_aliasing={{2}: (2, {})} | custom-call | bytes 4194304 | tf_op jit(solution)/shard_map/cond/branch_1_fun/pallas_call | solution.py:239
  54.1 6.9 %all-to-all-start.2 = ((bf16[32,208,128]{2,1,0:T(8,128)(2,1)}), bf16[32,208,128]{2,1,0:T(8,128)(2,1)S(1)}, u32[]{:S(2)}, u32[]{:S(2)}) async-start(bf16[32,208,128]{2,1,0:T(8,128)(2,1)} %bitcast.27), calls=%async_computation.2 | async-start | bytes 3407872 | tf_op jit(solution)/shard_map/cond/branch_1_fun/all_to_all | solution.py:317
  61.0 0.7 reshape.60.kept
  61.6 20.9 %all-to-all-done.2 = bf16[32,208,128]{2,1,0:T(8,128)(2,1)S(1)} async-done(((bf16[32,208,128]{2,1,0:T(8,128)(2,1)}), bf16[32,208,128]{2,1,0:T(8,128)(2,1)S(1)}, u32[]{:S(2)}, u32[]{:S(2)}) %all-to-all-start.2) | async-done | bytes 1703968 | tf_op jit(solution)/shard_map/cond/branch_1_fun/all_to_all | solution.py:317
  82.6 1.2 copy-done.2
  83.8 3.8 %branch_1_fun.5 = (bf16[64,32,128]{2,1,0:T(8,128)(2,1)}, bf16[64,32,128]{2,1,0:T(8,128)(2,1)}, bf16[64,128,128]{2,1,0:T(8,128)(2,1)}) custom-call(s32[256]{0:T(256)} %reshape.60.kept, bf16[6656,128]{1,0:T(8,128)(2,1)} %bitcast.33, bf16[64,128,128]{2,1,0:T(8,128)(2,1)} %get-tuple-element.51._), custom_call_target="tpu_custom_call", output_to_operand_aliasing={{2}: (2, {})} | custom-call | bytes 4194304 | tf_op jit(solution)/shard_map/cond/branch_1_fun/pallas_call | solution.py:239
  87.6 7.1 %all-to-all-start.3 = ((bf16[64,128,128]{2,1,0:T(8,128)(2,1)}), bf16[64,128,128]{2,1,0:T(8,128)(2,1)S(1)}, u32[]{:S(2)}, u32[]{:S(2)}) async-start(bf16[64,128,128]{2,1,0:T(8,128)(2,1)} %get-tuple-element.54), calls=%async_computation.3 | async-start | bytes 4194304 | tf_op jit(solution)/shard_map/cond/branch_1_fun/all_to_all | solution.py:317
  94.7 2.0 %collective-permute-start.20 = (bf16[64,32,128]{2,1,0:T(8,128)(2,1)}, bf16[64,32,128]{2,1,0:T(8,128)(2,1)S(1)}, u32[]{:S(2)}, u32[]{:S(2)}) collective-permute-start(bf16[64,32,128]{2,1,0:T(8,128)(2,1)} %get-tuple-element.55.refs_0_), channel_id=1, source_target_pairs={{0,32},{32,64},{64,96},{96,0},{1,33},{33,65},{65,97},{97,1},{2,34}... | collective-permute-start | bytes 1572872 | tf_op jit(solution)/shard_map/cond/branch_1_fun/ppermute | solution.py:321
  96.6 2.2 %collective-permute-start.19 = (bf16[64,32,128]{2,1,0:T(8,128)(2,1)}, bf16[64,32,128]{2,1,0:T(8,128)(2,1)S(1)}, u32[]{:S(2)}, u32[]{:S(2)}) collective-permute-start(bf16[64,32,128]{2,1,0:T(8,128)(2,1)} %get-tuple-element.56.refs_1_), channel_id=1, source_target_pairs={{0,96},{32,0},{64,32},{96,64},{1,97},{33,1},{65,33},{97,65},{2,98}... | collective-permute-start | bytes 1572872 | tf_op jit(solution)/shard_map/cond/branch_1_fun/ppermute | solution.py:325
  98.9 1.9 %collective-permute-start.18 = (bf16[64,32,128]{2,1,0:T(8,128)(2,1)}, bf16[64,32,128]{2,1,0:T(8,128)(2,1)S(1)}, u32[]{:S(2)}, u32[]{:S(2)}) collective-permute-start(bf16[64,32,128]{2,1,0:T(8,128)(2,1)} %get-tuple-element.55.refs_0_), channel_id=1, source_target_pairs={{0,96},{32,0},{64,32},{96,64},{1,97},{33,1},{65,33},{97,65},{2,98}... | collective-permute-start | bytes 1572872 | tf_op jit(solution)/shard_map/cond/branch_1_fun/ppermute | solution.py:325
  100.9 10.8 %collective-permute-done.20.refs_6_ = bf16[64,32,128]{2,1,0:T(8,128)(2,1)S(1)} collective-permute-done((bf16[64,32,128]{2,1,0:T(8,128)(2,1)}, bf16[64,32,128]{2,1,0:T(8,128)(2,1)S(1)}, u32[]{:S(2)}, u32[]{:S(2)}) %collective-permute-start.20) | collective-permute-done | bytes 524320 | tf_op jit(solution)/shard_map/cond/branch_1_fun/ppermute | solution.py:321
  111.7 1.9 %collective-permute-start.14 = (bf16[64,32,128]{2,1,0:T(8,128)(2,1)S(1)}, bf16[64,32,128]{2,1,0:T(8,128)(2,1)}, u32[]{:S(2)}, u32[]{:S(2)}) collective-permute-start(bf16[64,32,128]{2,1,0:T(8,128)(2,1)S(1)} %copy-done.7), channel_id=1, source_target_pairs={{0,32},{32,64},{64,96},{96,0},{1,33},{33,65},{65,97},{97,1},{2,34}... | collective-permute-start | bytes 1572872 | tf_op jit(solution)/shard_map/cond/branch_1_fun/ppermute | solution.py:321
  113.6 1.5 collective-permute-start.13
  115.1 7.8 %collective-permute-done.18.refs_2_ = bf16[64,32,128]{2,1,0:T(8,128)(2,1)S(1)} collective-permute-done((bf16[64,32,128]{2,1,0:T(8,128)(2,1)}, bf16[64,32,128]{2,1,0:T(8,128)(2,1)S(1)}, u32[]{:S(2)}, u32[]{:S(2)}) %collective-permute-start.18) | collective-permute-done | bytes 524320 | tf_op jit(solution)/shard_map/cond/branch_1_fun/ppermute | solution.py:325
  122.9 3.4 %collective-permute-start.22 = (bf16[64,32,128]{2,1,0:T(8,128)(2,1)S(1)}, bf16[64,32,128]{2,1,0:T(8,128)(2,1)S(1)}, u32[]{:S(2)}, u32[]{:S(2)}) collective-permute-start(bf16[64,32,128]{2,1,0:T(8,128)(2,1)S(1)} %collective-permute-done.19.refs_3_), channel_id=1, source_target_pairs={{0,96},{32,0},{64,32},{96,64},{1,97},{33,1},{65,33},{97,65},{2,98}... | collective-permute-start | bytes 1572872 | tf_op jit(solution)/shard_map/cond/branch_1_fun/ppermute | solution.py:325
  126.3 0.8 collective-permute-start.12
  127.1 7.1 %collective-permute-done.21.refs_4_ = bf16[64,32,128]{2,1,0:T(8,128)(2,1)S(1)} collective-permute-done((bf16[64,32,128]{2,1,0:T(8,128)(2,1)S(1)}, bf16[64,32,128]{2,1,0:T(8,128)(2,1)S(1)}, u32[]{:S(2)}, u32[]{:S(2)}) %collective-permute-start.21) | collective-permute-done | bytes 524320 | tf_op jit(solution)/shard_map/cond/branch_1_fun/ppermute | solution.py:321
  134.2 11.3 %collective-permute-done.14.refs_6_ = bf16[64,32,128]{2,1,0:T(8,128)(2,1)} collective-permute-done((bf16[64,32,128]{2,1,0:T(8,128)(2,1)S(1)}, bf16[64,32,128]{2,1,0:T(8,128)(2,1)}, u32[]{:S(2)}, u32[]{:S(2)}) %collective-permute-start.14) | collective-permute-done | bytes 524320 | tf_op jit(solution)/shard_map/cond/branch_1_fun/ppermute | solution.py:321
  145.5 3.2 %collective-permute-start.16 = (bf16[64,32,128]{2,1,0:T(8,128)(2,1)}, bf16[64,32,128]{2,1,0:T(8,128)(2,1)}, u32[]{:S(2)}, u32[]{:S(2)}) collective-permute-start(bf16[64,32,128]{2,1,0:T(8,128)(2,1)} %collective-permute-done.13.refs_3_), channel_id=1, source_target_pairs={{0,96},{32,0},{64,32},{96,64},{1,97},{33,1},{65,33},{97,65},{2,98}... | collective-permute-start | bytes 1572872 | tf_op jit(solution)/shard_map/cond/branch_1_fun/ppermute | solution.py:325
  148.8 0.8 copy-done.14
  149.6 8.5 %branch_1_fun.7 = bf16[256,128,128]{2,1,0:T(8,128)(2,1)} custom-call(s32[1]{0:T(128)} %get-tuple-element.47.replica, s32[256]{0:T(256)} %reshape.61.kept, bf16[64,32,128]{2,1,0:T(8,128)(2,1)} %get-tuple-element.55.refs_0_, bf16[64,32,128]{2,1,0:T(8,128)(2,1)} %get-tuple-element.56.refs_1_, bf16[64,32,128]{2,1,0:T(8,128)(2,1)} %copy-done.11, ...), custom_call_target="tpu_custom_call" | custom-call | bytes 14680064 | tf_op jit(solution)/shard_map/cond/branch_1_fun/pallas_call | solution.py:297
  158.1 0.9 slice.38
  159.0 8.5 %collective-permute-done.15.refs_4_ = bf16[64,32,128]{2,1,0:T(8,128)(2,1)} collective-permute-done((bf16[64,32,128]{2,1,0:T(8,128)(2,1)}, bf16[64,32,128]{2,1,0:T(8,128)(2,1)}, u32[]{:S(2)}, u32[]{:S(2)}) %collective-permute-start.15) | collective-permute-done | bytes 524320 | tf_op jit(solution)/shard_map/cond/branch_1_fun/ppermute | solution.py:321
  167.5 1.3 copy-done.1
  168.8 10.4 %branch_1_fun.6 = bf16[256,128,128]{2,1,0:T(8,128)(2,1)} custom-call(s32[1]{0:T(128)} %get-tuple-element.47.replica, s32[256]{0:T(256)} %reshape.60.kept, bf16[64,32,128]{2,1,0:T(8,128)(2,1)} %get-tuple-element.52.refs_0_, bf16[64,32,128]{2,1,0:T(8,128)(2,1)} %get-tuple-element.53.refs_1_, bf16[64,32,128]{2,1,0:T(8,128)(2,1)} %collective-permute-done.12.refs_2_, ...), custom_call_target="tpu_custom_call" | custom-call | bytes 14680064 | tf_op jit(solution)/shard_map/cond/branch_1_fun/pallas_call | solution.py:297
  (36 shorter events, 1.5 us)
Async XLA Ops:
  13.9 35.0 %all-to-all-start.4 = ((bf16[32,272,128]{2,1,0:T(8,128)(2,1)}), bf16[32,272,128]{2,1,0:T(8,128)(2,1)S(1)}, u32[]{:S(2)}, u32[]{:S(2)}) async-start(bf16[32,272,128]{2,1,0:T(8,128)(2,1)} %bitcast.28), calls=%async_computation.4 | async-start | bytes 4456448 | tf_op jit(solution)/shard_map/all_to_all | solution.py:317
  54.1 28.5 %all-to-all-start.2 = ((bf16[32,208,128]{2,1,0:T(8,128)(2,1)}), bf16[32,208,128]{2,1,0:T(8,128)(2,1)S(1)}, u32[]{:S(2)}, u32[]{:S(2)}) async-start(bf16[32,208,128]{2,1,0:T(8,128)(2,1)} %bitcast.27), calls=%async_computation.2 | async-start | bytes 3407872 | tf_op jit(solution)/shard_map/cond/branch_1_fun/all_to_all | solution.py:317
  82.6 1.2 copy-start.2
  87.6 24.1 %copy-start.7 = (bf16[64,32,128]{2,1,0:T(8,128)(2,1)S(1)}, bf16[64,32,128]{2,1,0:T(8,128)(2,1)}, u32[]{:S(2)}) copy-start(bf16[64,32,128]{2,1,0:T(8,128)(2,1)} %get-tuple-element.52.refs_0_) | copy-start | bytes 1572868 | tf_op jit(solution)/shard_map/cond
  87.6 26.0 %copy-start.8 = (bf16[64,32,128]{2,1,0:T(8,128)(2,1)S(1)}, bf16[64,32,128]{2,1,0:T(8,128)(2,1)}, u32[]{:S(2)}) copy-start(bf16[64,32,128]{2,1,0:T(8,128)(2,1)} %get-tuple-element.53.refs_1_) | copy-start | bytes 1572868 | tf_op jit(solution)/shard_map/cond
  87.6 79.9 %all-to-all-start.3 = ((bf16[64,128,128]{2,1,0:T(8,128)(2,1)}), bf16[64,128,128]{2,1,0:T(8,128)(2,1)S(1)}, u32[]{:S(2)}, u32[]{:S(2)}) async-start(bf16[64,128,128]{2,1,0:T(8,128)(2,1)} %get-tuple-element.54), calls=%async_computation.3 | async-start | bytes 4194304 | tf_op jit(solution)/shard_map/cond/branch_1_fun/all_to_all | solution.py:317
  94.7 17.0 %collective-permute-start.20 = (bf16[64,32,128]{2,1,0:T(8,128)(2,1)}, bf16[64,32,128]{2,1,0:T(8,128)(2,1)S(1)}, u32[]{:S(2)}, u32[]{:S(2)}) collective-permute-start(bf16[64,32,128]{2,1,0:T(8,128)(2,1)} %get-tuple-element.55.refs_0_), channel_id=1, source_target_pairs={{0,32},{32,64},{64,96},{96,0},{1,33},{33,65},{65,97},{97,1},{2,34}... | collective-permute-start | bytes 1572872 | tf_op jit(solution)/shard_map/cond/branch_1_fun/ppermute | solution.py:321
  96.6 16.9 %collective-permute-start.19 = (bf16[64,32,128]{2,1,0:T(8,128)(2,1)}, bf16[64,32,128]{2,1,0:T(8,128)(2,1)S(1)}, u32[]{:S(2)}, u32[]{:S(2)}) collective-permute-start(bf16[64,32,128]{2,1,0:T(8,128)(2,1)} %get-tuple-element.56.refs_1_), channel_id=1, source_target_pairs={{0,96},{32,0},{64,32},{96,64},{1,97},{33,1},{65,33},{97,65},{2,98}... | collective-permute-start | bytes 1572872 | tf_op jit(solution)/shard_map/cond/branch_1_fun/ppermute | solution.py:325
  98.9 24.0 %collective-permute-start.18 = (bf16[64,32,128]{2,1,0:T(8,128)(2,1)}, bf16[64,32,128]{2,1,0:T(8,128)(2,1)S(1)}, u32[]{:S(2)}, u32[]{:S(2)}) collective-permute-start(bf16[64,32,128]{2,1,0:T(8,128)(2,1)} %get-tuple-element.55.refs_0_), channel_id=1, source_target_pairs={{0,96},{32,0},{64,32},{96,64},{1,97},{33,1},{65,33},{97,65},{2,98}... | collective-permute-start | bytes 1572872 | tf_op jit(solution)/shard_map/cond/branch_1_fun/ppermute | solution.py:325
  100.8 25.5 %collective-permute-start.23 = (bf16[64,32,128]{2,1,0:T(8,128)(2,1)}, bf16[64,32,128]{2,1,0:T(8,128)(2,1)S(1)}, u32[]{:S(2)}, u32[]{:S(2)}) collective-permute-start(bf16[64,32,128]{2,1,0:T(8,128)(2,1)} %get-tuple-element.56.refs_1_), channel_id=1, source_target_pairs={{0,32},{32,64},{64,96},{96,0},{1,33},{33,65},{65,97},{97,1},{2,34}... | collective-permute-start | bytes 1572872 | tf_op jit(solution)/shard_map/cond/branch_1_fun/ppermute | solution.py:321
  111.7 37.9 %copy-start.9 = (bf16[64,32,128]{2,1,0:T(8,128)(2,1)}, bf16[64,32,128]{2,1,0:T(8,128)(2,1)S(1)}, u32[]{:S(2)}) copy-start(bf16[64,32,128]{2,1,0:T(8,128)(2,1)S(1)} %collective-permute-done.20.refs_6_) | copy-start | bytes 1572868 | tf_op jit(solution)/shard_map/cond
  111.7 22.5 %collective-permute-start.21 = (bf16[64,32,128]{2,1,0:T(8,128)(2,1)S(1)}, bf16[64,32,128]{2,1,0:T(8,128)(2,1)S(1)}, u32[]{:S(2)}, u32[]{:S(2)}) collective-permute-start(bf16[64,32,128]{2,1,0:T(8,128)(2,1)S(1)} %collective-permute-done.20.refs_6_), channel_id=1, source_target_pairs={{0,32},{32,64},{64,96},{96,0},{1,33},{33,65},{65,97},{97,1},{2,34}... | collective-permute-start | bytes 1572872 | tf_op jit(solution)/shard_map/cond/branch_1_fun/ppermute | solution.py:321
  111.7 33.8 %collective-permute-start.14 = (bf16[64,32,128]{2,1,0:T(8,128)(2,1)S(1)}, bf16[64,32,128]{2,1,0:T(8,128)(2,1)}, u32[]{:S(2)}, u32[]{:S(2)}) collective-permute-start(bf16[64,32,128]{2,1,0:T(8,128)(2,1)S(1)} %copy-done.7), channel_id=1, source_target_pairs={{0,32},{32,64},{64,96},{96,0},{1,33},{33,65},{65,97},{97,1},{2,34}... | collective-permute-start | bytes 1572872 | tf_op jit(solution)/shard_map/cond/branch_1_fun/ppermute | solution.py:321
  113.6 32.0 %copy-start.10 = (bf16[64,32,128]{2,1,0:T(8,128)(2,1)}, bf16[64,32,128]{2,1,0:T(8,128)(2,1)S(1)}, u32[]{:S(2)}) copy-start(bf16[64,32,128]{2,1,0:T(8,128)(2,1)S(1)} %collective-permute-done.19.refs_3_) | copy-start | bytes 1572868 | tf_op jit(solution)/shard_map/cond
  113.6 31.9 %collective-permute-start.13 = (bf16[64,32,128]{2,1,0:T(8,128)(2,1)S(1)}, bf16[64,32,128]{2,1,0:T(8,128)(2,1)}, u32[]{:S(2)}, u32[]{:S(2)}) collective-permute-start(bf16[64,32,128]{2,1,0:T(8,128)(2,1)S(1)} %copy-done.8), channel_id=1, source_target_pairs={{0,96},{32,0},{64,32},{96,64},{1,97},{33,1},{65,33},{97,65},{2,98}... | collective-permute-start | bytes 1572872 | tf_op jit(solution)/shard_map/cond/branch_1_fun/ppermute | solution.py:325
  122.9 25.9 %copy-start.11 = (bf16[64,32,128]{2,1,0:T(8,128)(2,1)}, bf16[64,32,128]{2,1,0:T(8,128)(2,1)S(1)}, u32[]{:S(2)}) copy-start(bf16[64,32,128]{2,1,0:T(8,128)(2,1)S(1)} %collective-permute-done.18.refs_2_) | copy-start | bytes 1572868 | tf_op jit(solution)/shard_map/cond
  122.9 25.9 %collective-permute-start.22 = (bf16[64,32,128]{2,1,0:T(8,128)(2,1)S(1)}, bf16[64,32,128]{2,1,0:T(8,128)(2,1)S(1)}, u32[]{:S(2)}, u32[]{:S(2)}) collective-permute-start(bf16[64,32,128]{2,1,0:T(8,128)(2,1)S(1)} %collective-permute-done.19.refs_3_), channel_id=1, source_target_pairs={{0,96},{32,0},{64,32},{96,64},{1,97},{33,1},{65,33},{97,65},{2,98}... | collective-permute-start | bytes 1572872 | tf_op jit(solution)/shard_map/cond/branch_1_fun/ppermute | solution.py:325
  126.3 22.5 %copy-start.12 = (bf16[64,32,128]{2,1,0:T(8,128)(2,1)}, bf16[64,32,128]{2,1,0:T(8,128)(2,1)S(1)}, u32[]{:S(2)}) copy-start(bf16[64,32,128]{2,1,0:T(8,128)(2,1)S(1)} %collective-permute-done.23.refs_7_) | copy-start | bytes 1572868 | tf_op jit(solution)/shard_map/cond
  126.3 32.7 %collective-permute-start.12 = (bf16[64,32,128]{2,1,0:T(8,128)(2,1)S(1)}, bf16[64,32,128]{2,1,0:T(8,128)(2,1)}, u32[]{:S(2)}, u32[]{:S(2)}) collective-permute-start(bf16[64,32,128]{2,1,0:T(8,128)(2,1)S(1)} %copy-done.7), channel_id=1, source_target_pairs={{0,96},{32,0},{64,32},{96,64},{1,97},{33,1},{65,33},{97,65},{2,98}... | collective-permute-start | bytes 1572872 | tf_op jit(solution)/shard_map/cond/branch_1_fun/ppermute | solution.py:325
  134.2 14.6 %copy-start.13 = (bf16[64,32,128]{2,1,0:T(8,128)(2,1)}, bf16[64,32,128]{2,1,0:T(8,128)(2,1)S(1)}, u32[]{:S(2)}) copy-start(bf16[64,32,128]{2,1,0:T(8,128)(2,1)S(1)} %collective-permute-done.21.refs_4_) | copy-start | bytes 1572868 | tf_op jit(solution)/shard_map/cond
  134.2 24.9 %collective-permute-start.17 = (bf16[64,32,128]{2,1,0:T(8,128)(2,1)S(1)}, bf16[64,32,128]{2,1,0:T(8,128)(2,1)}, u32[]{:S(2)}, u32[]{:S(2)}) collective-permute-start(bf16[64,32,128]{2,1,0:T(8,128)(2,1)S(1)} %copy-done.8), channel_id=1, source_target_pairs={{0,32},{32,64},{64,96},{96,0},{1,33},{33,65},{65,97},{97,1},{2,34}... | collective-permute-start | bytes 1572872 | tf_op jit(solution)/shard_map/cond/branch_1_fun/ppermute | solution.py:321
  145.5 22.0 %collective-permute-start.15 = (bf16[64,32,128]{2,1,0:T(8,128)(2,1)}, bf16[64,32,128]{2,1,0:T(8,128)(2,1)}, u32[]{:S(2)}, u32[]{:S(2)}) collective-permute-start(bf16[64,32,128]{2,1,0:T(8,128)(2,1)} %collective-permute-done.14.refs_6_), channel_id=1, source_target_pairs={{0,32},{32,64},{64,96},{96,0},{1,33},{33,65},{65,97},{97,1},{2,34}... | collective-permute-start | bytes 1572872 | tf_op jit(solution)/shard_map/cond/branch_1_fun/ppermute | solution.py:321
  145.5 22.0 %collective-permute-start.16 = (bf16[64,32,128]{2,1,0:T(8,128)(2,1)}, bf16[64,32,128]{2,1,0:T(8,128)(2,1)}, u32[]{:S(2)}, u32[]{:S(2)}) collective-permute-start(bf16[64,32,128]{2,1,0:T(8,128)(2,1)} %collective-permute-done.13.refs_3_), channel_id=1, source_target_pairs={{0,96},{32,0},{64,32},{96,64},{1,97},{33,1},{65,33},{97,65},{2,98}... | collective-permute-start | bytes 1572872 | tf_op jit(solution)/shard_map/cond/branch_1_fun/ppermute | solution.py:325
  148.8 0.8 copy-start.14
  167.5 1.3 copy-start.1

commit v3 on v2

--- a/solution.py
+++ b/solution.py
@@ -11,6 +11,7 @@
 WRITERS = 32
 CAP = 8
 GROUP = 8
+GROUP_MOMENT = 16
 ROWS = 32
 TILE = 16
 SLOTS = WRITERS * CAP
@@ -52,63 +53,51 @@
     return pl.ds(pl.multiple_of(writer * payload_rows(by_rows) + k * ROWS, TILE), ROWS)
 
 
-def moment_kernel(blocks, replica, writer, weight_mask, moment_mask, moment, payload, coded, scales, slot_of, kept_w, kept_m, count, count_w, count_m):
-    step = pl.program_id(0)
+def moment_kernel(replica, writer, weight_mask, moment_mask, moment, payload, held, sems, tiles, totals, count):
     rows = row_quarter(replica)
-
-    @pl.when(step == 0)
-    def _():
-        clear(slot_of, SLOTS, blocks)
-        clear(kept_w, SLOTS, 0)
-        clear(kept_m, SLOTS, 0)
-        clear(count, WRITERS, 0)
-        clear(count_w, WRITERS, 0)
-        clear(count_m, WRITERS, 0)
-        coded[blocks] = jnp.zeros(coded.shape[1:], coded.dtype)
-        scales[pl.ds(blocks, 8), :] = jnp.zeros((8, 128), jnp.float32)
-
-    for i in range(GROUP):
-        block = step * GROUP + i
-        target = writer[block]
-        rank = count[target]
-        count[target] = rank + 1
-        slot = target * CAP + rank
-        slot_of[slot] = block
-        keep_w = weight_mask[block]
-        keep_m = keep_w * moment_mask[block]
-        kept_w[slot] = keep_w
-        kept_m[slot] = keep_m
-        count_w[target] = count_w[target] + jnp.where(rank < BY_ROWS_WEIGHT, keep_w, 0)
-        count_m[target] = count_m[target] + jnp.where(rank < BY_ROWS_MOMENT, keep_m, 0)
-        scale = scale_of(moment[i])
-        scales[pl.ds(block, 1), :] = scale[0:1, :]
-        coded[block] = (moment[i, rows, :] * (keep_m.astype(jnp.float32) / scale)[0:1, :]).astype(jnp.bfloat16)
-
-    @pl.when(step == blocks // GROUP - 1)
-    def _():
-        lane = lax.broadcasted_iota(jnp.int32, (TILE, 128), 1)
-        line = lax.broadcasted_iota(jnp.int32, (TILE, 128), 0)
-
-        def counts(w, tile):
-            both = jnp.where(line == 3, count_w[w].astype(jnp.float32), jnp.where(line == 4, count_m[w].astype(jnp.float32), 0.0))
-            return jnp.where(lane == w, both, tile)
-
-        common = lax.fori_loop(0, WRITERS, counts, jnp.zeros((TILE, 128), jnp.float32))
-
-        def one(w, carry):
-            tile = common
-            for k in range(CAP):
-                slot = w * CAP + k
-                block = slot_of[slot]
-                if k < BY_ROWS_MOMENT:
-                    payload[slot_rows(w, k, BY_ROWS_MOMENT), :] = coded[block]
-                scale = jnp.broadcast_to(scales[pl.ds(block, 1), :], (TILE, 128))
-                kept = jnp.where(line == 1, kept_w[slot].astype(jnp.float32), kept_m[slot].astype(jnp.float32))
-                tile = jnp.where((lane == k) & (line <= 2), jnp.where(line == 0, scale, kept), tile)
-            payload[tile_rows(w, BY_ROWS_MOMENT), :] = tile.astype(jnp.bfloat16)
-            return carry
-
-        lax.fori_loop(0, WRITERS, one, 0)
+    lane = lax.broadcasted_iota(jnp.int32, (8, 128), 1)
+    line = lax.broadcasted_iota(jnp.int32, (8, 128), 0)
+    steps = held.shape[0] // GROUP_MOMENT
+
+    def fetch(step):
+        part = pl.ds(step * GROUP_MOMENT, GROUP_MOMENT)
+        return pltpu.make_async_copy(moment.at[part], held.at[part], sems.at[step])
+
+    for step in range(steps):
+        fetch(step).start()
+    clear(count, WRITERS, 0)
+    tiles[...] = jnp.zeros(tiles.shape, tiles.dtype)
+    totals[...] = jnp.zeros(totals.shape, totals.dtype)
+
+    def one_step(step, carry):
+        fetch(step).wait()
+        total = totals[...]
+        for i in range(GROUP_MOMENT):
+            block = step * GROUP_MOMENT + i
+            target = writer[block]
+            rank = count[target]
+            count[target] = rank + 1
+            keep_w = weight_mask[block].astype(jnp.float32)
+            keep_m = keep_w * moment_mask[block].astype(jnp.float32)
+            counted_w = jnp.where(rank < BY_ROWS_WEIGHT, keep_w, 0.0)
+            total = total + jnp.where(lane == target, jnp.where(line == 3, counted_w, jnp.where(line == 4, keep_m, 0.0)), 0.0)
+            scale = scale_of(held[block])
+            kept = jnp.where(line == 0, scale, jnp.where(line == 1, keep_w, jnp.where(line == 2, keep_m, 0.0)))
+            tiles[target] = jnp.where(lane == rank, kept, tiles[target])
+            payload[slot_rows(target, rank, BY_ROWS_MOMENT), :] = (held[block, rows, :] * (keep_m / scale)[0:1, :]).astype(jnp.bfloat16)
+        totals[...] = total
+        return carry
+
+    lax.fori_loop(0, steps, one_step, 0)
+    common = totals[...]
+    blank = jnp.zeros((TILE - 8, 128), jnp.float32)
+
+    def one(w, carry):
+        tile = jnp.concatenate([tiles[w] + common, blank], axis=0)
+        payload[tile_rows(w, BY_ROWS_MOMENT), :] = tile.astype(jnp.bfloat16)
+        return carry
+
+    lax.fori_loop(0, WRITERS, one, 0, unroll=4)
 
 
 def weight_kernel(blocks, replica, writer, weight_mask, base_scale, weight, codes, payload, whole, refreshed, coded, scales, slot_of, count):
@@ -168,20 +157,17 @@
     blocks, width = moment.shape[0], moment.shape[1]
     shape = (WRITERS * payload_rows(BY_ROWS_MOMENT), width)
     return pl.pallas_call(
-        functools.partial(moment_kernel, blocks),
+        moment_kernel,
         grid_spec=pltpu.PrefetchScalarGridSpec(
             num_scalar_prefetch=4,
-            grid=(blocks // GROUP,),
-            in_specs=[pl.BlockSpec((GROUP, width, width), lambda i, *_: (i, 0, 0))],
+            grid=(1,),
+            in_specs=[pl.BlockSpec(memory_space=pl.ANY)],
             out_specs=pl.BlockSpec(shape, lambda i, *_: (0, 0)),
             scratch_shapes=[
-                pltpu.VMEM((blocks + 1, ROWS, width), jnp.bfloat16),
-                pltpu.VMEM((blocks + 8, 128), jnp.float32),
-                pltpu.SMEM((SLOTS,), jnp.int32),
-                pltpu.SMEM((SLOTS,), jnp.int32),
-                pltpu.SMEM((SLOTS,), jnp.int32),
-                pltpu.SMEM((WRITERS,), jnp.int32),
-                pltpu.SMEM((WRITERS,), jnp.int32),
+                pltpu.VMEM(moment.shape, jnp.float32),
+                pltpu.SemaphoreType.DMA((blocks // GROUP_MOMENT,)),
+                pltpu.VMEM((WRITERS, 8, 128), jnp.float32),
+                pltpu.VMEM((8, 128), jnp.float32),
                 pltpu.SMEM((WRITERS,), jnp.int32),
             ],
         ),
@@ -220,7 +206,9 @@
     )(replica, writer, weight_mask, base_scale, weight, codes)
 
 
-def pack_kernel(by_rows, half, kept, payload, _, first, second, passed, packed):
+def pack_kernel(by_rows, half, kept, payload, *refs):
+    first, second, _, packed = refs[-4:]
+
     def one(s, place):
         for k in range(by_rows):
             packed[place] = payload[slot_rows(s, k, by_rows), :]
@@ -232,7 +220,7 @@
     second[...] = packed[half : 2 * half]
 
 
-def pack_call(by_rows, capacity, kept, payload, later):
+def pack_call(by_rows, capacity, kept, payload, later, earlier=()):
     width = payload.shape[-1]
     half = capacity // 2
     part = (half, ROWS, width)
@@ -241,7 +229,7 @@
         grid_spec=pltpu.PrefetchScalarGridSpec(
             num_scalar_prefetch=1,
             grid=(1,),
-            in_specs=[pl.BlockSpec(payload.shape, lambda i, *_: (0, 0)), pl.BlockSpec(memory_space=pl.ANY)],
+            in_specs=[pl.BlockSpec(payload.shape, lambda i, *_: (0, 0))] + [pl.BlockSpec(memory_space=pl.ANY)] * (1 + len(earlier)),
             out_specs=[pl.BlockSpec(part, lambda i, *_: (0, 0, 0))] * 2 + [pl.BlockSpec(memory_space=pl.ANY)],
             scratch_shapes=[pltpu.VMEM((capacity, ROWS, width), jnp.bfloat16)],
         ),
@@ -249,7 +237,7 @@
         input_output_aliases={2: 2},
         compiler_params=params(),
         cost_estimate=cost(0, 4 << 20),
-    )(kept, payload, later)
+    )(kept, payload, later, *earlier)
 
 
 SOURCES = 4
@@ -257,55 +245,66 @@
 
 def unpack_kernel(by_rows, half, replica, kept, *refs):
     parts, refs = refs[:8], refs[8:]
-    if by_rows < CAP:
+    n_whole = CAP - by_rows
+    if n_whole:
         whole, refs = refs[0], refs[1:]
-    out, held, sems, place_ref = refs
-    step = pl.program_id(0)
-
-    @pl.when(step == 0)
-    def _():
-        place_ref[0] = 0
-        copies = [
-            pltpu.make_async_copy(part, held.at[i // 2, pl.ds((i % 2) * half, half)], sems.at[i]) for i, part in enumerate(parts)
-        ]
-        for copy in copies:
-            copy.start()
-        for copy in copies:
-            copy.wait()
-
+    out, held, built, sems, out_sems = refs[:5]
+    copies = [pltpu.make_async_copy(part, held.at[i // 2, pl.ds((i % 2) * half, half)], sems.at[i]) for i, part in enumerate(parts)]
+    if n_whole:
+        copies.append(pltpu.make_async_copy(whole, refs[5], sems.at[8]))
+    for copy in copies:
+        copy.start()
+    for turn in range(4):
+        held[turn, 2 * half] = jnp.zeros(held.shape[2:], held.dtype)
+    for copy in copies:
+        copy.wait()
     rows = [pl.ds(pl.multiple_of(lax.rem(replica[0] + turn, 4) * ROWS, ROWS), ROWS) for turn in range(4)]
-    place = place_ref[0]
-    for s in range(SOURCES):
-        for k in range(by_rows):
-            flag = kept[(step * SOURCES + s) * CAP + k]
-            for turn in range(4):
-                values = held[turn, place]
-                out[s * CAP + k, rows[turn], :] = jnp.where(flag > 0, values, jnp.zeros_like(values))
-            place = place + flag
-        for k in range(by_rows, CAP):
-            out[s * CAP + k] = whole[s * (CAP - by_rows) + k - by_rows]
-    place_ref[0] = place
+
+    def send(step):
+        part = pl.ds(step * SOURCES * CAP, SOURCES * CAP)
+        return pltpu.make_async_copy(built.at[part], out.at[part], out_sems.at[step])
+
+    def one(step, place):
+        for s in range(SOURCES):
+            source = step * SOURCES + s
+            for k in range(by_rows):
+                slot = source * CAP + k
+                flag = kept[slot]
+                origin = jnp.where(flag > 0, place, 2 * half)
+                for turn in range(4):
+                    built[slot, rows[turn], :] = held[turn, origin]
+                place = place + flag
+            for k in range(n_whole):
+                built[source * CAP + by_rows + k] = refs[5][source * n_whole + k]
+        send(step).start()
+        return place
+
+    steps = WRITERS // SOURCES
+    lax.fori_loop(0, steps, one, 0)
+    for step in range(steps):
+        send(step).wait()
 
 
 def unpack_call(by_rows, capacity, replica, kept, parts, whole):
     width = parts[0].shape[-1]
     half = capacity // 2
-    specs = [pl.BlockSpec(memory_space=pl.ANY)] * 8
+    scratch = [
+        pltpu.VMEM((4, capacity + 1, ROWS, width), jnp.bfloat16),
+        pltpu.VMEM((SLOTS, width, width), jnp.bfloat16),
+        pltpu.SemaphoreType.DMA((9,)),
+        pltpu.SemaphoreType.DMA((WRITERS // SOURCES,)),
+    ]
     if whole is not None:
-        specs.append(pl.BlockSpec((SOURCES * (CAP - by_rows), width, width), lambda i, *_: (i, 0, 0)))
         parts = (*parts, whole)
+        scratch.append(pltpu.VMEM(whole.shape, whole.dtype))
     return pl.pallas_call(
         functools.partial(unpack_kernel, by_rows, half),
         grid_spec=pltpu.PrefetchScalarGridSpec(
             num_scalar_prefetch=2,
-            grid=(WRITERS // SOURCES,),
-            in_specs=specs,
-            out_specs=pl.BlockSpec((SOURCES * CAP, width, width), lambda i, *_: (i, 0, 0)),
-            scratch_shapes=[
-                pltpu.VMEM((4, capacity, ROWS, width), jnp.bfloat16),
-                pltpu.SemaphoreType.DMA((8,)),
-                pltpu.SMEM((1,), jnp.int32),
-            ],
+            grid=(1,),
+            in_specs=[pl.BlockSpec(memory_space=pl.ANY)] * len(parts),
+            out_specs=pl.BlockSpec(memory_space=pl.ANY),
+            scratch_shapes=scratch,
         ),
         out_shape=jax.ShapeDtypeStruct((SLOTS, width, width), jnp.bfloat16),
         compiler_params=params(),
@@ -335,7 +334,7 @@
     m_first, m_second, w_payload = pack_call(BY_ROWS_MOMENT, capacities[0], kept_m, m_payload, w_payload)
     m_parts = gather_rows(m_first, m_second)
     w_payload = regroup(w_payload)
-    w_first, w_second, w_whole = pack_call(BY_ROWS_WEIGHT, capacities[1], kept_w, w_payload, w_whole)
+    w_first, w_second, w_whole = pack_call(BY_ROWS_WEIGHT, capacities[1], kept_w, w_payload, w_whole, m_parts[2:])
     w_parts = gather_rows(w_first, w_second)
     w_whole = regroup(w_whole)
     written_moment = unpack_call(BY_ROWS_MOMENT, capacities[0], replica, kept_m, m_parts, None)

time: 182 us -> 154 us (0.85)
  waiting for transfers between devices: 76.8 us -> 61.3 us
  Pallas kernels: 55.4 us -> 42.5 us
    all_to_all x3, waiting for transfers between devices: 31.2 us -> 10.3 us  [regroup(): lax.all_to_all(values, 'fsdp', split_axis=0, concat_axis=0, tiled=True)]
    pallas_call x1, Pallas kernels: 13.3 us -> 5.76 us  [moment_call(): pl.pallas_call(moment_kernel, grid_spec=pltpu.PrefetchScalarGridSpec(num_...]
    pallas_call x2, Pallas kernels: 18.8 us -> 13.4 us  [unpack_call(): pl.pallas_call(functools.partial(unpack_kernel, by_rows, half), grid_spec...]
    ppermute x6, waiting for transfers between devices: 37.7 us -> 43 us  [upward(): return lax.ppermute(values, 'replica', [(i, (i + 1) % 4) for i in range(4)])]
  transfers between devices with their start and end apart: 15 -> 15, of which waited for: 7 -> 8; matrix products, arithmetic and copies ran while one was open for 1% -> 1% of each run, Pallas kernels for 14% -> 15%
where the time goes in v3:
time: 154 us; the launch traced here: 153 us
  waiting for transfers between devices  61.3 us (40%)
  Pallas kernels  42.5 us (28%)
  starting transfers between devices  40.4 us (26%)
  local copies, waits for them, and re-layouts  5.49 us (4%)
    ppermute x6, waiting for transfers between devices, upward(): return lax.ppermute(values, 'replica', [(i, (i + 1) % 4) for i in range(4)])  43 us
    all_to_all x3, starting transfers between devices, regroup(): lax.all_to_all(values, 'fsdp', split_axis=0, concat_axis=0, tiled=True)  22.3 us
    pallas_call x1, Pallas kernels, weight_call(): pl.pallas_call(functools.partial(weight_kernel, blocks), grid_spec=pltpu....  17.1 us
    ppermute x6, starting transfers between devices, downward(): return lax.ppermute(values, 'replica', [(i, (i - 1) % 4) for i in range(4)])  14.5 us
    pallas_call x2, Pallas kernels, unpack_call(): pl.pallas_call(functools.partial(unpack_kernel, by_rows, half), grid_spec...  13.4 us
    all_to_all x3, waiting for transfers between devices, regroup(): lax.all_to_all(values, 'fsdp', split_axis=0, concat_axis=0, tiled=True)  10.3 us
    ppermute x6, waiting for transfers between devices, downward(): return lax.ppermute(values, 'replica', [(i, (i - 1) % 4) for i in range(4)])  8 us
    pallas_call x2, Pallas kernels, pack_call(): pl.pallas_call(functools.partial(pack_kernel, by_rows, half), grid_spec=p...  6.27 us
  transfers between devices with their start and end apart: 15, of which 8 were waited for; matrix products, arithmetic and copies ran while one was open for 1% of the time, Pallas kernels for 15%

profile of v3, /device:TPU:2, one launch (start us, length us, event | category | flops | bytes accessed | tf_op | source)
XLA Modules:
  0.0 152.7 jit_solution(13085411619230754890)
XLA Ops:
  0.6 5.8 %shard_map.111 = bf16[8704,128]{1,0:T(8,128)(2,1)} custom-call(s32[1]{0:T(128)} %bitcast.12.replica, s32[128]{0:T(128)} %bitcast.38, s32[128]{0:T(128)} %weight_mask.3, s32[128]{0:T(128)} %moment_mask.1, f32[128,128,128]{2,1,0:T(8,128)} %moment.1), custom_call_target="tpu_custom_call" | custom-call | flops 10485760 | bytes 12582912 | tf_op jit(solution)/shard_map/pallas_call | solution.py:159
  6.4 7.6 %all-to-all-start.4 = ((bf16[32,272,128]{2,1,0:T(8,128)(2,1)}), bf16[32,272,128]{2,1,0:T(8,128)(2,1)S(1)}, u32[]{:S(2)}, u32[]{:S(2)}) async-start(bf16[32,272,128]{2,1,0:T(8,128)(2,1)} %bitcast.28), calls=%async_computation.4 | async-start | bytes 4456448 | tf_op jit(solution)/shard_map/all_to_all | solution.py:316
  14.1 17.1 %shard_map.112 = (bf16[6656,128]{1,0:T(8,128)(2,1)}, bf16[64,128,128]{2,1,0:T(8,128)(2,1)}, bf16[128,128,128]{2,1,0:T(8,128)(2,1)}) custom-call(s32[1]{0:T(128)} %bitcast.12.replica, s32[128]{0:T(128)} %bitcast.39, s32[128]{0:T(128)} %weight_mask.3, f32[128]{0:T(128)} %base_scale.1, f32[128,128,128]{2,1,0:T(8,128)} %weight.1, s32[128,128,128]{2,1,0:T(8,128)} %codes.1), custom_call_target="tpu_custom_call" | custom-call | flops 20971520 | bytes 29360128 | tf_op jit(solution)/shard_map/pallas_call | solution.py:185
  31.1 10.3 %all-to-all-done.4 = bf16[32,272,128]{2,1,0:T(8,128)(2,1)S(1)} async-done(((bf16[32,272,128]{2,1,0:T(8,128)(2,1)}), bf16[32,272,128]{2,1,0:T(8,128)(2,1)S(1)}, u32[]{:S(2)}, u32[]{:S(2)}) %all-to-all-start.4) | async-done | bytes 2228256 | tf_op jit(solution)/shard_map/all_to_all | solution.py:316
  41.5 0.6 compare_reduce_fusion
  42.9 109.2 %conditional.1 = (bf16[32,8,128,128]{3,2,1,0:T(8,128)(2,1)}, bf16[32,8,128,128]{3,2,1,0:T(8,128)(2,1)}, bf16[1,32,8]{1,2,0:T(8,128)(2,1)S(1)}) conditional(s32[]{:T(128)} %convert_element_type.35, (bf16[32,272,128]{2,1,0:T(8,128)(2,1)S(1)}, bf16[6656,128]{1,0:T(8,128)(2,1)}, bf16[64,128,128]{2,1,0:T(8,128)(2,1)}, s32[1]{0:T(128)}) %tuple.22, ...), branch_computations={%region_2.0_spmd, %region_3.0_spmd} | conditional | flops 512 | bytes 122037936 | solution.py:357
  43.4 0.7 reshape.61.kept
  44.1 2.5 %branch_1_fun.4 = (bf16[64,32,128]{2,1,0:T(8,128)(2,1)}, bf16[64,32,128]{2,1,0:T(8,128)(2,1)}, bf16[6656,128]{1,0:T(8,128)(2,1)}) custom-call(s32[256]{0:T(256)} %reshape.61.kept, bf16[8704,128]{1,0:T(8,128)(2,1)S(1)} %bitcast.25, bf16[6656,128]{1,0:T(8,128)(2,1)} %get-tuple-element.49.refs_0_), custom_call_target="tpu_custom_call", output_to_operand_aliasing={{2}: (2, {})} | custom-call | bytes 4194304 | tf_op jit(solution)/shard_map/cond/branch_1_fun/pallas_call | solution.py:227
  46.6 6.9 %all-to-all-start.2 = ((bf16[32,208,128]{2,1,0:T(8,128)(2,1)}), bf16[32,208,128]{2,1,0:T(8,128)(2,1)S(1)}, u32[]{:S(2)}, u32[]{:S(2)}) async-start(bf16[32,208,128]{2,1,0:T(8,128)(2,1)} %bitcast.27), calls=%async_computation.2 | async-start | bytes 3407872 | tf_op jit(solution)/shard_map/cond/branch_1_fun/all_to_all | solution.py:316
  53.6 2.0 %collective-permute-start.14 = (bf16[64,32,128]{2,1,0:T(8,128)(2,1)}, bf16[64,32,128]{2,1,0:T(8,128)(2,1)S(1)}, u32[]{:S(2)}, u32[]{:S(2)}) collective-permute-start(bf16[64,32,128]{2,1,0:T(8,128)(2,1)} %get-tuple-element.52.refs_0_), channel_id=1, source_target_pairs={{0,32},{32,64},{64,96},{96,0},{1,33},{33,65},{65,97},{97,1},{2,34}... | collective-permute-start | bytes 1572872 | tf_op jit(solution)/shard_map/cond/branch_1_fun/ppermute | solution.py:320
  55.6 2.2 %collective-permute-start.13 = (bf16[64,32,128]{2,1,0:T(8,128)(2,1)}, bf16[64,32,128]{2,1,0:T(8,128)(2,1)S(1)}, u32[]{:S(2)}, u32[]{:S(2)}) collective-permute-start(bf16[64,32,128]{2,1,0:T(8,128)(2,1)} %get-tuple-element.53.refs_1_), channel_id=1, source_target_pairs={{0,96},{32,0},{64,32},{96,64},{1,97},{33,1},{65,33},{97,65},{2,98}... | collective-permute-start | bytes 1572872 | tf_op jit(solution)/shard_map/cond/branch_1_fun/ppermute | solution.py:324
  57.8 1.9 %collective-permute-start.12 = (bf16[64,32,128]{2,1,0:T(8,128)(2,1)}, bf16[64,32,128]{2,1,0:T(8,128)(2,1)S(1)}, u32[]{:S(2)}, u32[]{:S(2)}) collective-permute-start(bf16[64,32,128]{2,1,0:T(8,128)(2,1)} %get-tuple-element.52.refs_0_), channel_id=1, source_target_pairs={{0,96},{32,0},{64,32},{96,64},{1,97},{33,1},{65,33},{97,65},{2,98}... | collective-permute-start | bytes 1572872 | tf_op jit(solution)/shard_map/cond/branch_1_fun/ppermute | solution.py:324
  59.8 10.8 %collective-permute-done.14.refs_5_.refs_6_ = bf16[64,32,128]{2,1,0:T(8,128)(2,1)S(1)} collective-permute-done((bf16[64,32,128]{2,1,0:T(8,128)(2,1)}, bf16[64,32,128]{2,1,0:T(8,128)(2,1)S(1)}, u32[]{:S(2)}, u32[]{:S(2)}) %collective-permute-start.14) | collective-permute-done | bytes 524320 | tf_op jit(solution)/shard_map/cond/branch_1_fun/ppermute | solution.py:320
  70.6 3.3 %collective-permute-start.16 = (bf16[64,32,128]{2,1,0:T(8,128)(2,1)S(1)}, bf16[64,32,128]{2,1,0:T(8,128)(2,1)}, u32[]{:S(2)}, u32[]{:S(2)}) collective-permute-start(bf16[64,32,128]{2,1,0:T(8,128)(2,1)S(1)} %collective-permute-done.13.refs_2_.refs_3_), channel_id=1, source_target_pairs={{0,96},{32,0},{64,32},{96,64},{1,97},{33,1},{65,33},{97,65},{2,98}... | collective-permute-start | bytes 1572872 | tf_op jit(solution)/shard_map/cond/branch_1_fun/ppermute | solution.py:324
  74.0 0.7 reshape.60.kept
  74.6 7.2 %collective-permute-done.12.refs_1_.refs_2_ = bf16[64,32,128]{2,1,0:T(8,128)(2,1)S(1)} collective-permute-done((bf16[64,32,128]{2,1,0:T(8,128)(2,1)}, bf16[64,32,128]{2,1,0:T(8,128)(2,1)S(1)}, u32[]{:S(2)}, u32[]{:S(2)}) %collective-permute-start.12) | collective-permute-done | bytes 524320 | tf_op jit(solution)/shard_map/cond/branch_1_fun/ppermute | solution.py:324
  81.9 10.8 %collective-permute-done.15.refs_3_.refs_4_ = bf16[64,32,128]{2,1,0:T(8,128)(2,1)} collective-permute-done((bf16[64,32,128]{2,1,0:T(8,128)(2,1)S(1)}, bf16[64,32,128]{2,1,0:T(8,128)(2,1)}, u32[]{:S(2)}, u32[]{:S(2)}) %collective-permute-start.15) | collective-permute-done | bytes 524320 | tf_op jit(solution)/shard_map/cond/branch_1_fun/ppermute | solution.py:320
  92.7 1.2 copy-done.2
  93.9 3.8 %branch_1_fun.5 = (bf16[64,32,128]{2,1,0:T(8,128)(2,1)}, bf16[64,32,128]{2,1,0:T(8,128)(2,1)}, bf16[64,128,128]{2,1,0:T(8,128)(2,1)}) custom-call(s32[256]{0:T(256)} %reshape.60.kept, bf16[6656,128]{1,0:T(8,128)(2,1)} %bitcast.33, bf16[64,128,128]{2,1,0:T(8,128)(2,1)} %get-tuple-element.51.refs_0_, ...), custom_call_target="tpu_custom_call", output_to_operand_aliasing={{2}: (2, {})} | custom-call | bytes 4194304 | tf_op jit(solution)/shard_map/cond/branch_1_fun/pallas_call | solution.py:227
  97.7 7.8 %all-to-all-start.3 = ((bf16[64,128,128]{2,1,0:T(8,128)(2,1)}), bf16[64,128,128]{2,1,0:T(8,128)(2,1)S(1)}, u32[]{:S(2)}, u32[]{:S(2)}) async-start(bf16[64,128,128]{2,1,0:T(8,128)(2,1)} %get-tuple-element.56), calls=%async_computation.3 | async-start | bytes 4194304 | tf_op jit(solution)/shard_map/cond/branch_1_fun/all_to_all | solution.py:316
  105.4 1.3 collective-permute-start.20
  106.8 2.0 %collective-permute-start.19 = (bf16[64,32,128]{2,1,0:T(8,128)(2,1)S(1)}, bf16[64,32,128]{2,1,0:T(8,128)(2,1)}, u32[]{:S(2)}, u32[]{:S(2)}) collective-permute-start(bf16[64,32,128]{2,1,0:T(8,128)(2,1)S(1)} %copy-done.10), channel_id=1, source_target_pairs={{0,96},{32,0},{64,32},{96,64},{1,97},{33,1},{65,33},{97,65},{2,98}... | collective-permute-start | bytes 1572872 | tf_op jit(solution)/shard_map/cond/branch_1_fun/ppermute | solution.py:324
  108.7 1.8 %collective-permute-start.18 = (bf16[64,32,128]{2,1,0:T(8,128)(2,1)S(1)}, bf16[64,32,128]{2,1,0:T(8,128)(2,1)}, u32[]{:S(2)}, u32[]{:S(2)}) collective-permute-start(bf16[64,32,128]{2,1,0:T(8,128)(2,1)S(1)} %copy-done.9), channel_id=1, source_target_pairs={{0,96},{32,0},{64,32},{96,64},{1,97},{33,1},{65,33},{97,65},{2,98}... | collective-permute-start | bytes 1572872 | tf_op jit(solution)/shard_map/cond/branch_1_fun/ppermute | solution.py:324
  110.8 10.8 %collective-permute-done.20.refs_6_ = bf16[64,32,128]{2,1,0:T(8,128)(2,1)} collective-permute-done((bf16[64,32,128]{2,1,0:T(8,128)(2,1)S(1)}, bf16[64,32,128]{2,1,0:T(8,128)(2,1)}, u32[]{:S(2)}, u32[]{:S(2)}) %collective-permute-start.20) | collective-permute-done | bytes 524320 | tf_op jit(solution)/shard_map/cond/branch_1_fun/ppermute | solution.py:320
  121.7 3.2 %collective-permute-start.22 = (bf16[64,32,128]{2,1,0:T(8,128)(2,1)}, bf16[64,32,128]{2,1,0:T(8,128)(2,1)}, u32[]{:S(2)}, u32[]{:S(2)}) collective-permute-start(bf16[64,32,128]{2,1,0:T(8,128)(2,1)} %collective-permute-done.19.refs_3_), channel_id=1, source_target_pairs={{0,96},{32,0},{64,32},{96,64},{1,97},{33,1},{65,33},{97,65},{2,98}... | collective-permute-start | bytes 1572872 | tf_op jit(solution)/shard_map/cond/branch_1_fun/ppermute | solution.py:324
  124.9 6.3 %branch_1_fun.7 = bf16[256,128,128]{2,1,0:T(8,128)(2,1)} custom-call(s32[1]{0:T(128)} %get-tuple-element.47.replica, s32[256]{0:T(256)} %reshape.61.kept, bf16[64,32,128]{2,1,0:T(8,128)(2,1)} %get-tuple-element.52.refs_0_, bf16[64,32,128]{2,1,0:T(8,128)(2,1)} %get-tuple-element.53.refs_1_, bf16[64,32,128]{2,1,0:T(8,128)(2,1)} %copy-done.7, ...), custom_call_target="tpu_custom_call" | custom-call | bytes 14680064 | tf_op jit(solution)/shard_map/cond/branch_1_fun/pallas_call | solution.py:300
  131.2 0.9 slice.38
  132.1 0.8 collective-permute-done.18.refs_2_
  132.9 10.4 %collective-permute-done.21.refs_4_ = bf16[64,32,128]{2,1,0:T(8,128)(2,1)} collective-permute-done((bf16[64,32,128]{2,1,0:T(8,128)(2,1)}, bf16[64,32,128]{2,1,0:T(8,128)(2,1)}, u32[]{:S(2)}, u32[]{:S(2)}) %collective-permute-start.21) | collective-permute-done | bytes 524320 | tf_op jit(solution)/shard_map/cond/branch_1_fun/ppermute | solution.py:320
  143.4 1.4 copy-done.1
  144.8 7.1 %branch_1_fun.6 = bf16[256,128,128]{2,1,0:T(8,128)(2,1)} custom-call(s32[1]{0:T(128)} %get-tuple-element.47.replica, s32[256]{0:T(256)} %reshape.60.kept, bf16[64,32,128]{2,1,0:T(8,128)(2,1)} %get-tuple-element.54.refs_0_, bf16[64,32,128]{2,1,0:T(8,128)(2,1)} %get-tuple-element.55.refs_1_, bf16[64,32,128]{2,1,0:T(8,128)(2,1)} %collective-permute-done.18.refs_2_, ...), custom_call_target="tpu_custom_call" | custom-call | bytes 14680064 | tf_op jit(solution)/shard_map/cond/branch_1_fun/pallas_call | solution.py:300
  152.1 0.6 pad_maximum_fusion
  (30 shorter events, 1.4 us)
Async XLA Ops:
  6.4 35.0 %all-to-all-start.4 = ((bf16[32,272,128]{2,1,0:T(8,128)(2,1)}), bf16[32,272,128]{2,1,0:T(8,128)(2,1)S(1)}, u32[]{:S(2)}, u32[]{:S(2)}) async-start(bf16[32,272,128]{2,1,0:T(8,128)(2,1)} %bitcast.28), calls=%async_computation.4 | async-start | bytes 4456448 | tf_op jit(solution)/shard_map/all_to_all | solution.py:316
  46.6 46.1 %all-to-all-start.2 = ((bf16[32,208,128]{2,1,0:T(8,128)(2,1)}), bf16[32,208,128]{2,1,0:T(8,128)(2,1)S(1)}, u32[]{:S(2)}, u32[]{:S(2)}) async-start(bf16[32,208,128]{2,1,0:T(8,128)(2,1)} %bitcast.27), calls=%async_computation.2 | async-start | bytes 3407872 | tf_op jit(solution)/shard_map/cond/branch_1_fun/all_to_all | solution.py:316
  53.6 17.0 %collective-permute-start.14 = (bf16[64,32,128]{2,1,0:T(8,128)(2,1)}, bf16[64,32,128]{2,1,0:T(8,128)(2,1)S(1)}, u32[]{:S(2)}, u32[]{:S(2)}) collective-permute-start(bf16[64,32,128]{2,1,0:T(8,128)(2,1)} %get-tuple-element.52.refs_0_), channel_id=1, source_target_pairs={{0,32},{32,64},{64,96},{96,0},{1,33},{33,65},{65,97},{97,1},{2,34}... | collective-permute-start | bytes 1572872 | tf_op jit(solution)/shard_map/cond/branch_1_fun/ppermute | solution.py:320
  55.6 15.0 %collective-permute-start.13 = (bf16[64,32,128]{2,1,0:T(8,128)(2,1)}, bf16[64,32,128]{2,1,0:T(8,128)(2,1)S(1)}, u32[]{:S(2)}, u32[]{:S(2)}) collective-permute-start(bf16[64,32,128]{2,1,0:T(8,128)(2,1)} %get-tuple-element.53.refs_1_), channel_id=1, source_target_pairs={{0,96},{32,0},{64,32},{96,64},{1,97},{33,1},{65,33},{97,65},{2,98}... | collective-permute-start | bytes 1572872 | tf_op jit(solution)/shard_map/cond/branch_1_fun/ppermute | solution.py:324
  57.8 24.0 %collective-permute-start.12 = (bf16[64,32,128]{2,1,0:T(8,128)(2,1)}, bf16[64,32,128]{2,1,0:T(8,128)(2,1)S(1)}, u32[]{:S(2)}, u32[]{:S(2)}) collective-permute-start(bf16[64,32,128]{2,1,0:T(8,128)(2,1)} %get-tuple-element.52.refs_0_), channel_id=1, source_target_pairs={{0,96},{32,0},{64,32},{96,64},{1,97},{33,1},{65,33},{97,65},{2,98}... | collective-permute-start | bytes 1572872 | tf_op jit(solution)/shard_map/cond/branch_1_fun/ppermute | solution.py:324
  59.7 22.2 %collective-permute-start.17 = (bf16[64,32,128]{2,1,0:T(8,128)(2,1)}, bf16[64,32,128]{2,1,0:T(8,128)(2,1)}, u32[]{:S(2)}, u32[]{:S(2)}) collective-permute-start(bf16[64,32,128]{2,1,0:T(8,128)(2,1)} %get-tuple-element.53.refs_1_), channel_id=1, source_target_pairs={{0,32},{32,64},{64,96},{96,0},{1,33},{33,65},{65,97},{97,1},{2,34}... | collective-permute-start | bytes 1572872 | tf_op jit(solution)/shard_map/cond/branch_1_fun/ppermute | solution.py:320
  70.6 22.1 %copy-start.5 = (bf16[64,32,128]{2,1,0:T(8,128)(2,1)}, bf16[64,32,128]{2,1,0:T(8,128)(2,1)S(1)}, u32[]{:S(2)}) copy-start(bf16[64,32,128]{2,1,0:T(8,128)(2,1)S(1)} %collective-permute-done.14.refs_5_.refs_6_) | copy-start | bytes 1572868 | tf_op jit(solution)/shard_map/cond
  70.6 22.1 %collective-permute-start.15 = (bf16[64,32,128]{2,1,0:T(8,128)(2,1)S(1)}, bf16[64,32,128]{2,1,0:T(8,128)(2,1)}, u32[]{:S(2)}, u32[]{:S(2)}) collective-permute-start(bf16[64,32,128]{2,1,0:T(8,128)(2,1)S(1)} %collective-permute-done.14.refs_5_.refs_6_), channel_id=1, source_target_pairs={{0,32},{32,64},{64,96},{96,0},{1,33},{33,65},{65,97},{97,1},{2,34}... | collective-permute-start | bytes 1572872 | tf_op jit(solution)/shard_map/cond/branch_1_fun/ppermute | solution.py:320
  70.6 22.1 %copy-start.6 = (bf16[64,32,128]{2,1,0:T(8,128)(2,1)}, bf16[64,32,128]{2,1,0:T(8,128)(2,1)S(1)}, u32[]{:S(2)}) copy-start(bf16[64,32,128]{2,1,0:T(8,128)(2,1)S(1)} %collective-permute-done.13.refs_2_.refs_3_) | copy-start | bytes 1572868 | tf_op jit(solution)/shard_map/cond
  70.6 22.1 %collective-permute-start.16 = (bf16[64,32,128]{2,1,0:T(8,128)(2,1)S(1)}, bf16[64,32,128]{2,1,0:T(8,128)(2,1)}, u32[]{:S(2)}, u32[]{:S(2)}) collective-permute-start(bf16[64,32,128]{2,1,0:T(8,128)(2,1)S(1)} %collective-permute-done.13.refs_2_.refs_3_), channel_id=1, source_target_pairs={{0,96},{32,0},{64,32},{96,64},{1,97},{33,1},{65,33},{97,65},{2,98}... | collective-permute-start | bytes 1572872 | tf_op jit(solution)/shard_map/cond/branch_1_fun/ppermute | solution.py:324
  81.8 10.9 %copy-start.7 = (bf16[64,32,128]{2,1,0:T(8,128)(2,1)}, bf16[64,32,128]{2,1,0:T(8,128)(2,1)S(1)}, u32[]{:S(2)}) copy-start(bf16[64,32,128]{2,1,0:T(8,128)(2,1)S(1)} %collective-permute-done.12.refs_1_.refs_2_) | copy-start | bytes 1572868 | tf_op jit(solution)/shard_map/cond
  92.7 1.2 copy-start.2
  97.7 7.8 %copy-start.9 = (bf16[64,32,128]{2,1,0:T(8,128)(2,1)S(1)}, bf16[64,32,128]{2,1,0:T(8,128)(2,1)}, u32[]{:S(2)}) copy-start(bf16[64,32,128]{2,1,0:T(8,128)(2,1)} %get-tuple-element.54.refs_0_) | copy-start | bytes 1572868 | tf_op jit(solution)/shard_map/cond
  97.7 9.1 %copy-start.10 = (bf16[64,32,128]{2,1,0:T(8,128)(2,1)S(1)}, bf16[64,32,128]{2,1,0:T(8,128)(2,1)}, u32[]{:S(2)}) copy-start(bf16[64,32,128]{2,1,0:T(8,128)(2,1)} %get-tuple-element.55.refs_1_) | copy-start | bytes 1572868 | tf_op jit(solution)/shard_map/cond
  97.7 45.7 %all-to-all-start.3 = ((bf16[64,128,128]{2,1,0:T(8,128)(2,1)}), bf16[64,128,128]{2,1,0:T(8,128)(2,1)S(1)}, u32[]{:S(2)}, u32[]{:S(2)}) async-start(bf16[64,128,128]{2,1,0:T(8,128)(2,1)} %get-tuple-element.56), calls=%async_computation.3 | async-start | bytes 4194304 | tf_op jit(solution)/shard_map/cond/branch_1_fun/all_to_all | solution.py:316
  105.4 16.1 %collective-permute-start.20 = (bf16[64,32,128]{2,1,0:T(8,128)(2,1)S(1)}, bf16[64,32,128]{2,1,0:T(8,128)(2,1)}, u32[]{:S(2)}, u32[]{:S(2)}) collective-permute-start(bf16[64,32,128]{2,1,0:T(8,128)(2,1)S(1)} %copy-done.9), channel_id=1, source_target_pairs={{0,32},{32,64},{64,96},{96,0},{1,33},{33,65},{65,97},{97,1},{2,34}... | collective-permute-start | bytes 1572872 | tf_op jit(solution)/shard_map/cond/branch_1_fun/ppermute | solution.py:320
  106.8 14.9 %collective-permute-start.19 = (bf16[64,32,128]{2,1,0:T(8,128)(2,1)S(1)}, bf16[64,32,128]{2,1,0:T(8,128)(2,1)}, u32[]{:S(2)}, u32[]{:S(2)}) collective-permute-start(bf16[64,32,128]{2,1,0:T(8,128)(2,1)S(1)} %copy-done.10), channel_id=1, source_target_pairs={{0,96},{32,0},{64,32},{96,64},{1,97},{33,1},{65,33},{97,65},{2,98}... | collective-permute-start | bytes 1572872 | tf_op jit(solution)/shard_map/cond/branch_1_fun/ppermute | solution.py:324
  108.7 24.2 %collective-permute-start.18 = (bf16[64,32,128]{2,1,0:T(8,128)(2,1)S(1)}, bf16[64,32,128]{2,1,0:T(8,128)(2,1)}, u32[]{:S(2)}, u32[]{:S(2)}) collective-permute-start(bf16[64,32,128]{2,1,0:T(8,128)(2,1)S(1)} %copy-done.9), channel_id=1, source_target_pairs={{0,96},{32,0},{64,32},{96,64},{1,97},{33,1},{65,33},{97,65},{2,98}... | collective-permute-start | bytes 1572872 | tf_op jit(solution)/shard_map/cond/branch_1_fun/ppermute | solution.py:324
  110.6 22.3 %collective-permute-start.23 = (bf16[64,32,128]{2,1,0:T(8,128)(2,1)S(1)}, bf16[64,32,128]{2,1,0:T(8,128)(2,1)}, u32[]{:S(2)}, u32[]{:S(2)}) collective-permute-start(bf16[64,32,128]{2,1,0:T(8,128)(2,1)S(1)} %copy-done.10), channel_id=1, source_target_pairs={{0,32},{32,64},{64,96},{96,0},{1,33},{33,65},{65,97},{97,1},{2,34}... | collective-permute-start | bytes 1572872 | tf_op jit(solution)/shard_map/cond/branch_1_fun/ppermute | solution.py:320
  121.6 21.8 %collective-permute-start.21 = (bf16[64,32,128]{2,1,0:T(8,128)(2,1)}, bf16[64,32,128]{2,1,0:T(8,128)(2,1)}, u32[]{:S(2)}, u32[]{:S(2)}) collective-permute-start(bf16[64,32,128]{2,1,0:T(8,128)(2,1)} %collective-permute-done.20.refs_6_), channel_id=1, source_target_pairs={{0,32},{32,64},{64,96},{96,0},{1,33},{33,65},{65,97},{97,1},{2,34}... | collective-permute-start | bytes 1572872 | tf_op jit(solution)/shard_map/cond/branch_1_fun/ppermute | solution.py:320
  121.7 21.7 %collective-permute-start.22 = (bf16[64,32,128]{2,1,0:T(8,128)(2,1)}, bf16[64,32,128]{2,1,0:T(8,128)(2,1)}, u32[]{:S(2)}, u32[]{:S(2)}) collective-permute-start(bf16[64,32,128]{2,1,0:T(8,128)(2,1)} %collective-permute-done.19.refs_3_), channel_id=1, source_target_pairs={{0,96},{32,0},{64,32},{96,64},{1,97},{33,1},{65,33},{97,65},{2,98}... | collective-permute-start | bytes 1572872 | tf_op jit(solution)/shard_map/cond/branch_1_fun/ppermute | solution.py:324
  143.4 1.4 copy-start.1

commit v4 on v3

v4 whole, which is shorter than its diff:
```python
import functools

import jax
import jax.numpy as jnp
from jax import lax
from jax.experimental import pallas as pl
from jax.experimental.pallas import tpu as pltpu
from jax.sharding import PartitionSpec as P

EPSILON = 1e-06
WRITERS = 32
CAP = 8
GROUP = 8
GROUP_MOMENT = 16
ROWS = 32
TILE = 16
SLOTS = WRITERS * CAP
VMEM = 60 * 1024 * 1024

WHOLE = 2
BY_ROWS_MOMENT = CAP
BY_ROWS_WEIGHT = CAP - WHOLE
USUAL = (116, 96)
FULL = (WRITERS * BY_ROWS_MOMENT + 8, WRITERS * BY_ROWS_WEIGHT + 8)


def clear(ref, length, value):
    def one(i, carry):
        ref[i] = value
        return carry

    lax.fori_loop(0, length, one, 0, unroll=8)


def scale_of(values):
    top = jnp.max(jnp.max(jnp.abs(values), axis=0, keepdims=True), axis=1, keepdims=True)
    top = jnp.broadcast_to(top + EPSILON, (8, 128))
    return top.astype(jnp.bfloat16).astype(jnp.float32)


def row_quarter(replica):
    return pl.ds(pl.multiple_of(replica[0] * ROWS, ROWS), ROWS)


def payload_rows(by_rows):
    return by_rows * ROWS + TILE


def tile_rows(writer, by_rows):
    return pl.ds(pl.multiple_of(writer * payload_rows(by_rows) + by_rows * ROWS, TILE), TILE)


def slot_rows(writer, k, by_rows):
    return pl.ds(pl.multiple_of(writer * payload_rows(by_rows) + k * ROWS, TILE), ROWS)


def moment_kernel(replica, writer, weight_mask, moment_mask, moment, payload, held, sems, tiles, totals, count):
    rows = row_quarter(replica)
    lane = lax.broadcasted_iota(jnp.int32, (8, 128), 1)
    line = lax.broadcasted_iota(jnp.int32, (8, 128), 0)
    steps = held.shape[0] // GROUP_MOMENT

    def fetch(step):
        part = pl.ds(step * GROUP_MOMENT, GROUP_MOMENT)
        return pltpu.make_async_copy(moment.at[part], held.at[part], sems.at[step])

    for step in range(steps):
        fetch(step).start()
    clear(count, WRITERS, 0)
    tiles[...] = jnp.zeros(tiles.shape, tiles.dtype)
    totals[...] = jnp.zeros(totals.shape, totals.dtype)

    def one_step(step, carry):
        fetch(step).wait()
        total = totals[...]
        for i in range(GROUP_MOMENT):
            block = step * GROUP_MOMENT + i
            target = writer[block]
            rank = count[target]
            count[target] = rank + 1
            keep_w = weight_mask[block].astype(jnp.float32)
            keep_m = keep_w * moment_mask[block].astype(jnp.float32)
            total = total + jnp.where(lane == target, jnp.where(line == 3, keep_w, jnp.where(line == 4, keep_m, 0.0)), 0.0)
            scale = scale_of(held[block])
            kept = jnp.where(line == 0, scale, jnp.where(line == 1, keep_w, jnp.where(line == 2, keep_m, 0.0)))
            tiles[target] = jnp.where(lane == rank, kept, tiles[target])
            payload[slot_rows(target, rank, BY_ROWS_MOMENT), :] = (held[block, rows, :] * (keep_m / scale)[0:1, :]).astype(jnp.bfloat16)
        totals[...] = total
        return carry

    lax.fori_loop(0, steps, one_step, 0)
    common = totals[...]
    common = jnp.where(line == 3, jnp.maximum(common - WHOLE, 0.0), common)
    blank = jnp.zeros((TILE - 8, 128), jnp.float32)

    def one(w, carry):
        tile = jnp.concatenate([tiles[w] + common, blank], axis=0)
        payload[tile_rows(w, BY_ROWS_MOMENT), :] = tile.astype(jnp.bfloat16)
        return carry

    lax.fori_loop(0, WRITERS, one, 0, unroll=4)


def weight_kernel(blocks, replica, writer, weight_mask, base_scale, weight, codes, payload, whole, refreshed, coded, scales, slot_of, kept_of, count, count_kept):
    step = pl.program_id(0)

    @pl.when(step == 0)
    def _():
        clear(slot_of, SLOTS, blocks)
        clear(kept_of, SLOTS, blocks)
        clear(count, WRITERS, 0)
        clear(count_kept, WRITERS, 0)
        coded[blocks] = jnp.zeros(coded.shape[1:], coded.dtype)
        scales[pl.ds(blocks, 8), :] = jnp.zeros((8, 128), jnp.float32)

    for i in range(GROUP):
        block = step * GROUP + i
        target = writer[block]
        rank = count[target]
        count[target] = rank + 1
        slot_of[target * CAP + rank] = block
        rank_kept = count_kept[target]
        count_kept[target] = rank_kept + weight_mask[block]
        kept_of[target * CAP + rank_kept] = block
        keep = weight_mask[block].astype(jnp.float32)
        base = codes[i].astype(jnp.float32) * base_scale[block]
        values = weight[i] - base
        scale = scale_of(values)
        scales[pl.ds(block, 1), :] = scale[0:1, :]
        rounded = (values * (keep / scale)[0:1, :]).astype(jnp.bfloat16)
        coded[block] = rounded
        refreshed[i] = (base + rounded.astype(jnp.float32) * scale[0:1, :]).astype(jnp.bfloat16)

    @pl.when(step == blocks // GROUP - 1)
    def _():
        rows = row_quarter(replica)
        lane = lax.broadcasted_iota(jnp.int32, (TILE, 128), 1)

        def one(w, carry):
            tile = jnp.zeros((TILE, 128), jnp.float32)
            for k in range(CAP):
                block = kept_of[w * CAP + k]
                if k < WHOLE:
                    whole[w * WHOLE + k] = coded[block]
                else:
                    payload[slot_rows(w, k - WHOLE, BY_ROWS_WEIGHT), :] = coded[block, rows, :]
                scale = scales[pl.ds(slot_of[w * CAP + k], 1), :]
                tile = jnp.where(lane == k, jnp.broadcast_to(scale, (TILE, 128)), tile)
            payload[tile_rows(w, BY_ROWS_WEIGHT), :] = tile.astype(jnp.bfloat16)
            return carry

        lax.fori_loop(0, WRITERS, one, 0)


def cost(flops, moved):
    return pl.CostEstimate(flops=flops, bytes_accessed=moved, transcendentals=0)


def params():
    return pltpu.CompilerParams(dimension_semantics=("arbitrary",), vmem_limit_bytes=VMEM)


def moment_call(replica, writer, weight_mask, moment_mask, moment):
    blocks, width = moment.shape[0], moment.shape[1]
    shape = (WRITERS * payload_rows(BY_ROWS_MOMENT), width)
    return pl.pallas_call(
        moment_kernel,
        grid_spec=pltpu.PrefetchScalarGridSpec(
            num_scalar_prefetch=4,
            grid=(1,),
            in_specs=[pl.BlockSpec(memory_space=pl.ANY)],
            out_specs=pl.BlockSpec(shape, lambda i, *_: (0, 0)),
            scratch_shapes=[
                pltpu.VMEM(moment.shape, jnp.float32),
                pltpu.SemaphoreType.DMA((blocks // GROUP_MOMENT,)),
                pltpu.VMEM((WRITERS, 8, 128), jnp.float32),
                pltpu.VMEM((8, 128), jnp.float32),
                pltpu.SMEM((WRITERS,), jnp.int32),
            ],
        ),
        out_shape=jax.ShapeDtypeStruct(shape, jnp.bfloat16),
        compiler_params=params(),
        cost_estimate=cost(10 << 20, 12 << 20),
    )(replica, writer, weight_mask, moment_mask, moment)


def weight_call(replica, writer, weight_mask, base_scale, weight, codes):
    blocks, width = weight.shape[0], weight.shape[1]
    moving = pl.BlockSpec((GROUP, width, width), lambda i, *_: (i, 0, 0))
    payload = (WRITERS * payload_rows(BY_ROWS_WEIGHT), width)
    whole = (WRITERS * WHOLE, width, width)
    return pl.pallas_call(
        functools.partial(weight_kernel, blocks),
        grid_spec=pltpu.PrefetchScalarGridSpec(
            num_scalar_prefetch=4,
            grid=(blocks // GROUP,),
            in_specs=[moving, moving],
            out_specs=[pl.BlockSpec(payload, lambda i, *_: (0, 0)), pl.BlockSpec(whole, lambda i, *_: (0, 0, 0)), moving],
            scratch_shapes=[
                pltpu.VMEM((blocks + 1, width, width), jnp.bfloat16),
                pltpu.VMEM((blocks + 8, 128), jnp.float32),
                pltpu.SMEM((SLOTS,), jnp.int32),
                pltpu.SMEM((SLOTS,), jnp.int32),
                pltpu.SMEM((WRITERS,), jnp.int32),
                pltpu.SMEM((WRITERS,), jnp.int32),
            ],
        ),
        out_shape=[
            jax.ShapeDtypeStruct(payload, jnp.bfloat16),
            jax.ShapeDtypeStruct(whole, jnp.bfloat16),
            jax.ShapeDtypeStruct((blocks, width, width), jnp.bfloat16),
        ],
        compiler_params=params(),
        cost_estimate=cost(20 << 20, 28 << 20),
    )(replica, writer, weight_mask, base_scale, weight, codes)


HBM = pl.BlockSpec(memory_space=pltpu.HBM)
SOURCES = 8


def spread_lines(payload, by_rows, tiles, staged, spread, sems):
    copy = pltpu.make_async_copy(payload.at[:, pl.ds(by_rows * ROWS, TILE), :], tiles, sems.at[0])
    copy.start()
    copy.wait()
    line = lax.broadcasted_iota(jnp.int32, tiles.shape, 1)
    values = tiles[...].astype(jnp.float32)
    lines = [jnp.sum(jnp.where(line == i, values, 0.0), axis=1) for i in range(5)]
    for i in range(2):
        staged[i] = lines[1 + i].astype(jnp.int32)
    copy = pltpu.make_async_copy(staged, spread, sems.at[1])
    copy.start()
    copy.wait()
    return lines


def pack(by_rows, payload, held, packed, sems, advance):
    last = packed.shape[0] - 1
    steps = WRITERS // SOURCES

    def fetch(step):
        part = pl.ds(step * SOURCES, SOURCES)
        return pltpu.make_async_copy(payload.at[part], held.at[part], sems.at[step])

    for step in range(steps):
        fetch(step).start()
    yield

    def one(s, place):
        moves = advance(s)
        for k in range(by_rows):
            packed[jnp.minimum(place, last)] = held[s, pl.ds(k * ROWS, ROWS), :]
            place = place + moves[k]
        return place

    place = 0
    for step in range(steps):
        fetch(step).wait()
        place = lax.fori_loop(step * SOURCES, (step + 1) * SOURCES, one, place)
    yield


def pack_moment_kernel(half, ticket, payload, first, second, kept_w, kept_m, totals, scales, held, packed, tiles, staged, spread, sems, tile_sems):
    steps = pack(BY_ROWS_MOMENT, payload, held, packed, sems, lambda s: [spread[1, s, k] for k in range(CAP)])
    next(steps)
    lines = spread_lines(payload, BY_ROWS_MOMENT, tiles, staged, spread, tile_sems)
    next(steps)
    first[...] = packed[0:half]
    second[...] = packed[half : 2 * half]
    scales[...] = lines[0]
    kept_w[...] = lines[1].astype(jnp.int32)
    kept_m[...] = lines[2].astype(jnp.int32)
    row = lax.broadcasted_iota(jnp.int32, (8, 128), 0)
    total_w, total_m = (jnp.sum(lines[i], axis=0, keepdims=True) for i in (3, 4))
    totals[...] = jnp.where(row == 0, total_w, jnp.where(row == 1, total_m, 0.0))


def pack_moment(capacity, ticket, payload):
    width = payload.shape[-1]
    half = capacity // 2
    part = jax.ShapeDtypeStruct((half, ROWS, width), jnp.bfloat16)
    flags = jax.ShapeDtypeStruct((WRITERS, width), jnp.int32)
    return pl.pallas_call(
        functools.partial(pack_moment_kernel, half),
        in_specs=[pl.BlockSpec(memory_space=pltpu.SMEM), HBM],
        out_shape=[
            part,
            part,
            flags,
            flags,
            jax.ShapeDtypeStruct((8, width), jnp.float32),
            jax.ShapeDtypeStruct((WRITERS, width), jnp.float32),
        ],
        scratch_shapes=[
            pltpu.VMEM((WRITERS, payload_rows(BY_ROWS_MOMENT), width), jnp.bfloat16),
            pltpu.VMEM((capacity, ROWS, width), jnp.bfloat16),
            pltpu.VMEM((WRITERS, TILE, width), jnp.bfloat16),
            pltpu.VMEM((2, WRITERS, width), jnp.int32),
            pltpu.SMEM((2, WRITERS, width), jnp.int32),
            pltpu.SemaphoreType.DMA((WRITERS // SOURCES,)),
            pltpu.SemaphoreType.DMA((2,)),
        ],
        compiler_params=pltpu.CompilerParams(vmem_limit_bytes=VMEM),
        cost_estimate=cost(0, 0),
    )(ticket, payload.reshape(WRITERS, -1, width))


def pack_weight_kernel(half, kept, payload, *refs):
    first, second, scales, held, packed, sems = refs[-6:]

    def advance(s):
        found = functools.reduce(jnp.add, [kept[s, k] for k in range(CAP)])
        return [jnp.where(found > WHOLE + k, 1, 0) for k in range(BY_ROWS_WEIGHT)]

    steps = pack(BY_ROWS_WEIGHT, payload, held, packed, sems, advance)
    next(steps)
    next(steps)
    first[...] = packed[0:half]
    second[...] = packed[half : 2 * half]
    scales[...] = held[:, pl.ds(BY_ROWS_WEIGHT * ROWS, TILE), :].astype(jnp.float32)[:, 0, :]


def pack_weight(capacity, kept, payload, earlier):
    width = payload.shape[-1]
    half = capacity // 2
    part = jax.ShapeDtypeStruct((half, ROWS, width), jnp.bfloat16)
    return pl.pallas_call(
        functools.partial(pack_weight_kernel, half),
        grid_spec=pltpu.PrefetchScalarGridSpec(
            num_scalar_prefetch=1,
            grid=(1,),
            in_specs=[HBM] * (1 + len(earlier)),
            out_specs=[pl.BlockSpec(part.shape, lambda i, *_: (0, 0, 0))] * 2 + [pl.BlockSpec((WRITERS, width), lambda i, *_: (0, 0))],
            scratch_shapes=[
                pltpu.VMEM((WRITERS, payload_rows(BY_ROWS_WEIGHT), width), jnp.bfloat16),
                pltpu.VMEM((capacity, ROWS, width), jnp.bfloat16),
                pltpu.SemaphoreType.DMA((WRITERS // SOURCES,)),
            ],
        ),
        out_shape=[part, part, jax.ShapeDtypeStruct((WRITERS, width), jnp.float32)],
        compiler_params=params(),
        cost_estimate=cost(0, 0),
    )(kept, payload.reshape(WRITERS, -1, width), *earlier)


def after_kernel(*refs):
    pass


def after(values, earlier):
    return pl.pallas_call(
        after_kernel,
        in_specs=[HBM] * (1 + len(earlier)),
        out_specs=HBM,
        out_shape=jax.ShapeDtypeStruct(values.shape, values.dtype),
        input_output_aliases={0: 0},
        compiler_params=pltpu.CompilerParams(vmem_limit_bytes=VMEM),
    )(values, *earlier)


ALL_TURNS, NEAR_TURNS, FAR_TURN = (0, 1, 2, 3), (0, 1, 3), (2,)


def unpack_kernel(by_rows, half, turns, replica, kept, *refs):
    n_whole = CAP - by_rows
    n_parts = 2 * len(turns)
    parts, refs = refs[:n_parts], refs[n_parts:]
    whole = refs[0] if n_whole else None
    out, held, built, sems, out_sems = refs[-5:]
    nothing, first_whole = 2 * half, 2 * half + 1
    rows = [pl.ds(pl.multiple_of(lax.rem(replica[0] + turn, 4) * ROWS, ROWS), ROWS) for turn in turns]
    copies = [pltpu.make_async_copy(part, held.at[i // 2, pl.ds((i % 2) * half, half)], sems.at[i]) for i, part in enumerate(parts)]
    if n_whole:
        for i in range(len(turns)):
            here = held.at[i, pl.ds(first_whole, WRITERS * n_whole)]
            copies.append(pltpu.make_async_copy(whole.at[:, rows[i], :], here, sems.at[n_parts + i]))
    for copy in copies:
        copy.start()
    for i in range(len(turns)):
        held[i, nothing] = jnp.zeros(held.shape[2:], held.dtype)
    for copy in copies:
        copy.wait()

    def send(step):
        part = pl.ds(step * SOURCES * CAP, SOURCES * CAP)
        there = out.at[part, rows[0], :] if len(turns) == 1 else out.at[part]
        return pltpu.make_async_copy(built.at[part], there, out_sems.at[step])

    def one(step, place):
        for s in range(SOURCES):
            source = step * SOURCES + s
            rank = 0
            for k in range(CAP):
                flag = kept[source, k]
                if n_whole:
                    as_whole = rank < n_whole
                    origin = jnp.where(as_whole, first_whole + source * n_whole + rank, jnp.minimum(place, nothing - 1))
                    place = place + jnp.where(as_whole, 0, flag)
                    rank = rank + flag
                else:
                    origin = jnp.minimum(place, nothing - 1)
                    place = place + flag
                origin = jnp.where(flag > 0, origin, nothing)
                for i in range(len(turns)):
                    if len(turns) == 1:
                        built[source * CAP + k] = held[i, origin]
                    else:
                        built[source * CAP + k, rows[i], :] = held[i, origin]
        send(step).start()
        return place

    steps = WRITERS // SOURCES
    lax.fori_loop(0, steps, one, 0)
    for step in range(steps):
        send(step).wait()


def unpack_call(by_rows, capacity, turns, replica, kept, parts, whole=None, out=None):
    width = parts[0].shape[-1]
    n_whole = WRITERS * (CAP - by_rows)
    parts = [part for turn in turns for part in parts[2 * turn : 2 * turn + 2]]
    operands = [*parts] + ([] if whole is None else [whole]) + ([] if out is None else [out])
    return pl.pallas_call(
        functools.partial(unpack_kernel, by_rows, capacity // 2, turns),
        grid_spec=pltpu.PrefetchScalarGridSpec(
            num_scalar_prefetch=2,
            grid=(1,),
            in_specs=[HBM] * len(operands),
            out_specs=HBM,
            scratch_shapes=[
                pltpu.VMEM((len(turns), capacity + 1 + n_whole, ROWS, width), jnp.bfloat16),
                pltpu.VMEM((SLOTS, ROWS if len(turns) == 1 else width, width), jnp.bfloat16),
                pltpu.SemaphoreType.DMA((3 * len(turns),)),
                pltpu.SemaphoreType.DMA((WRITERS // SOURCES,)),
            ],
        ),
        out_shape=jax.ShapeDtypeStruct((SLOTS, width, width), jnp.bfloat16),
        input_output_aliases={} if out is None else {1 + len(operands): 0},
        compiler_params=params(),
        cost_estimate=cost(0, 0),
    )(replica, kept, *operands)


def regroup(values):
    return lax.all_to_all(values, "fsdp", split_axis=0, concat_axis=0, tiled=True)


def upward(values):
    return lax.ppermute(values, "replica", [(i, (i + 1) % 4) for i in range(4)])


def downward(values):
    return lax.ppermute(values, "replica", [(i, (i - 1) % 4) for i in range(4)])


def first_round(first, second):
    first_up, second_down = upward(first), downward(second)
    return first_up, downward(first), upward(second), second_down


def second_round(first_up, second_down):
    return upward(first_up), downward(second_down)


def by_turn(first, second, near, far):
    return (first, second, near[1], near[3], *far, near[0], near[2])


def rest(capacities, replica, m_read, m_near, m_far, w_read, w_near, w_far, w_whole):
    written_moment = unpack_call(BY_ROWS_MOMENT, capacities[0], ALL_TURNS, replica, m_read[3], by_turn(*m_read[:2], m_near, m_far))
    if w_far is None:
        w_near = (after(w_near[0], (written_moment,)), *w_near[1:3], after(w_near[3], (written_moment,)))
        w_far = second_round(w_near[0], w_near[3])
    written_weight = unpack_call(
        BY_ROWS_WEIGHT, capacities[1], ALL_TURNS, replica, m_read[2], by_turn(*w_read[:2], w_near, w_far), w_whole
    )
    return written_weight, written_moment


def exchange_again(ticket, replica, m_payload, w_payload, w_whole):
    m_read = pack_moment(FULL[0], ticket, m_payload)
    m_near = first_round(*m_read[:2])
    m_far = second_round(m_near[0], m_near[3])
    w_read = pack_weight(FULL[1], m_read[2], w_payload, ())
    w_near = first_round(*w_read[:2])
    w_far = second_round(w_near[0], w_near[3])
    return rest(FULL, replica, m_read, m_near, m_far, w_read, w_near, w_far, w_whole)


def on_device(weight, moment, base_codes, base_scale, weight_mask, moment_mask, writer):
    width = weight.shape[1]
    target = writer[:, 0]
    replica = lax.axis_index("replica").astype(jnp.int32).reshape(1)
    m_payload = regroup(moment_call(replica, target, weight_mask, moment_mask, moment))
    w_payload, w_whole, refreshed = weight_call(replica, target, weight_mask, base_scale, weight, base_codes)
    w_payload = regroup(after(w_payload, (m_payload,)))
    m_read = pack_moment(USUAL[0], replica, m_payload)
    m_near = first_round(*m_read[:2])
    m_far = second_round(m_near[0], m_near[3])
    w_read = pack_weight(USUAL[1], m_read[2], w_payload, m_near)
    w_whole = regroup(after(w_whole, (*w_read[:2], *m_far)))
    w_near = first_round(*w_read[:2])
    written_weight, written_moment = rest(USUAL, replica, m_read, m_near, m_far, w_read, w_near, None, w_whole)

    over = jnp.any(m_read[4][:2, :WRITERS] >= jnp.array([[USUAL[1]], [USUAL[0]]], jnp.float32)).astype(jnp.int32)
    _, written_weight, written_moment = lax.while_loop(
        lambda carry: carry[0] < over,
        lambda carry: (carry[0] + 1, *exchange_again(carry[0].reshape(1), replica, m_payload, w_payload, w_whole)),
        (jnp.int32(0), written_weight, written_moment),
    )
    written_scales = jnp.stack([w_read[2][:, :CAP], m_read[5][:, :CAP]], axis=0).astype(jnp.bfloat16)
    shape = (WRITERS, CAP, width, width)
    return written_weight.reshape(shape), written_moment.reshape(shape), written_scales, refreshed


def solution(mesh):
    placed = (
        P("fsdp", None, None),
        P("fsdp", None, None),
        P("fsdp", None, None),
        P("fsdp"),
        P("fsdp"),
        P("fsdp"),
        P("fsdp", None),
    )
    return jax.shard_map(
        on_device,
        mesh=mesh,
        in_specs=placed,
        out_specs=(
            P("fsdp", None, None, None),
            P("fsdp", None, None, None),
            P(None, "fsdp", None),
            P("fsdp", None, None),
        ),
        check_vma=False,
    )
```

time: 154 us -> 137 us (0.89)
  waiting for transfers between devices: 61.3 us -> 45.3 us
  local copies, waits for them, and re-layouts: 5.49 us -> 2.61 us
    ppermute x6, waiting for transfers between devices: 43 us -> 26.3 us  [upward(): return lax.ppermute(values, 'replica', [(i, (i + 1) % 4) for i in range(4)])]
    cond x15 -> x0, local copies, waits for them, and re-layouts: 2.64 us -> none
    unnamed x1 -> x20, local copies, waits for them, and re-layouts: 0.08 us -> 2.45 us
    pallas_call x4 -> x8, Pallas kernels: 19.7 us -> 20.5 us  [the longest x2 13.6 us: unpack_call(): pl.pallas_call(functools.partial(unpack_kernel, by_rows, capacity // 2, t...]
  transfers between devices with their start and end apart: 15 -> 15, of which waited for: 8 -> 8; matrix products, arithmetic and copies ran while one was open for 1% -> 2% of each run, Pallas kernels for 15% -> 23%
where the time goes in v4:
time: 137 us; the launch traced here: 136 us
  waiting for transfers between devices  45.3 us (33%)
  Pallas kernels  43.5 us (32%)
  starting transfers between devices  41.1 us (30%)
  local copies, waits for them, and re-layouts  2.61 us (2%)
  other arithmetic  2 us (1%)
  between operations  1.58 us (1%)
    ppermute x6, waiting for transfers between devices, upward(): return lax.ppermute(values, 'replica', [(i, (i + 1) % 4) for i in range(4)])  26.3 us
    all_to_all x3, starting transfers between devices, regroup(): lax.all_to_all(values, 'fsdp', split_axis=0, concat_axis=0, tiled=True)  22.9 us
    pallas_call x1, Pallas kernels, weight_call(): pl.pallas_call(functools.partial(weight_kernel, blocks), grid_spec=pltpu....  17.2 us
    ppermute x6, starting transfers between devices, downward(): return lax.ppermute(values, 'replica', [(i, (i - 1) % 4) for i in range(4)])  14.6 us
    pallas_call x2, Pallas kernels, unpack_call(): pl.pallas_call(functools.partial(unpack_kernel, by_rows, capacity // 2, t...  13.6 us
    all_to_all x3, waiting for transfers between devices, regroup(): lax.all_to_all(values, 'fsdp', split_axis=0, concat_axis=0, tiled=True)  10.1 us
    ppermute x6, waiting for transfers between devices, downward(): return lax.ppermute(values, 'replica', [(i, (i - 1) % 4) for i in range(4)])  8.85 us
    pallas_call x1, Pallas kernels, moment_call(): pl.pallas_call(moment_kernel, grid_spec=pltpu.PrefetchScalarGridSpec(num_...  5.76 us
  transfers between devices with their start and end apart: 15, of which 8 were waited for; matrix products, arithmetic and copies ran while one was open for 2% of the time, Pallas kernels for 23%

profile of v4, /device:TPU:2, one launch (start us, length us, event | category | flops | bytes accessed | tf_op | source)
XLA Modules:
  0.0 136.2 jit_solution(7246339033084458911)
XLA Ops:
  0.6 5.8 %shard_map.111 = bf16[8704,128]{1,0:T(8,128)(2,1)} custom-call(s32[1]{0:T(128)} %bitcast.3.replica.ticket, s32[128]{0:T(128)} %bitcast.28, s32[128]{0:T(128)} %weight_mask.3, s32[128]{0:T(128)} %moment_mask.1, f32[128,128,128]{2,1,0:T(8,128)} %moment.1), custom_call_target="tpu_custom_call" | custom-call | flops 10485760 | bytes 12582912 | tf_op jit(solution)/shard_map/pallas_call | solution.py:166
  6.4 7.6 %all-to-all-start = ((bf16[32,272,128]{2,1,0:T(8,128)(2,1)}), bf16[32,272,128]{2,1,0:T(8,128)(2,1)S(1)}, u32[]{:S(2)}, u32[]{:S(2)}) async-start(bf16[32,272,128]{2,1,0:T(8,128)(2,1)} %bitcast.25), calls=%async_computation | async-start | bytes 4456448 | tf_op jit(solution)/shard_map/all_to_all | solution.py:445
  14.0 17.2 %shard_map.113 = (bf16[6656,128]{1,0:T(8,128)(2,1)}, bf16[64,128,128]{2,1,0:T(8,128)(2,1)}, bf16[128,128,128]{2,1,0:T(8,128)(2,1)}) custom-call(s32[1]{0:T(128)} %bitcast.3.replica.ticket, s32[128]{0:T(128)} %bitcast.29, s32[128]{0:T(128)} %weight_mask.3, f32[128]{0:T(128)} %base_scale.1, f32[128,128,128]{2,1,0:T(8,128)} %weight.1, s32[128,128,128]{2,1,0:T(8,128)} %codes.1), custom_call_target="tpu_custom_call" | custom-call | flops 20971520 | bytes 29360128 | tf_op jit(solution)/shard_map/pallas_call | solution.py:192
  31.3 10.1 %all-to-all-done.payload = bf16[32,272,128]{2,1,0:T(8,128)(2,1)S(1)} async-done(((bf16[32,272,128]{2,1,0:T(8,128)(2,1)}), bf16[32,272,128]{2,1,0:T(8,128)(2,1)S(1)}, u32[]{:S(2)}, u32[]{:S(2)}) %all-to-all-start) | async-done | bytes 2228256 | tf_op jit(solution)/shard_map/all_to_all | solution.py:445
  41.4 7.6 %all-to-all-start.1 = ((bf16[32,208,128]{2,1,0:T(8,128)(2,1)}), bf16[32,208,128]{2,1,0:T(8,128)(2,1)}, u32[]{:S(2)}, u32[]{:S(2)}) async-start(bf16[32,208,128]{2,1,0:T(8,128)(2,1)} %bitcast.27), calls=%async_computation.1 | async-start | bytes 3407872 | tf_op jit(solution)/shard_map/all_to_all | solution.py:445
  49.0 3.3 %shard_map.112 = (bf16[58,32,128]{2,1,0:T(8,128)(2,1)}, bf16[58,32,128]{2,1,0:T(8,128)(2,1)}, s32[32,128]{1,0:T(8,128)}, s32[32,128]{1,0:T(8,128)}, f32[8,128]{1,0:T(8,128)}, /*index=5*/f32[32,128]{1,0:T(8,128)}) custom-call(s32[1]{0:T(128)} %bitcast.3.replica.ticket, bf16[32,272,128]{2,1,0:T(8,128)(2,1)S(1)} %all-to-all-done.payload), custom_call_target="tpu_custom_call" | custom-call | tf_op jit(solution)/shard_map/pallas_call | solution.py:283
  52.3 2.0 %collective-permute-start.12 = (bf16[58,32,128]{2,1,0:T(8,128)(2,1)}, bf16[58,32,128]{2,1,0:T(8,128)(2,1)S(1)}, u32[]{:S(2)}, u32[]{:S(2)}) collective-permute-start(bf16[58,32,128]{2,1,0:T(8,128)(2,1)} %get-tuple-element.66.refs_0_), channel_id=1, source_target_pairs={{0,32},{32,64},{64,96},{96,0},{1,33},{33,65},{65,97},{97,1},{2,34}... | collective-permute-start | bytes 1425416 | tf_op jit(solution)/shard_map/ppermute | solution.py:449
  54.3 2.2 %collective-permute-start.15 = (bf16[58,32,128]{2,1,0:T(8,128)(2,1)}, bf16[58,32,128]{2,1,0:T(8,128)(2,1)S(1)}, u32[]{:S(2)}, u32[]{:S(2)}) collective-permute-start(bf16[58,32,128]{2,1,0:T(8,128)(2,1)} %get-tuple-element.67.refs_1_), channel_id=1, source_target_pairs={{0,96},{32,0},{64,32},{96,64},{1,97},{33,1},{65,33},{97,65},{2,98}... | collective-permute-start | bytes 1425416 | tf_op jit(solution)/shard_map/ppermute | solution.py:453
  56.5 1.9 %collective-permute-start.13 = (bf16[58,32,128]{2,1,0:T(8,128)(2,1)}, bf16[58,32,128]{2,1,0:T(8,128)(2,1)}, u32[]{:S(2)}, u32[]{:S(2)}) collective-permute-start(bf16[58,32,128]{2,1,0:T(8,128)(2,1)} %get-tuple-element.66.refs_0_), channel_id=1, source_target_pairs={{0,96},{32,0},{64,32},{96,64},{1,97},{33,1},{65,33},{97,65},{2,98}... | collective-permute-start | bytes 1425416 | tf_op jit(solution)/shard_map/ppermute | solution.py:453
  58.5 9.8 %collective-permute-done.12.refs_0_.refs_6_ = bf16[58,32,128]{2,1,0:T(8,128)(2,1)S(1)} collective-permute-done((bf16[58,32,128]{2,1,0:T(8,128)(2,1)}, bf16[58,32,128]{2,1,0:T(8,128)(2,1)S(1)}, u32[]{:S(2)}, u32[]{:S(2)}) %collective-permute-start.12) | collective-permute-done | bytes 475168 | tf_op jit(solution)/shard_map/ppermute | solution.py:449
  68.3 3.3 %collective-permute-start.19 = (bf16[58,32,128]{2,1,0:T(8,128)(2,1)S(1)}, bf16[58,32,128]{2,1,0:T(8,128)(2,1)}, u32[]{:S(2)}, u32[]{:S(2)}) collective-permute-start(bf16[58,32,128]{2,1,0:T(8,128)(2,1)S(1)} %collective-permute-done.15.refs_3_), channel_id=1, source_target_pairs={{0,96},{32,0},{64,32},{96,64},{1,97},{33,1},{65,33},{97,65},{2,98}... | collective-permute-start | bytes 1425416 | tf_op jit(solution)/shard_map/ppermute | solution.py:453
  71.6 6.9 %collective-permute-done.13.refs_1_.refs_2_ = bf16[58,32,128]{2,1,0:T(8,128)(2,1)} collective-permute-done((bf16[58,32,128]{2,1,0:T(8,128)(2,1)}, bf16[58,32,128]{2,1,0:T(8,128)(2,1)}, u32[]{:S(2)}, u32[]{:S(2)}) %collective-permute-start.13) | collective-permute-done | bytes 475168 | tf_op jit(solution)/shard_map/ppermute | solution.py:453
  78.6 3.6 %shard_map.115 = (bf16[48,32,128]{2,1,0:T(8,128)(2,1)}, bf16[48,32,128]{2,1,0:T(8,128)(2,1)}, f32[32,128]{1,0:T(8,128)}) custom-call(s32[32,128]{1,0:T(8,128)} %get-tuple-element.64.kept, bf16[32,208,128]{2,1,0:T(8,128)(2,1)} %all-to-all-done.1.payload, bf16[58,32,128]{2,1,0:T(8,128)(2,1)} %copy-done.5, ...), custom_call_target="tpu_custom_call" | custom-call | tf_op jit(solution)/shard_map/pallas_call | solution.py:327
  82.2 6.1 %collective-permute-done.18.refs_4_.refs_3_ = bf16[58,32,128]{2,1,0:T(8,128)(2,1)} collective-permute-done((bf16[58,32,128]{2,1,0:T(8,128)(2,1)S(1)}, bf16[58,32,128]{2,1,0:T(8,128)(2,1)}, u32[]{:S(2)}, u32[]{:S(2)}) %collective-permute-start.18) | collective-permute-done | bytes 475168 | tf_op jit(solution)/shard_map/ppermute | solution.py:449
  88.3 7.6 %all-to-all-start.2 = ((bf16[64,128,128]{2,1,0:T(8,128)(2,1)}), bf16[64,128,128]{2,1,0:T(8,128)(2,1)}, u32[]{:S(2)}, u32[]{:S(2)}) async-start(bf16[64,128,128]{2,1,0:T(8,128)(2,1)} %shard_map.119), calls=%async_computation.2 | async-start | bytes 4194304 | tf_op jit(solution)/shard_map/all_to_all | solution.py:445
  96.0 1.3 collective-permute-start.20
  97.3 2.0 %collective-permute-start.17 = (bf16[48,32,128]{2,1,0:T(8,128)(2,1)}, bf16[48,32,128]{2,1,0:T(8,128)(2,1)S(1)}, u32[]{:S(2)}, u32[]{:S(2)}) collective-permute-start(bf16[48,32,128]{2,1,0:T(8,128)(2,1)} %get-tuple-element.69.refs_2_.refs_1_), channel_id=1, source_target_pairs={{0,96},{32,0},{64,32},{96,64},{1,97},{33,1},{65,33},{97,65},{2,98}... | collective-permute-start | bytes 1179656 | tf_op jit(solution)/shard_map/ppermute | solution.py:453
  99.3 6.6 %shard_map.116.refs_1_ = bf16[256,128,128]{2,1,0:T(8,128)(2,1)} custom-call(s32[1]{0:T(128)} %bitcast.3.replica.ticket, s32[32,128]{1,0:T(8,128)} %get-tuple-element.70.kept, bf16[58,32,128]{2,1,0:T(8,128)(2,1)} %get-tuple-element.66.refs_0_, bf16[58,32,128]{2,1,0:T(8,128)(2,1)} %get-tuple-element.67.refs_1_, ...), custom_call_target="tpu_custom_call" | custom-call | tf_op jit(solution)/shard_map/pallas_call | solution.py:423
  105.8 1.9 %collective-permute-start.16 = (bf16[48,32,128]{2,1,0:T(8,128)(2,1)S(1)}, bf16[48,32,128]{2,1,0:T(8,128)(2,1)}, u32[]{:S(2)}, u32[]{:S(2)}) collective-permute-start(bf16[48,32,128]{2,1,0:T(8,128)(2,1)S(1)} %copy-done.9), channel_id=1, source_target_pairs={{0,96},{32,0},{64,32},{96,64},{1,97},{33,1},{65,33},{97,65},{2,98}... | collective-permute-start | bytes 1179656 | tf_op jit(solution)/shard_map/ppermute | solution.py:453
  107.7 0.2 collective-permute-start.23
  107.9 0.5 collective-permute-done.20.refs_0_
  108.5 0.8 copy-done.8
  109.3 0.8 copy-done.7
  110.0 3.2 %collective-permute-start.22 = (bf16[48,32,128]{2,1,0:T(8,128)(2,1)}, bf16[48,32,128]{2,1,0:T(8,128)(2,1)S(1)}, u32[]{:S(2)}, u32[]{:S(2)}) collective-permute-start(bf16[48,32,128]{2,1,0:T(8,128)(2,1)} %shard_map.117.refs_3_), channel_id=1, source_target_pairs={{0,96},{32,0},{64,32},{96,64},{1,97},{33,1},{65,33},{97,65},{2,98}... | collective-permute-start | bytes 1179656 | tf_op jit(solution)/shard_map/ppermute | solution.py:453
  113.3 1.4 %compare_reduce_fusion = pred[]{:T(512)} fusion(f32[8,128]{1,0:T(8,128)} %get-tuple-element.72, f32[2]{0:T(128)S(1)} %copy-done.14), kind=kLoop, calls=%fused_computation.5 | loop fusion | flops 127 | bytes 265 | tf_op jit(solution)/shard_map/reduce_or | solution.py:505
  115.5 0.6 pad_maximum_fusion
  116.1 1.9 %collective-permute-done.16.refs_2_ = bf16[48,32,128]{2,1,0:T(8,128)(2,1)} collective-permute-done((bf16[48,32,128]{2,1,0:T(8,128)(2,1)S(1)}, bf16[48,32,128]{2,1,0:T(8,128)(2,1)}, u32[]{:S(2)}, u32[]{:S(2)}) %collective-permute-start.16) | collective-permute-done | bytes 393248 | tf_op jit(solution)/shard_map/ppermute | solution.py:453
  118.0 3.3 %collective-permute-done.23.refs_7_ = bf16[48,32,128]{2,1,0:T(8,128)(2,1)} collective-permute-done((bf16[48,32,128]{2,1,0:T(8,128)(2,1)}, bf16[48,32,128]{2,1,0:T(8,128)(2,1)}, u32[]{:S(2)}, u32[]{:S(2)}) %collective-permute-start.23) | collective-permute-done | bytes 393248 | tf_op jit(solution)/shard_map/ppermute | solution.py:449
  121.3 6.6 %collective-permute-done.21.refs_4_ = bf16[48,32,128]{2,1,0:T(8,128)(2,1)S(1)} collective-permute-done((bf16[48,32,128]{2,1,0:T(8,128)(2,1)}, bf16[48,32,128]{2,1,0:T(8,128)(2,1)S(1)}, u32[]{:S(2)}, u32[]{:S(2)}) %collective-permute-start.21) | collective-permute-done | bytes 393248 | tf_op jit(solution)/shard_map/ppermute | solution.py:449
  127.9 0.8 copy-done.10
  128.8 7.0 %shard_map.120 = bf16[256,128,128]{2,1,0:T(8,128)(2,1)} custom-call(s32[1]{0:T(128)} %bitcast.3.replica.ticket, s32[32,128]{1,0:T(8,128)} %get-tuple-element.64.kept, bf16[48,32,128]{2,1,0:T(8,128)(2,1)} %get-tuple-element.68.refs_1_.refs_0_, bf16[48,32,128]{2,1,0:T(8,128)(2,1)} %get-tuple-element.69.refs_2_.refs_1_, ...), custom_call_target="tpu_custom_call" | custom-call | tf_op jit(solution)/shard_map/pallas_call | solution.py:423
  135.8 0.2 while.12
  (35 shorter events, 0.5 us)
Async XLA Ops:
  6.4 35.0 %all-to-all-start = ((bf16[32,272,128]{2,1,0:T(8,128)(2,1)}), bf16[32,272,128]{2,1,0:T(8,128)(2,1)S(1)}, u32[]{:S(2)}, u32[]{:S(2)}) async-start(bf16[32,272,128]{2,1,0:T(8,128)(2,1)} %bitcast.25), calls=%async_computation | async-start | bytes 4456448 | tf_op jit(solution)/shard_map/all_to_all | solution.py:445
  41.4 37.2 %all-to-all-start.1 = ((bf16[32,208,128]{2,1,0:T(8,128)(2,1)}), bf16[32,208,128]{2,1,0:T(8,128)(2,1)}, u32[]{:S(2)}, u32[]{:S(2)}) async-start(bf16[32,208,128]{2,1,0:T(8,128)(2,1)} %bitcast.27), calls=%async_computation.1 | async-start | bytes 3407872 | tf_op jit(solution)/shard_map/all_to_all | solution.py:445
  52.3 16.0 %collective-permute-start.12 = (bf16[58,32,128]{2,1,0:T(8,128)(2,1)}, bf16[58,32,128]{2,1,0:T(8,128)(2,1)S(1)}, u32[]{:S(2)}, u32[]{:S(2)}) collective-permute-start(bf16[58,32,128]{2,1,0:T(8,128)(2,1)} %get-tuple-element.66.refs_0_), channel_id=1, source_target_pairs={{0,32},{32,64},{64,96},{96,0},{1,33},{33,65},{65,97},{97,1},{2,34}... | collective-permute-start | bytes 1425416 | tf_op jit(solution)/shard_map/ppermute | solution.py:449
  54.3 14.0 %collective-permute-start.15 = (bf16[58,32,128]{2,1,0:T(8,128)(2,1)}, bf16[58,32,128]{2,1,0:T(8,128)(2,1)S(1)}, u32[]{:S(2)}, u32[]{:S(2)}) collective-permute-start(bf16[58,32,128]{2,1,0:T(8,128)(2,1)} %get-tuple-element.67.refs_1_), channel_id=1, source_target_pairs={{0,96},{32,0},{64,32},{96,64},{1,97},{33,1},{65,33},{97,65},{2,98}... | collective-permute-start | bytes 1425416 | tf_op jit(solution)/shard_map/ppermute | solution.py:453
  56.5 22.0 %collective-permute-start.13 = (bf16[58,32,128]{2,1,0:T(8,128)(2,1)}, bf16[58,32,128]{2,1,0:T(8,128)(2,1)}, u32[]{:S(2)}, u32[]{:S(2)}) collective-permute-start(bf16[58,32,128]{2,1,0:T(8,128)(2,1)} %get-tuple-element.66.refs_0_), channel_id=1, source_target_pairs={{0,96},{32,0},{64,32},{96,64},{1,97},{33,1},{65,33},{97,65},{2,98}... | collective-permute-start | bytes 1425416 | tf_op jit(solution)/shard_map/ppermute | solution.py:453
  58.4 20.1 %collective-permute-start.14 = (bf16[58,32,128]{2,1,0:T(8,128)(2,1)}, bf16[58,32,128]{2,1,0:T(8,128)(2,1)}, u32[]{:S(2)}, u32[]{:S(2)}) collective-permute-start(bf16[58,32,128]{2,1,0:T(8,128)(2,1)} %get-tuple-element.67.refs_1_), channel_id=1, source_target_pairs={{0,32},{32,64},{64,96},{96,0},{1,33},{33,65},{65,97},{97,1},{2,34}... | collective-permute-start | bytes 1425416 | tf_op jit(solution)/shard_map/ppermute | solution.py:449
  68.3 10.3 %copy-start.5 = (bf16[58,32,128]{2,1,0:T(8,128)(2,1)}, bf16[58,32,128]{2,1,0:T(8,128)(2,1)S(1)}, u32[]{:S(2)}) copy-start(bf16[58,32,128]{2,1,0:T(8,128)(2,1)S(1)} %collective-permute-done.12.refs_0_.refs_6_) | copy-start | bytes 1425412
  68.3 20.0 %collective-permute-start.18 = (bf16[58,32,128]{2,1,0:T(8,128)(2,1)S(1)}, bf16[58,32,128]{2,1,0:T(8,128)(2,1)}, u32[]{:S(2)}, u32[]{:S(2)}) collective-permute-start(bf16[58,32,128]{2,1,0:T(8,128)(2,1)S(1)} %collective-permute-done.12.refs_0_.refs_6_), channel_id=1, source_target_pairs={{0,32},{32,64},{64,96},{96,0},{1,33},{33,65},{65,97},{97,1},{2,34}... | collective-permute-start | bytes 1425416 | tf_op jit(solution)/shard_map/ppermute | solution.py:449
  68.3 10.3 %copy-start.6 = (bf16[58,32,128]{2,1,0:T(8,128)(2,1)}, bf16[58,32,128]{2,1,0:T(8,128)(2,1)S(1)}, u32[]{:S(2)}) copy-start(bf16[58,32,128]{2,1,0:T(8,128)(2,1)S(1)} %collective-permute-done.15.refs_3_) | copy-start | bytes 1425412
  68.3 20.0 %collective-permute-start.19 = (bf16[58,32,128]{2,1,0:T(8,128)(2,1)S(1)}, bf16[58,32,128]{2,1,0:T(8,128)(2,1)}, u32[]{:S(2)}, u32[]{:S(2)}) collective-permute-start(bf16[58,32,128]{2,1,0:T(8,128)(2,1)S(1)} %collective-permute-done.15.refs_3_), channel_id=1, source_target_pairs={{0,96},{32,0},{64,32},{96,64},{1,97},{33,1},{65,33},{97,65},{2,98}... | collective-permute-start | bytes 1425416 | tf_op jit(solution)/shard_map/ppermute | solution.py:453
  88.3 7.7 %copy-start.9 = (bf16[48,32,128]{2,1,0:T(8,128)(2,1)S(1)}, bf16[48,32,128]{2,1,0:T(8,128)(2,1)}, u32[]{:S(2)}) copy-start(bf16[48,32,128]{2,1,0:T(8,128)(2,1)} %get-tuple-element.68.refs_1_.refs_0_) | copy-start | bytes 1179652
  88.3 11.0 %copy-start.12 = (f32[32,128]{1,0:T(8,128)S(1)}, f32[32,128]{1,0:T(8,128)}, u32[]{:S(2)}) copy-start(f32[32,128]{1,0:T(8,128)} %get-tuple-element.76) | copy-start | bytes 49156
  88.3 39.6 %all-to-all-start.2 = ((bf16[64,128,128]{2,1,0:T(8,128)(2,1)}), bf16[64,128,128]{2,1,0:T(8,128)(2,1)}, u32[]{:S(2)}, u32[]{:S(2)}) async-start(bf16[64,128,128]{2,1,0:T(8,128)(2,1)} %shard_map.119), calls=%async_computation.2 | async-start | bytes 4194304 | tf_op jit(solution)/shard_map/all_to_all | solution.py:445
  96.0 12.5 %collective-permute-start.20 = (bf16[48,32,128]{2,1,0:T(8,128)(2,1)S(1)}, bf16[48,32,128]{2,1,0:T(8,128)(2,1)S(1)}, u32[]{:S(2)}, u32[]{:S(2)}) collective-permute-start(bf16[48,32,128]{2,1,0:T(8,128)(2,1)S(1)} %copy-done.9), channel_id=1, source_target_pairs={{0,32},{32,64},{64,96},{96,0},{1,33},{33,65},{65,97},{97,1},{2,34}... | collective-permute-start | bytes 1179656 | tf_op jit(solution)/shard_map/ppermute | solution.py:449
  97.3 12.0 %collective-permute-start.17 = (bf16[48,32,128]{2,1,0:T(8,128)(2,1)}, bf16[48,32,128]{2,1,0:T(8,128)(2,1)S(1)}, u32[]{:S(2)}, u32[]{:S(2)}) collective-permute-start(bf16[48,32,128]{2,1,0:T(8,128)(2,1)} %get-tuple-element.69.refs_2_.refs_1_), channel_id=1, source_target_pairs={{0,96},{32,0},{64,32},{96,64},{1,97},{33,1},{65,33},{97,65},{2,98}... | collective-permute-start | bytes 1179656 | tf_op jit(solution)/shard_map/ppermute | solution.py:453
  105.8 12.2 %collective-permute-start.16 = (bf16[48,32,128]{2,1,0:T(8,128)(2,1)S(1)}, bf16[48,32,128]{2,1,0:T(8,128)(2,1)}, u32[]{:S(2)}, u32[]{:S(2)}) collective-permute-start(bf16[48,32,128]{2,1,0:T(8,128)(2,1)S(1)} %copy-done.9), channel_id=1, source_target_pairs={{0,96},{32,0},{64,32},{96,64},{1,97},{33,1},{65,33},{97,65},{2,98}... | collective-permute-start | bytes 1179656 | tf_op jit(solution)/shard_map/ppermute | solution.py:453
  107.7 13.6 %collective-permute-start.23 = (bf16[48,32,128]{2,1,0:T(8,128)(2,1)}, bf16[48,32,128]{2,1,0:T(8,128)(2,1)}, u32[]{:S(2)}, u32[]{:S(2)}) collective-permute-start(bf16[48,32,128]{2,1,0:T(8,128)(2,1)} %get-tuple-element.69.refs_2_.refs_1_), channel_id=1, source_target_pairs={{0,32},{32,64},{64,96},{96,0},{1,33},{33,65},{65,97},{97,1},{2,34}... | collective-permute-start | bytes 1179656 | tf_op jit(solution)/shard_map/ppermute | solution.py:449
  108.5 0.8 copy-start.8
  109.2 4.0 %copy-start.14 = (f32[2]{0:T(128)S(1)}, f32[2]{0:T(128)}, u32[]{:S(2)}) copy-start(f32[2]{0:T(128)} %constant.15) | copy-start | bytes 28
  109.2 6.2 %copy-start.13 = (f32[32,128]{1,0:T(8,128)S(1)}, f32[32,128]{1,0:T(8,128)}, u32[]{:S(2)}) copy-start(f32[32,128]{1,0:T(8,128)} %get-tuple-element.75) | copy-start | bytes 49156
  109.2 18.7 %collective-permute-start.21 = (bf16[48,32,128]{2,1,0:T(8,128)(2,1)}, bf16[48,32,128]{2,1,0:T(8,128)(2,1)S(1)}, u32[]{:S(2)}, u32[]{:S(2)}) collective-permute-start(bf16[48,32,128]{2,1,0:T(8,128)(2,1)} %shard_map.118.refs_6_), channel_id=1, source_target_pairs={{0,32},{32,64},{64,96},{96,0},{1,33},{33,65},{65,97},{97,1},{2,34}... | collective-permute-start | bytes 1179656 | tf_op jit(solution)/shard_map/ppermute | solution.py:449
  109.3 0.8 copy-start.7
  110.0 17.9 %collective-permute-start.22 = (bf16[48,32,128]{2,1,0:T(8,128)(2,1)}, bf16[48,32,128]{2,1,0:T(8,128)(2,1)S(1)}, u32[]{:S(2)}, u32[]{:S(2)}) collective-permute-start(bf16[48,32,128]{2,1,0:T(8,128)(2,1)} %shard_map.117.refs_3_), channel_id=1, source_target_pairs={{0,96},{32,0},{64,32},{96,64},{1,97},{33,1},{65,33},{97,65},{2,98}... | collective-permute-start | bytes 1179656 | tf_op jit(solution)/shard_map/ppermute | solution.py:453
  127.9 0.8 copy-start.10
  127.9 0.9 copy-start.11

commit v5 on v4

--- a/solution.py
+++ b/solution.py
@@ -17,11 +17,11 @@
 SLOTS = WRITERS * CAP
 VMEM = 60 * 1024 * 1024
 
-WHOLE = 2
+WHOLE = 3
 BY_ROWS_MOMENT = CAP
 BY_ROWS_WEIGHT = CAP - WHOLE
-USUAL = (116, 96)
-FULL = (WRITERS * BY_ROWS_MOMENT + 8, WRITERS * BY_ROWS_WEIGHT + 8)
+USUAL = ((54, 54), (56,))
+FULL = ((132, 132), (168,))
 
 
 def clear(ref, length, value):
@@ -260,13 +260,20 @@
     yield
 
 
-def pack_moment_kernel(half, ticket, payload, first, second, kept_w, kept_m, totals, scales, held, packed, tiles, staged, spread, sems, tile_sems):
+def share(packed, own):
+    start = 0
+    for part in own:
+        part[...] = packed[start : start + part.shape[0]]
+        start += part.shape[0]
+
+
+def pack_moment_kernel(ticket, payload, *refs):
+    *own, kept_w, kept_m, totals, scales, held, packed, tiles, staged, spread, sems, tile_sems = refs
     steps = pack(BY_ROWS_MOMENT, payload, held, packed, sems, lambda s: [spread[1, s, k] for k in range(CAP)])
     next(steps)
     lines = spread_lines(payload, BY_ROWS_MOMENT, tiles, staged, spread, tile_sems)
     next(steps)
-    first[...] = packed[0:half]
-    second[...] = packed[half : 2 * half]
+    share(packed, own)
     scales[...] = lines[0]
     kept_w[...] = lines[1].astype(jnp.int32)
     kept_m[...] = lines[2].astype(jnp.int32)
@@ -277,15 +284,13 @@
 
 def pack_moment(capacity, ticket, payload):
     width = payload.shape[-1]
-    half = capacity // 2
-    part = jax.ShapeDtypeStruct((half, ROWS, width), jnp.bfloat16)
+    parts = [jax.ShapeDtypeStruct((size, ROWS, width), jnp.bfloat16) for size in capacity]
     flags = jax.ShapeDtypeStruct((WRITERS, width), jnp.int32)
     return pl.pallas_call(
-        functools.partial(pack_moment_kernel, half),
+        pack_moment_kernel,
         in_specs=[pl.BlockSpec(memory_space=pltpu.SMEM), HBM],
         out_shape=[
-            part,
-            part,
+            *parts,
             flags,
             flags,
             jax.ShapeDtypeStruct((8, width), jnp.float32),
@@ -293,7 +298,7 @@
         ],
         scratch_shapes=[
             pltpu.VMEM((WRITERS, payload_rows(BY_ROWS_MOMENT), width), jnp.bfloat16),
-            pltpu.VMEM((capacity, ROWS, width), jnp.bfloat16),
+            pltpu.VMEM((sum(capacity), ROWS, width), jnp.bfloat16),
             pltpu.VMEM((WRITERS, TILE, width), jnp.bfloat16),
             pltpu.VMEM((2, WRITERS, width), jnp.int32),
             pltpu.SMEM((2, WRITERS, width), jnp.int32),
@@ -305,8 +310,8 @@
     )(ticket, payload.reshape(WRITERS, -1, width))
 
 
-def pack_weight_kernel(half, kept, payload, *refs):
-    first, second, scales, held, packed, sems = refs[-6:]
+def pack_weight_kernel(kept, payload, *refs):
+    *own, scales, held, packed, sems = refs
 
     def advance(s):
         found = functools.reduce(jnp.add, [kept[s, k] for k in range(CAP)])
@@ -315,32 +320,30 @@
     steps = pack(BY_ROWS_WEIGHT, payload, held, packed, sems, advance)
     next(steps)
     next(steps)
-    first[...] = packed[0:half]
-    second[...] = packed[half : 2 * half]
+    share(packed, own)
     scales[...] = held[:, pl.ds(BY_ROWS_WEIGHT * ROWS, TILE), :].astype(jnp.float32)[:, 0, :]
 
 
-def pack_weight(capacity, kept, payload, earlier):
+def pack_weight(capacity, kept, payload):
     width = payload.shape[-1]
-    half = capacity // 2
-    part = jax.ShapeDtypeStruct((half, ROWS, width), jnp.bfloat16)
+    parts = [jax.ShapeDtypeStruct((size, ROWS, width), jnp.bfloat16) for size in capacity]
     return pl.pallas_call(
-        functools.partial(pack_weight_kernel, half),
+        pack_weight_kernel,
         grid_spec=pltpu.PrefetchScalarGridSpec(
             num_scalar_prefetch=1,
             grid=(1,),
-            in_specs=[HBM] * (1 + len(earlier)),
-            out_specs=[pl.BlockSpec(part.shape, lambda i, *_: (0, 0, 0))] * 2 + [pl.BlockSpec((WRITERS, width), lambda i, *_: (0, 0))],
+            in_specs=[HBM],
+            out_specs=[pl.BlockSpec(part.shape, lambda i, *_: (0, 0, 0)) for part in parts] + [pl.BlockSpec((WRITERS, width), lambda i, *_: (0, 0))],
             scratch_shapes=[
                 pltpu.VMEM((WRITERS, payload_rows(BY_ROWS_WEIGHT), width), jnp.bfloat16),
-                pltpu.VMEM((capacity, ROWS, width), jnp.bfloat16),
+                pltpu.VMEM((sum(capacity), ROWS, width), jnp.bfloat16),
                 pltpu.SemaphoreType.DMA((WRITERS // SOURCES,)),
             ],
         ),
-        out_shape=[part, part, jax.ShapeDtypeStruct((WRITERS, width), jnp.float32)],
+        out_shape=[*parts, jax.ShapeDtypeStruct((WRITERS, width), jnp.float32)],
         compiler_params=params(),
         cost_estimate=cost(0, 0),
-    )(kept, payload.reshape(WRITERS, -1, width), *earlier)
+    )(kept, payload.reshape(WRITERS, -1, width))
 
 
 def after_kernel(*refs):
@@ -358,33 +361,33 @@
     )(values, *earlier)
 
 
-ALL_TURNS, NEAR_TURNS, FAR_TURN = (0, 1, 2, 3), (0, 1, 3), (2,)
-
-
-def unpack_kernel(by_rows, half, turns, replica, kept, *refs):
-    n_whole = CAP - by_rows
-    n_parts = 2 * len(turns)
-    parts, refs = refs[:n_parts], refs[n_parts:]
-    whole = refs[0] if n_whole else None
+def unpack_kernel(n_whole, sizes, replica, kept, *refs):
     out, held, built, sems, out_sems = refs[-5:]
-    nothing, first_whole = 2 * half, 2 * half + 1
-    rows = [pl.ds(pl.multiple_of(lax.rem(replica[0] + turn, 4) * ROWS, ROWS), ROWS) for turn in turns]
-    copies = [pltpu.make_async_copy(part, held.at[i // 2, pl.ds((i % 2) * half, half)], sems.at[i]) for i, part in enumerate(parts)]
+    nothing = sum(sizes[0])
+    first_whole = nothing + 1
+    rows = [pl.ds(pl.multiple_of(lax.rem(replica[0] + turn, 4) * ROWS, ROWS), ROWS) for turn in range(4)]
+    copies = []
+    for turn in range(4):
+        start = 0
+        for size in sizes[turn]:
+            i = len(copies)
+            copies.append(pltpu.make_async_copy(refs[i], held.at[turn, pl.ds(start, size)], sems.at[i]))
+            start += size
     if n_whole:
-        for i in range(len(turns)):
-            here = held.at[i, pl.ds(first_whole, WRITERS * n_whole)]
-            copies.append(pltpu.make_async_copy(whole.at[:, rows[i], :], here, sems.at[n_parts + i]))
+        whole = refs[len(copies)]
+        for turn in range(4):
+            there = held.at[turn, pl.ds(first_whole, WRITERS * n_whole)]
+            copies.append(pltpu.make_async_copy(whole.at[:, rows[turn], :], there, sems.at[len(copies)]))
     for copy in copies:
         copy.start()
-    for i in range(len(turns)):
-        held[i, nothing] = jnp.zeros(held.shape[2:], held.dtype)
+    for turn in range(4):
+        held[turn, nothing] = jnp.zeros(held.shape[2:], held.dtype)
     for copy in copies:
         copy.wait()
 
     def send(step):
         part = pl.ds(step * SOURCES * CAP, SOURCES * CAP)
-        there = out.at[part, rows[0], :] if len(turns) == 1 else out.at[part]
-        return pltpu.make_async_copy(built.at[part], there, out_sems.at[step])
+        return pltpu.make_async_copy(built.at[part], out.at[part], out_sems.at[step])
 
     def one(step, place):
         for s in range(SOURCES):
@@ -392,20 +395,17 @@
             rank = 0
             for k in range(CAP):
                 flag = kept[source, k]
+                origin = jnp.minimum(place, nothing - 1)
                 if n_whole:
                     as_whole = rank < n_whole
-                    origin = jnp.where(as_whole, first_whole + source * n_whole + rank, jnp.minimum(place, nothing - 1))
+                    origin = jnp.where(as_whole, first_whole + source * n_whole + rank, origin)
                     place = place + jnp.where(as_whole, 0, flag)
                     rank = rank + flag
                 else:
-                    origin = jnp.minimum(place, nothing - 1)
                     place = place + flag
                 origin = jnp.where(flag > 0, origin, nothing)
-                for i in range(len(turns)):
-                    if len(turns) == 1:
-                        built[source * CAP + k] = held[i, origin]
-                    else:
-                        built[source * CAP + k, rows[i], :] = held[i, origin]
+                for turn in range(4):
+                    built[source * CAP + k, rows[turn], :] = held[turn, origin]
         send(step).start()
         return place
 
@@ -415,27 +415,26 @@
         send(step).wait()
 
 
-def unpack_call(by_rows, capacity, turns, replica, kept, parts, whole=None, out=None):
-    width = parts[0].shape[-1]
-    n_whole = WRITERS * (CAP - by_rows)
-    parts = [part for turn in turns for part in parts[2 * turn : 2 * turn + 2]]
-    operands = [*parts] + ([] if whole is None else [whole]) + ([] if out is None else [out])
+def unpack(replica, kept, parts, whole=None):
+    sizes = [[piece.shape[0] for piece in part] for part in parts]
+    operands = [piece for part in parts for piece in part] + ([] if whole is None else [whole])
+    n_whole = 0 if whole is None else WHOLE
+    width = operands[0].shape[-1]
     return pl.pallas_call(
-        functools.partial(unpack_kernel, by_rows, capacity // 2, turns),
+        functools.partial(unpack_kernel, n_whole, sizes),
         grid_spec=pltpu.PrefetchScalarGridSpec(
             num_scalar_prefetch=2,
             grid=(1,),
             in_specs=[HBM] * len(operands),
             out_specs=HBM,
             scratch_shapes=[
-                pltpu.VMEM((len(turns), capacity + 1 + n_whole, ROWS, width), jnp.bfloat16),
-                pltpu.VMEM((SLOTS, ROWS if len(turns) == 1 else width, width), jnp.bfloat16),
-                pltpu.SemaphoreType.DMA((3 * len(turns),)),
+                pltpu.VMEM((4, sum(sizes[0]) + 1 + WRITERS * n_whole, ROWS, width), jnp.bfloat16),
+                pltpu.VMEM((SLOTS, width, width), jnp.bfloat16),
+                pltpu.SemaphoreType.DMA((len(operands) + 4,)),
                 pltpu.SemaphoreType.DMA((WRITERS // SOURCES,)),
             ],
         ),
         out_shape=jax.ShapeDtypeStruct((SLOTS, width, width), jnp.bfloat16),
-        input_output_aliases={} if out is None else {1 + len(operands): 0},
         compiler_params=params(),
         cost_estimate=cost(0, 0),
     )(replica, kept, *operands)
@@ -453,38 +452,23 @@
     return lax.ppermute(values, "replica", [(i, (i - 1) % 4) for i in range(4)])
 
 
-def first_round(first, second):
-    first_up, second_down = upward(first), downward(second)
-    return first_up, downward(first), upward(second), second_down
-
-
-def second_round(first_up, second_down):
-    return upward(first_up), downward(second_down)
-
-
-def by_turn(first, second, near, far):
-    return (first, second, near[1], near[3], *far, near[0], near[2])
-
-
-def rest(capacities, replica, m_read, m_near, m_far, w_read, w_near, w_far, w_whole):
-    written_moment = unpack_call(BY_ROWS_MOMENT, capacities[0], ALL_TURNS, replica, m_read[3], by_turn(*m_read[:2], m_near, m_far))
-    if w_far is None:
-        w_near = (after(w_near[0], (written_moment,)), *w_near[1:3], after(w_near[3], (written_moment,)))
-        w_far = second_round(w_near[0], w_near[3])
-    written_weight = unpack_call(
-        BY_ROWS_WEIGHT, capacities[1], ALL_TURNS, replica, m_read[2], by_turn(*w_read[:2], w_near, w_far), w_whole
-    )
+def along_z(first, second):
+    first_up, first_down = upward(first), downward(first)
+    second_up, second_down = upward(second), downward(second)
+    return (first_up, second_down), ((first, second), (first_down, second_down), (upward(first_up), downward(second_down)), (first_up, second_up))
+
+
+def along_z_down(own):
+    up, down = upward(own), downward(own)
+    return ((own,), (down,), (downward(down),), (up,))
+
+
+def exchange_again(ticket, replica, m_payload, w_payload, w_whole):
+    *m_own, kept_w, kept_m, _, _ = pack_moment(FULL[0], ticket, m_payload)
+    written_moment = unpack(replica, kept_m, along_z(*m_own)[1])
+    *w_own, _ = pack_weight(FULL[1], kept_w, w_payload)
+    written_weight = unpack(replica, kept_w, along_z_down(*w_own), w_whole)
     return written_weight, written_moment
-
-
-def exchange_again(ticket, replica, m_payload, w_payload, w_whole):
-    m_read = pack_moment(FULL[0], ticket, m_payload)
-    m_near = first_round(*m_read[:2])
-    m_far = second_round(m_near[0], m_near[3])
-    w_read = pack_weight(FULL[1], m_read[2], w_payload, ())
-    w_near = first_round(*w_read[:2])
-    w_far = second_round(w_near[0], w_near[3])
-    return rest(FULL, replica, m_read, m_near, m_far, w_read, w_near, w_far, w_whole)
 
 
 def on_device(weight, moment, base_codes, base_scale, weight_mask, moment_mask, writer):
@@ -494,21 +478,21 @@
     m_payload = regroup(moment_call(replica, target, weight_mask, moment_mask, moment))
     w_payload, w_whole, refreshed = weight_call(replica, target, weight_mask, base_scale, weight, base_codes)
     w_payload = regroup(after(w_payload, (m_payload,)))
-    m_read = pack_moment(USUAL[0], replica, m_payload)
-    m_near = first_round(*m_read[:2])
-    m_far = second_round(m_near[0], m_near[3])
-    w_read = pack_weight(USUAL[1], m_read[2], w_payload, m_near)
-    w_whole = regroup(after(w_whole, (*w_read[:2], *m_far)))
-    w_near = first_round(*w_read[:2])
-    written_weight, written_moment = rest(USUAL, replica, m_read, m_near, m_far, w_read, w_near, None, w_whole)
-
-    over = jnp.any(m_read[4][:2, :WRITERS] >= jnp.array([[USUAL[1]], [USUAL[0]]], jnp.float32)).astype(jnp.int32)
+    *m_own, kept_w, kept_m, totals, m_scales = pack_moment(USUAL[0], replica, m_payload)
+    m_near, m_parts = along_z(*m_own)
+    w_whole = regroup(after(w_whole, (w_payload, *m_near)))
+    *w_own, w_scales = pack_weight(USUAL[1], kept_w, w_payload)
+    w_parts = along_z_down(*w_own)
+    written_moment = unpack(replica, kept_m, m_parts)
+    written_weight = unpack(replica, kept_w, w_parts, w_whole)
+
+    over = jnp.any(totals[:2, :WRITERS] >= jnp.array([[sum(USUAL[1])], [sum(USUAL[0])]], jnp.float32)).astype(jnp.int32)
     _, written_weight, written_moment = lax.while_loop(
         lambda carry: carry[0] < over,
         lambda carry: (carry[0] + 1, *exchange_again(carry[0].reshape(1), replica, m_payload, w_payload, w_whole)),
         (jnp.int32(0), written_weight, written_moment),
     )
-    written_scales = jnp.stack([w_read[2][:, :CAP], m_read[5][:, :CAP]], axis=0).astype(jnp.bfloat16)
+    written_scales = jnp.stack([w_scales[:, :CAP], m_scales[:, :CAP]], axis=0).astype(jnp.bfloat16)
     shape = (WRITERS, CAP, width, width)
     return written_weight.reshape(shape), written_moment.reshape(shape), written_scales, refreshed
 

time: 137 us -> 129 us (0.942)
  waiting for transfers between devices: 45.3 us -> 42 us
  local copies, waits for them, and re-layouts: 2.61 us -> 0.36 us
  starting transfers between devices: 41.1 us -> 39.2 us
    ppermute x6 -> x4, waiting for transfers between devices: 26.3 us -> 10.6 us  [upward(): return lax.ppermute(values, 'replica', [(i, (i + 1) % 4) for i in range(4)])]
    ppermute x6 -> x5, waiting for transfers between devices: 8.85 us -> 20.7 us  [downward(): return lax.ppermute(values, 'replica', [(i, (i - 1) % 4) for i in range(4)])]
    unnamed x20 -> x12, local copies, waits for them, and re-layouts: 2.45 us -> 0.2 us
    ppermute x6 -> x5, starting transfers between devices: 14.6 us -> 12.5 us  [downward(): return lax.ppermute(values, 'replica', [(i, (i - 1) % 4) for i in range(4)])]
    ppermute x6 -> x4, starting transfers between devices: 3.61 us -> 3.97 us  [upward(): return lax.ppermute(values, 'replica', [(i, (i + 1) % 4) for i in range(4)])]
  transfers between devices with their start and end apart: 15 -> 12, of which waited for: 8 -> 6; matrix products, arithmetic and copies ran while one was open for 2% -> 2% of each run, Pallas kernels for 23% -> 24%
where the time goes in v5:
time: 129 us; the launch traced here: 128 us
  Pallas kernels  42.5 us (33%)
  waiting for transfers between devices  42 us (33%)
  starting transfers between devices  39.2 us (30%)
  other arithmetic  2.06 us (2%)
  between operations  1.58 us (1%)
    all_to_all x3, starting transfers between devices, regroup(): lax.all_to_all(values, 'fsdp', split_axis=0, concat_axis=0, tiled=True)  22.8 us
    ppermute x5, waiting for transfers between devices, downward(): return lax.ppermute(values, 'replica', [(i, (i - 1) % 4) for i in range(4)])  20.7 us
    pallas_call x1, Pallas kernels, weight_call(): pl.pallas_call(functools.partial(weight_kernel, blocks), grid_spec=pltpu....  17.4 us
    pallas_call x2, Pallas kernels, unpack(): pl.pallas_call(functools.partial(unpack_kernel, n_whole, sizes), grid_spe...  12.6 us
    ppermute x5, starting transfers between devices, downward(): return lax.ppermute(values, 'replica', [(i, (i - 1) % 4) for i in range(4)])  12.5 us
    all_to_all x3, waiting for transfers between devices, regroup(): lax.all_to_all(values, 'fsdp', split_axis=0, concat_axis=0, tiled=True)  10.7 us
    ppermute x4, waiting for transfers between devices, upward(): return lax.ppermute(values, 'replica', [(i, (i + 1) % 4) for i in range(4)])  10.6 us
    pallas_call x1, Pallas kernels, moment_call(): pl.pallas_call(moment_kernel, grid_spec=pltpu.PrefetchScalarGridSpec(num_...  5.76 us
  transfers between devices with their start and end apart: 12, of which 6 were waited for; matrix products, arithmetic and copies ran while one was open for 2% of the time, Pallas kernels for 24%

profile of v5, /device:TPU:2, one launch (start us, length us, event | category | flops | bytes accessed | tf_op | source)
XLA Modules:
  0.0 127.9 jit_solution(15987548430527796544)
XLA Ops:
  0.6 5.8 %shard_map.111 = bf16[8704,128]{1,0:T(8,128)(2,1)} custom-call(s32[1]{0:T(128)} %bitcast.3.replica.ticket, s32[128]{0:T(128)} %bitcast.28, s32[128]{0:T(128)} %weight_mask.3, s32[128]{0:T(128)} %moment_mask.1, f32[128,128,128]{2,1,0:T(8,128)} %moment.1), custom_call_target="tpu_custom_call" | custom-call | flops 10485760 | bytes 12582912 | tf_op jit(solution)/shard_map/pallas_call | solution.py:166
  6.4 7.6 %all-to-all-start = ((bf16[32,272,128]{2,1,0:T(8,128)(2,1)}), bf16[32,272,128]{2,1,0:T(8,128)(2,1)S(1)}, u32[]{:S(2)}, u32[]{:S(2)}) async-start(bf16[32,272,128]{2,1,0:T(8,128)(2,1)} %bitcast.24), calls=%async_computation | async-start | bytes 4456448 | tf_op jit(solution)/shard_map/all_to_all | solution.py:444
  14.0 17.4 %shard_map.113 = (bf16[5632,128]{1,0:T(8,128)(2,1)}, bf16[96,128,128]{2,1,0:T(8,128)(2,1)}, bf16[128,128,128]{2,1,0:T(8,128)(2,1)}) custom-call(s32[1]{0:T(128)} %bitcast.3.replica.ticket, s32[128]{0:T(128)} %bitcast.29, s32[128]{0:T(128)} %weight_mask.3, f32[128]{0:T(128)} %base_scale.1, f32[128,128,128]{2,1,0:T(8,128)} %weight.1, s32[128,128,128]{2,1,0:T(8,128)} %codes.1), custom_call_target="tpu_custom_call" | custom-call | flops 20971520 | bytes 29360128 | tf_op jit(solution)/shard_map/pallas_call | solution.py:192
  31.5 9.9 %all-to-all-done.payload = bf16[32,272,128]{2,1,0:T(8,128)(2,1)S(1)} async-done(((bf16[32,272,128]{2,1,0:T(8,128)(2,1)}), bf16[32,272,128]{2,1,0:T(8,128)(2,1)S(1)}, u32[]{:S(2)}, u32[]{:S(2)}) %all-to-all-start) | async-done | bytes 2228256 | tf_op jit(solution)/shard_map/all_to_all | solution.py:444
  41.4 7.6 %all-to-all-start.1 = ((bf16[32,176,128]{2,1,0:T(8,128)(2,1)}), bf16[32,176,128]{2,1,0:T(8,128)(2,1)}, u32[]{:S(2)}, u32[]{:S(2)}) async-start(bf16[32,176,128]{2,1,0:T(8,128)(2,1)} %bitcast.27), calls=%async_computation.1 | async-start | bytes 2883584 | tf_op jit(solution)/shard_map/all_to_all | solution.py:444
  49.0 3.3 %shard_map.112 = (bf16[54,32,128]{2,1,0:T(8,128)(2,1)}, bf16[54,32,128]{2,1,0:T(8,128)(2,1)}, s32[32,128]{1,0:T(8,128)}, s32[32,128]{1,0:T(8,128)}, f32[8,128]{1,0:T(8,128)}, /*index=5*/f32[32,128]{1,0:T(8,128)}) custom-call(s32[1]{0:T(128)} %bitcast.3.replica.ticket, bf16[32,272,128]{2,1,0:T(8,128)(2,1)S(1)} %all-to-all-done.payload), custom_call_target="tpu_custom_call" | custom-call | tf_op jit(solution)/shard_map/pallas_call | solution.py:289
  52.3 2.0 %collective-permute-start.12 = (bf16[54,32,128]{2,1,0:T(8,128)(2,1)}, bf16[54,32,128]{2,1,0:T(8,128)(2,1)S(1)}, u32[]{:S(2)}, u32[]{:S(2)}) collective-permute-start(bf16[54,32,128]{2,1,0:T(8,128)(2,1)} %get-tuple-element.66.refs_0_), channel_id=1, source_target_pairs={{0,32},{32,64},{64,96},{96,0},{1,33},{33,65},{65,97},{97,1},{2,34}... | collective-permute-start | bytes 1327112 | tf_op jit(solution)/shard_map/ppermute | solution.py:448
  54.3 2.2 %collective-permute-start.13 = (bf16[54,32,128]{2,1,0:T(8,128)(2,1)}, bf16[54,32,128]{2,1,0:T(8,128)(2,1)S(1)}, u32[]{:S(2)}, u32[]{:S(2)}) collective-permute-start(bf16[54,32,128]{2,1,0:T(8,128)(2,1)} %get-tuple-element.67.refs_1_), channel_id=1, source_target_pairs={{0,96},{32,0},{64,32},{96,64},{1,97},{33,1},{65,33},{97,65},{2,98}... | collective-permute-start | bytes 1327112 | tf_op jit(solution)/shard_map/ppermute | solution.py:452
  56.5 10.6 %collective-permute-done.12.refs_2_.refs_6_ = bf16[54,32,128]{2,1,0:T(8,128)(2,1)S(1)} collective-permute-done((bf16[54,32,128]{2,1,0:T(8,128)(2,1)}, bf16[54,32,128]{2,1,0:T(8,128)(2,1)S(1)}, u32[]{:S(2)}, u32[]{:S(2)}) %collective-permute-start.12) | collective-permute-done | bytes 442400 | tf_op jit(solution)/shard_map/ppermute | solution.py:448
  67.1 0.0 collective-permute-done.13.refs_3_
  67.1 0.7 all-to-all-done.1.payload
  67.8 0.0 copy-done.1
  67.9 0.1 copy-done.2
  68.0 7.6 %all-to-all-start.2 = ((bf16[96,128,128]{2,1,0:T(8,128)(2,1)}), bf16[96,128,128]{2,1,0:T(8,128)(2,1)S(1)}, u32[]{:S(2)}, u32[]{:S(2)}) async-start(bf16[96,128,128]{2,1,0:T(8,128)(2,1)} %shard_map.116), calls=%async_computation.2 | async-start | bytes 6291456 | tf_op jit(solution)/shard_map/all_to_all | solution.py:444
  75.6 3.4 %shard_map.115 = (bf16[56,32,128]{2,1,0:T(8,128)(2,1)}, f32[32,128]{1,0:T(8,128)}) custom-call(s32[32,128]{1,0:T(8,128)} %get-tuple-element.62.kept, bf16[32,176,128]{2,1,0:T(8,128)(2,1)} %all-to-all-done.1.payload), custom_call_target="tpu_custom_call" | custom-call | tf_op jit(solution)/shard_map/pallas_call | solution.py:330
  79.0 3.3 %collective-permute-start.9 = (bf16[56,32,128]{2,1,0:T(8,128)(2,1)}, bf16[56,32,128]{2,1,0:T(8,128)(2,1)}, u32[]{:S(2)}, u32[]{:S(2)}) collective-permute-start(bf16[56,32,128]{2,1,0:T(8,128)(2,1)} %get-tuple-element.64.refs_0_), channel_id=1, source_target_pairs={{0,96},{32,0},{64,32},{96,64},{1,97},{33,1},{65,33},{97,65},{2,98}... | collective-permute-start | bytes 1376264 | tf_op jit(solution)/shard_map/ppermute | solution.py:452
  82.3 0.4 collective-permute-start.14
  82.7 1.6 %collective-permute-start.17 = (bf16[54,32,128]{2,1,0:T(8,128)(2,1)}, bf16[54,32,128]{2,1,0:T(8,128)(2,1)}, u32[]{:S(2)}, u32[]{:S(2)}) collective-permute-start(bf16[54,32,128]{2,1,0:T(8,128)(2,1)} %get-tuple-element.67.refs_1_), channel_id=1, source_target_pairs={{0,32},{32,64},{64,96},{96,0},{1,33},{33,65},{65,97},{97,1},{2,34}... | collective-permute-start | bytes 1327112 | tf_op jit(solution)/shard_map/ppermute | solution.py:448
  84.3 0.0 collective-permute-start.15
  84.4 3.2 %collective-permute-start.16 = (bf16[54,32,128]{2,1,0:T(8,128)(2,1)}, bf16[54,32,128]{2,1,0:T(8,128)(2,1)}, u32[]{:S(2)}, u32[]{:S(2)}) collective-permute-start(bf16[54,32,128]{2,1,0:T(8,128)(2,1)} %copy-done.2), channel_id=1, source_target_pairs={{0,96},{32,0},{64,32},{96,64},{1,97},{33,1},{65,33},{97,65},{2,98}... | collective-permute-start | bytes 1327112 | tf_op jit(solution)/shard_map/ppermute | solution.py:452
  87.6 1.5 %compare_reduce_fusion = pred[]{:T(512)} fusion(f32[8,128]{1,0:T(8,128)} %get-tuple-element.69, f32[2]{0:T(128)S(1)} %copy-done.5), kind=kLoop, calls=%fused_computation.5 | loop fusion | flops 127 | bytes 265 | tf_op jit(solution)/shard_map/reduce_or | solution.py:489
  89.7 13.3 %collective-permute-done.14.refs_2_ = bf16[54,32,128]{2,1,0:T(8,128)(2,1)} collective-permute-done((bf16[54,32,128]{2,1,0:T(8,128)(2,1)}, bf16[54,32,128]{2,1,0:T(8,128)(2,1)}, u32[]{:S(2)}, u32[]{:S(2)}) %collective-permute-start.14) | collective-permute-done | bytes 442400 | tf_op jit(solution)/shard_map/ppermute | solution.py:452
  103.0 0.3 collective-permute-start.11
  103.3 3.4 %collective-permute-start.10 = (bf16[56,32,128]{2,1,0:T(8,128)(2,1)}, bf16[56,32,128]{2,1,0:T(8,128)(2,1)}, u32[]{:S(2)}, u32[]{:S(2)}) collective-permute-start(bf16[56,32,128]{2,1,0:T(8,128)(2,1)} %collective-permute-done.9.refs_1_), channel_id=1, source_target_pairs={{0,96},{32,0},{64,32},{96,64},{1,97},{33,1},{65,33},{97,65},{2,98}... | collective-permute-start | bytes 1376264 | tf_op jit(solution)/shard_map/ppermute | solution.py:452
  106.7 0.1 copy.16
  106.8 5.7 %collective-permute-done.16.refs_5_ = bf16[54,32,128]{2,1,0:T(8,128)(2,1)} collective-permute-done((bf16[54,32,128]{2,1,0:T(8,128)(2,1)}, bf16[54,32,128]{2,1,0:T(8,128)(2,1)}, u32[]{:S(2)}, u32[]{:S(2)}) %collective-permute-start.16) | collective-permute-done | bytes 442400 | tf_op jit(solution)/shard_map/ppermute | solution.py:452
  112.5 6.6 %shard_map.118 = bf16[256,128,128]{2,1,0:T(8,128)(2,1)} custom-call(s32[1]{0:T(128)} %bitcast.3.replica.ticket, s32[32,128]{1,0:T(8,128)} %get-tuple-element.68.kept, bf16[54,32,128]{2,1,0:T(8,128)(2,1)} %get-tuple-element.66.refs_0_, bf16[54,32,128]{2,1,0:T(8,128)(2,1)} %get-tuple-element.67.refs_1_, bf16[54,32,128]{2,1,0:T(8,128)(2,1)} %collective-permute-done.14.refs_2_, ...), custom_call_target="tpu_custom_call" | custom-call | tf_op jit(solution)/shard_map/pallas_call | solution.py:423
  119.1 0.1 copy.15
  119.2 0.6 pad_maximum_fusion
  119.8 1.7 %collective-permute-done.10.refs_2_ = bf16[56,32,128]{2,1,0:T(8,128)(2,1)} collective-permute-done((bf16[56,32,128]{2,1,0:T(8,128)(2,1)}, bf16[56,32,128]{2,1,0:T(8,128)(2,1)}, u32[]{:S(2)}, u32[]{:S(2)}) %collective-permute-start.10) | collective-permute-done | bytes 458784 | tf_op jit(solution)/shard_map/ppermute | solution.py:452
  121.5 6.0 %shard_map.117 = bf16[256,128,128]{2,1,0:T(8,128)(2,1)} custom-call(s32[1]{0:T(128)} %bitcast.3.replica.ticket, s32[32,128]{1,0:T(8,128)} %get-tuple-element.62.kept, bf16[56,32,128]{2,1,0:T(8,128)(2,1)} %get-tuple-element.64.refs_0_, bf16[56,32,128]{2,1,0:T(8,128)(2,1)} %collective-permute-done.9.refs_1_, ...), custom_call_target="tpu_custom_call" | custom-call | tf_op jit(solution)/shard_map/pallas_call | solution.py:423
  127.5 0.2 while.12
  (19 shorter events, 0.0 us)
Async XLA Ops:
  6.4 35.0 %all-to-all-start = ((bf16[32,272,128]{2,1,0:T(8,128)(2,1)}), bf16[32,272,128]{2,1,0:T(8,128)(2,1)S(1)}, u32[]{:S(2)}, u32[]{:S(2)}) async-start(bf16[32,272,128]{2,1,0:T(8,128)(2,1)} %bitcast.24), calls=%async_computation | async-start | bytes 4456448 | tf_op jit(solution)/shard_map/all_to_all | solution.py:444
  41.4 7.6 %copy-start = (bf16[32,272,128]{2,1,0:T(8,128)(2,1)}, bf16[32,272,128]{2,1,0:T(8,128)(2,1)S(1)}, u32[]{:S(2)}) copy-start(bf16[32,272,128]{2,1,0:T(8,128)(2,1)S(1)} %all-to-all-done.payload) | copy-start | bytes 6684676
  41.4 26.4 %all-to-all-start.1 = ((bf16[32,176,128]{2,1,0:T(8,128)(2,1)}), bf16[32,176,128]{2,1,0:T(8,128)(2,1)}, u32[]{:S(2)}, u32[]{:S(2)}) async-start(bf16[32,176,128]{2,1,0:T(8,128)(2,1)} %bitcast.27), calls=%async_computation.1 | async-start | bytes 2883584 | tf_op jit(solution)/shard_map/all_to_all | solution.py:444
  52.3 14.8 %collective-permute-start.12 = (bf16[54,32,128]{2,1,0:T(8,128)(2,1)}, bf16[54,32,128]{2,1,0:T(8,128)(2,1)S(1)}, u32[]{:S(2)}, u32[]{:S(2)}) collective-permute-start(bf16[54,32,128]{2,1,0:T(8,128)(2,1)} %get-tuple-element.66.refs_0_), channel_id=1, source_target_pairs={{0,32},{32,64},{64,96},{96,0},{1,33},{33,65},{65,97},{97,1},{2,34}... | collective-permute-start | bytes 1327112 | tf_op jit(solution)/shard_map/ppermute | solution.py:448
  54.3 12.8 %collective-permute-start.13 = (bf16[54,32,128]{2,1,0:T(8,128)(2,1)}, bf16[54,32,128]{2,1,0:T(8,128)(2,1)S(1)}, u32[]{:S(2)}, u32[]{:S(2)}) collective-permute-start(bf16[54,32,128]{2,1,0:T(8,128)(2,1)} %get-tuple-element.67.refs_1_), channel_id=1, source_target_pairs={{0,96},{32,0},{64,32},{96,64},{1,97},{33,1},{65,33},{97,65},{2,98}... | collective-permute-start | bytes 1327112 | tf_op jit(solution)/shard_map/ppermute | solution.py:452
  67.1 0.8 copy-start.1
  67.1 0.9 copy-start.2
  68.0 19.6 %copy-start.5 = (f32[2]{0:T(128)S(1)}, f32[2]{0:T(128)}, u32[]{:S(2)}) copy-start(f32[2]{0:T(128)} %constant.15) | copy-start | bytes 28
  68.0 38.7 %copy-start.3 = (f32[32,128]{1,0:T(8,128)S(1)}, f32[32,128]{1,0:T(8,128)}, u32[]{:S(2)}) copy-start(f32[32,128]{1,0:T(8,128)} %get-tuple-element.73) | copy-start | bytes 49156
  68.0 53.5 %all-to-all-start.2 = ((bf16[96,128,128]{2,1,0:T(8,128)(2,1)}), bf16[96,128,128]{2,1,0:T(8,128)(2,1)S(1)}, u32[]{:S(2)}, u32[]{:S(2)}) async-start(bf16[96,128,128]{2,1,0:T(8,128)(2,1)} %shard_map.116), calls=%async_computation.2 | async-start | bytes 6291456 | tf_op jit(solution)/shard_map/all_to_all | solution.py:444
  79.0 24.3 %collective-permute-start.9 = (bf16[56,32,128]{2,1,0:T(8,128)(2,1)}, bf16[56,32,128]{2,1,0:T(8,128)(2,1)}, u32[]{:S(2)}, u32[]{:S(2)}) collective-permute-start(bf16[56,32,128]{2,1,0:T(8,128)(2,1)} %get-tuple-element.64.refs_0_), channel_id=1, source_target_pairs={{0,96},{32,0},{64,32},{96,64},{1,97},{33,1},{65,33},{97,65},{2,98}... | collective-permute-start | bytes 1376264 | tf_op jit(solution)/shard_map/ppermute | solution.py:452
  82.3 20.7 %collective-permute-start.14 = (bf16[54,32,128]{2,1,0:T(8,128)(2,1)}, bf16[54,32,128]{2,1,0:T(8,128)(2,1)}, u32[]{:S(2)}, u32[]{:S(2)}) collective-permute-start(bf16[54,32,128]{2,1,0:T(8,128)(2,1)} %get-tuple-element.66.refs_0_), channel_id=1, source_target_pairs={{0,96},{32,0},{64,32},{96,64},{1,97},{33,1},{65,33},{97,65},{2,98}... | collective-permute-start | bytes 1327112 | tf_op jit(solution)/shard_map/ppermute | solution.py:452
  82.7 24.1 %collective-permute-start.17 = (bf16[54,32,128]{2,1,0:T(8,128)(2,1)}, bf16[54,32,128]{2,1,0:T(8,128)(2,1)}, u32[]{:S(2)}, u32[]{:S(2)}) collective-permute-start(bf16[54,32,128]{2,1,0:T(8,128)(2,1)} %get-tuple-element.67.refs_1_), channel_id=1, source_target_pairs={{0,32},{32,64},{64,96},{96,0},{1,33},{33,65},{65,97},{97,1},{2,34}... | collective-permute-start | bytes 1327112 | tf_op jit(solution)/shard_map/ppermute | solution.py:448
  84.3 22.4 %collective-permute-start.15 = (bf16[54,32,128]{2,1,0:T(8,128)(2,1)}, bf16[54,32,128]{2,1,0:T(8,128)(2,1)}, u32[]{:S(2)}, u32[]{:S(2)}) collective-permute-start(bf16[54,32,128]{2,1,0:T(8,128)(2,1)} %copy-done.1), channel_id=1, source_target_pairs={{0,32},{32,64},{64,96},{96,0},{1,33},{33,65},{65,97},{97,1},{2,34}... | collective-permute-start | bytes 1327112 | tf_op jit(solution)/shard_map/ppermute | solution.py:448
  84.4 28.1 %collective-permute-start.16 = (bf16[54,32,128]{2,1,0:T(8,128)(2,1)}, bf16[54,32,128]{2,1,0:T(8,128)(2,1)}, u32[]{:S(2)}, u32[]{:S(2)}) collective-permute-start(bf16[54,32,128]{2,1,0:T(8,128)(2,1)} %copy-done.2), channel_id=1, source_target_pairs={{0,96},{32,0},{64,32},{96,64},{1,97},{33,1},{65,33},{97,65},{2,98}... | collective-permute-start | bytes 1327112 | tf_op jit(solution)/shard_map/ppermute | solution.py:452
  103.0 16.8 %collective-permute-start.11 = (bf16[56,32,128]{2,1,0:T(8,128)(2,1)}, bf16[56,32,128]{2,1,0:T(8,128)(2,1)}, u32[]{:S(2)}, u32[]{:S(2)}) collective-permute-start(bf16[56,32,128]{2,1,0:T(8,128)(2,1)} %get-tuple-element.64.refs_0_), channel_id=1, source_target_pairs={{0,32},{32,64},{64,96},{96,0},{1,33},{33,65},{65,97},{97,1},{2,34}... | collective-permute-start | bytes 1376264 | tf_op jit(solution)/shard_map/ppermute | solution.py:448
  103.3 18.2 %collective-permute-start.10 = (bf16[56,32,128]{2,1,0:T(8,128)(2,1)}, bf16[56,32,128]{2,1,0:T(8,128)(2,1)}, u32[]{:S(2)}, u32[]{:S(2)}) collective-permute-start(bf16[56,32,128]{2,1,0:T(8,128)(2,1)} %collective-permute-done.9.refs_1_), channel_id=1, source_target_pairs={{0,96},{32,0},{64,32},{96,64},{1,97},{33,1},{65,33},{97,65},{2,98}... | collective-permute-start | bytes 1376264 | tf_op jit(solution)/shard_map/ppermute | solution.py:452
  112.5 6.6 %copy-start.4 = (f32[32,128]{1,0:T(8,128)S(1)}, f32[32,128]{1,0:T(8,128)}, u32[]{:S(2)}) copy-start(f32[32,128]{1,0:T(8,128)} %get-tuple-element.72) | copy-start | bytes 49156

commit v6 on v5

--- a/solution.py
+++ b/solution.py
@@ -16,12 +16,13 @@
 TILE = 16
 SLOTS = WRITERS * CAP
 VMEM = 60 * 1024 * 1024
+HBM = pl.BlockSpec(memory_space=pltpu.HBM)
 
 WHOLE = 3
 BY_ROWS_MOMENT = CAP
 BY_ROWS_WEIGHT = CAP - WHOLE
-USUAL = ((54, 54), (56,))
-FULL = ((132, 132), (168,))
+USUAL = ((54, 54), (28, 28))
+FULL = ((132, 132), (84, 84))
 
 
 def clear(ref, length, value):
@@ -38,8 +39,8 @@
     return top.astype(jnp.bfloat16).astype(jnp.float32)
 
 
-def row_quarter(replica):
-    return pl.ds(pl.multiple_of(replica[0] * ROWS, ROWS), ROWS)
+def row_quarter():
+    return pl.ds(pl.multiple_of(lax.axis_index("replica") * ROWS, ROWS), ROWS)
 
 
 def payload_rows(by_rows):
@@ -54,8 +55,10 @@
     return pl.ds(pl.multiple_of(writer * payload_rows(by_rows) + k * ROWS, TILE), ROWS)
 
 
-def moment_kernel(replica, writer, weight_mask, moment_mask, moment, payload, held, sems, tiles, totals, count):
-    rows = row_quarter(replica)
+def moment_kernel(
+    writer_in, weight_mask_in, moment_mask_in, moment, payload, held, sems, tiles, totals, count, writer, weight_mask, moment_mask, scalar_sems
+):
+    rows = row_quarter()
     lane = lax.broadcasted_iota(jnp.int32, (8, 128), 1)
     line = lax.broadcasted_iota(jnp.int32, (8, 128), 0)
     steps = held.shape[0] // GROUP_MOMENT
@@ -64,11 +67,17 @@
         part = pl.ds(step * GROUP_MOMENT, GROUP_MOMENT)
         return pltpu.make_async_copy(moment.at[part], held.at[part], sems.at[step])
 
+    scalars = ((writer_in, writer), (weight_mask_in, weight_mask), (moment_mask_in, moment_mask))
+    scalars = [pltpu.make_async_copy(source, there, scalar_sems.at[i]) for i, (source, there) in enumerate(scalars)]
+    for copy in scalars:
+        copy.start()
     for step in range(steps):
         fetch(step).start()
     clear(count, WRITERS, 0)
     tiles[...] = jnp.zeros(tiles.shape, tiles.dtype)
     totals[...] = jnp.zeros(totals.shape, totals.dtype)
+    for copy in scalars:
+        copy.wait()
 
     def one_step(step, carry):
         fetch(step).wait()
@@ -101,7 +110,7 @@
     lax.fori_loop(0, WRITERS, one, 0, unroll=4)
 
 
-def weight_kernel(blocks, replica, writer, weight_mask, base_scale, weight, codes, payload, whole, refreshed, coded, scales, slot_of, kept_of, count, count_kept):
+def weight_kernel(blocks, writer, weight_mask, base_scale, weight, codes, payload, whole, refreshed, coded, scales, slot_of, kept_of, count, count_kept):
     step = pl.program_id(0)
 
     @pl.when(step == 0)
@@ -133,7 +142,7 @@
 
     @pl.when(step == blocks // GROUP - 1)
     def _():
-        rows = row_quarter(replica)
+        rows = row_quarter()
         lane = lax.broadcasted_iota(jnp.int32, (TILE, 128), 1)
 
         def one(w, carry):
@@ -160,31 +169,30 @@
     return pltpu.CompilerParams(dimension_semantics=("arbitrary",), vmem_limit_bytes=VMEM)
 
 
-def moment_call(replica, writer, weight_mask, moment_mask, moment):
+def moment_call(writer, weight_mask, moment_mask, moment):
     blocks, width = moment.shape[0], moment.shape[1]
     shape = (WRITERS * payload_rows(BY_ROWS_MOMENT), width)
     return pl.pallas_call(
         moment_kernel,
-        grid_spec=pltpu.PrefetchScalarGridSpec(
-            num_scalar_prefetch=4,
-            grid=(1,),
-            in_specs=[pl.BlockSpec(memory_space=pl.ANY)],
-            out_specs=pl.BlockSpec(shape, lambda i, *_: (0, 0)),
-            scratch_shapes=[
-                pltpu.VMEM(moment.shape, jnp.float32),
-                pltpu.SemaphoreType.DMA((blocks // GROUP_MOMENT,)),
-                pltpu.VMEM((WRITERS, 8, 128), jnp.float32),
-                pltpu.VMEM((8, 128), jnp.float32),
-                pltpu.SMEM((WRITERS,), jnp.int32),
-            ],
-        ),
+        in_specs=[HBM] * 4,
         out_shape=jax.ShapeDtypeStruct(shape, jnp.bfloat16),
-        compiler_params=params(),
+        scratch_shapes=[
+            pltpu.VMEM(moment.shape, jnp.float32),
+            pltpu.SemaphoreType.DMA((blocks // GROUP_MOMENT,)),
+            pltpu.VMEM((WRITERS, 8, 128), jnp.float32),
+            pltpu.VMEM((8, 128), jnp.float32),
+            pltpu.SMEM((WRITERS,), jnp.int32),
+            pltpu.SMEM((blocks,), jnp.int32),
+            pltpu.SMEM((blocks,), jnp.int32),
+            pltpu.SMEM((blocks,), jnp.int32),
+            pltpu.SemaphoreType.DMA((3,)),
+        ],
+        compiler_params=pltpu.CompilerParams(vmem_limit_bytes=VMEM),
         cost_estimate=cost(10 << 20, 12 << 20),
-    )(replica, writer, weight_mask, moment_mask, moment)
-
-
-def weight_call(replica, writer, weight_mask, base_scale, weight, codes):
+    )(writer, weight_mask, moment_mask, moment)
+
+
+def weight_call(writer, weight_mask, base_scale, weight, codes):
     blocks, width = weight.shape[0], weight.shape[1]
     moving = pl.BlockSpec((GROUP, width, width), lambda i, *_: (i, 0, 0))
     payload = (WRITERS * payload_rows(BY_ROWS_WEIGHT), width)
@@ -192,7 +200,7 @@
     return pl.pallas_call(
         functools.partial(weight_kernel, blocks),
         grid_spec=pltpu.PrefetchScalarGridSpec(
-            num_scalar_prefetch=4,
+            num_scalar_prefetch=3,
             grid=(blocks // GROUP,),
             in_specs=[moving, moving],
             out_specs=[pl.BlockSpec(payload, lambda i, *_: (0, 0)), pl.BlockSpec(whole, lambda i, *_: (0, 0, 0)), moving],
@@ -212,10 +220,9 @@
         ],
         compiler_params=params(),
         cost_estimate=cost(20 << 20, 28 << 20),
-    )(replica, writer, weight_mask, base_scale, weight, codes)
-
-
-HBM = pl.BlockSpec(memory_space=pltpu.HBM)
+    )(writer, weight_mask, base_scale, weight, codes)
+
+
 SOURCES = 8
 
 
@@ -288,7 +295,7 @@
     flags = jax.ShapeDtypeStruct((WRITERS, width), jnp.int32)
     return pl.pallas_call(
         pack_moment_kernel,
-        in_specs=[pl.BlockSpec(memory_space=pltpu.SMEM), HBM],
+        in_specs=[HBM, HBM],
         out_shape=[
             *parts,
             flags,
@@ -310,8 +317,10 @@
     )(ticket, payload.reshape(WRITERS, -1, width))
 
 
-def pack_weight_kernel(kept, payload, *refs):
-    *own, scales, held, packed, sems = refs
+def pack_weight_kernel(kept_in, payload, *refs):
+    *own, scales, held, packed, sems, kept, kept_sem = refs
+    copy = pltpu.make_async_copy(kept_in, kept, kept_sem)
+    copy.start()
 
     def advance(s):
         found = functools.reduce(jnp.add, [kept[s, k] for k in range(CAP)])
@@ -319,6 +328,7 @@
 
     steps = pack(BY_ROWS_WEIGHT, payload, held, packed, sems, advance)
     next(steps)
+    copy.wait()
     next(steps)
     share(packed, own)
     scales[...] = held[:, pl.ds(BY_ROWS_WEIGHT * ROWS, TILE), :].astype(jnp.float32)[:, 0, :]
@@ -329,19 +339,16 @@
     parts = [jax.ShapeDtypeStruct((size, ROWS, width), jnp.bfloat16) for size in capacity]
     return pl.pallas_call(
         pack_weight_kernel,
-        grid_spec=pltpu.PrefetchScalarGridSpec(
-            num_scalar_prefetch=1,
-            grid=(1,),
-            in_specs=[HBM],
-            out_specs=[pl.BlockSpec(part.shape, lambda i, *_: (0, 0, 0)) for part in parts] + [pl.BlockSpec((WRITERS, width), lambda i, *_: (0, 0))],
-            scratch_shapes=[
-                pltpu.VMEM((WRITERS, payload_rows(BY_ROWS_WEIGHT), width), jnp.bfloat16),
-                pltpu.VMEM((sum(capacity), ROWS, width), jnp.bfloat16),
-                pltpu.SemaphoreType.DMA((WRITERS // SOURCES,)),
-            ],
-        ),
+        in_specs=[HBM, HBM],
         out_shape=[*parts, jax.ShapeDtypeStruct((WRITERS, width), jnp.float32)],
-        compiler_params=params(),
+        scratch_shapes=[
+            pltpu.VMEM((WRITERS, payload_rows(BY_ROWS_WEIGHT), width), jnp.bfloat16),
+            pltpu.VMEM((sum(capacity), ROWS, width), jnp.bfloat16),
+            pltpu.SemaphoreType.DMA((WRITERS // SOURCES,)),
+            pltpu.SMEM(kept.shape, jnp.int32),
+            pltpu.SemaphoreType.DMA,
+        ],
+        compiler_params=pltpu.CompilerParams(vmem_limit_bytes=VMEM),
         cost_estimate=cost(0, 0),
     )(kept, payload.reshape(WRITERS, -1, width))
 
@@ -361,11 +368,14 @@
     )(values, *earlier)
 
 
-def unpack_kernel(n_whole, sizes, replica, kept, *refs):
-    out, held, built, sems, out_sems = refs[-5:]
+def unpack_kernel(n_whole, sizes, kept_in, *refs):
+    out, held, built, sems, out_sems, kept, kept_sem = refs[-7:]
+    replica = lax.axis_index("replica")
+    copy_kept = pltpu.make_async_copy(kept_in, kept, kept_sem)
+    copy_kept.start()
     nothing = sum(sizes[0])
     first_whole = nothing + 1
-    rows = [pl.ds(pl.multiple_of(lax.rem(replica[0] + turn, 4) * ROWS, ROWS), ROWS) for turn in range(4)]
+    rows = [pl.ds(pl.multiple_of(lax.rem(replica + turn, 4) * ROWS, ROWS), ROWS) for turn in range(4)]
     copies = []
     for turn in range(4):
         start = 0
@@ -373,15 +383,22 @@
             i = len(copies)
             copies.append(pltpu.make_async_copy(refs[i], held.at[turn, pl.ds(start, size)], sems.at[i]))
             start += size
-    if n_whole:
-        whole = refs[len(copies)]
-        for turn in range(4):
-            there = held.at[turn, pl.ds(first_whole, WRITERS * n_whole)]
-            copies.append(pltpu.make_async_copy(whole.at[:, rows[turn], :], there, sems.at[len(copies)]))
+    whole = refs[len(copies)] if n_whole else None
+
+    def fetch_whole(step, turn):
+        size = SOURCES * n_whole
+        there = held.at[turn, pl.ds(first_whole + step * size, size)]
+        return pltpu.make_async_copy(whole.at[pl.ds(step * size, size), rows[turn], :], there, sems.at[len(copies) + 4 * step + turn])
+
     for copy in copies:
         copy.start()
+    if n_whole:
+        for step in range(WRITERS // SOURCES):
+            for turn in range(4):
+                fetch_whole(step, turn).start()
     for turn in range(4):
         held[turn, nothing] = jnp.zeros(held.shape[2:], held.dtype)
+    copy_kept.wait()
     for copy in copies:
         copy.wait()
 
@@ -390,6 +407,9 @@
         return pltpu.make_async_copy(built.at[part], out.at[part], out_sems.at[step])
 
     def one(step, place):
+        if n_whole:
+            for turn in range(4):
+                fetch_whole(step, turn).wait()
         for s in range(SOURCES):
             source = step * SOURCES + s
             rank = 0
@@ -415,29 +435,27 @@
         send(step).wait()
 
 
-def unpack(replica, kept, parts, whole=None):
+def unpack(kept, parts, whole=None):
     sizes = [[piece.shape[0] for piece in part] for part in parts]
     operands = [piece for part in parts for piece in part] + ([] if whole is None else [whole])
     n_whole = 0 if whole is None else WHOLE
     width = operands[0].shape[-1]
     return pl.pallas_call(
         functools.partial(unpack_kernel, n_whole, sizes),
-        grid_spec=pltpu.PrefetchScalarGridSpec(
-            num_scalar_prefetch=2,
-            grid=(1,),
-            in_specs=[HBM] * len(operands),
-            out_specs=HBM,
-            scratch_shapes=[
-                pltpu.VMEM((4, sum(sizes[0]) + 1 + WRITERS * n_whole, ROWS, width), jnp.bfloat16),
-                pltpu.VMEM((SLOTS, width, width), jnp.bfloat16),
-                pltpu.SemaphoreType.DMA((len(operands) + 4,)),
-                pltpu.SemaphoreType.DMA((WRITERS // SOURCES,)),
-            ],
-        ),
+        in_specs=[HBM] * (1 + len(operands)),
+        out_specs=HBM,
         out_shape=jax.ShapeDtypeStruct((SLOTS, width, width), jnp.bfloat16),
-        compiler_params=params(),
+        scratch_shapes=[
+            pltpu.VMEM((4, sum(sizes[0]) + 1 + WRITERS * n_whole, ROWS, width), jnp.bfloat16),
+            pltpu.VMEM((SLOTS, width, width), jnp.bfloat16),
+            pltpu.SemaphoreType.DMA((len(operands) + 4 * (WRITERS // SOURCES),)),
+            pltpu.SemaphoreType.DMA((WRITERS // SOURCES,)),
+            pltpu.SMEM(kept.shape, jnp.int32),
+            pltpu.SemaphoreType.DMA,
+        ],
+        compiler_params=pltpu.CompilerParams(vmem_limit_bytes=VMEM),
         cost_estimate=cost(0, 0),
-    )(replica, kept, *operands)
+    )(kept, *operands)
 
 
 def regroup(values):
@@ -458,38 +476,38 @@
     return (first_up, second_down), ((first, second), (first_down, second_down), (upward(first_up), downward(second_down)), (first_up, second_up))
 
 
-def along_z_down(own):
-    up, down = upward(own), downward(own)
-    return ((own,), (down,), (downward(down),), (up,))
-
-
-def exchange_again(ticket, replica, m_payload, w_payload, w_whole):
+def along_z_in_turn(first, second):
+    near = (upward(first), downward(second), downward(first), upward(second))
+    first_up, second_down = after(near[0], near[2:]), after(near[1], near[2:])
+    return ((first, second), (near[2], second_down), (upward(first_up), downward(second_down)), (first_up, near[3]))
+
+
+def exchange_again(ticket, m_payload, w_payload, w_whole):
     *m_own, kept_w, kept_m, _, _ = pack_moment(FULL[0], ticket, m_payload)
-    written_moment = unpack(replica, kept_m, along_z(*m_own)[1])
+    written_moment = unpack(kept_m, along_z(*m_own)[1])
     *w_own, _ = pack_weight(FULL[1], kept_w, w_payload)
-    written_weight = unpack(replica, kept_w, along_z_down(*w_own), w_whole)
+    written_weight = unpack(kept_w, along_z(*w_own)[1], w_whole)
     return written_weight, written_moment
 
 
 def on_device(weight, moment, base_codes, base_scale, weight_mask, moment_mask, writer):
     width = weight.shape[1]
     target = writer[:, 0]
-    replica = lax.axis_index("replica").astype(jnp.int32).reshape(1)
-    m_payload = regroup(moment_call(replica, target, weight_mask, moment_mask, moment))
-    w_payload, w_whole, refreshed = weight_call(replica, target, weight_mask, base_scale, weight, base_codes)
+    m_payload = regroup(moment_call(target, weight_mask, moment_mask, moment))
+    w_payload, w_whole, refreshed = weight_call(target, weight_mask, base_scale, weight, base_codes)
     w_payload = regroup(after(w_payload, (m_payload,)))
-    *m_own, kept_w, kept_m, totals, m_scales = pack_moment(USUAL[0], replica, m_payload)
+    *m_own, kept_w, kept_m, totals, m_scales = pack_moment(USUAL[0], jnp.zeros((1,), jnp.int32), m_payload)
     m_near, m_parts = along_z(*m_own)
     w_whole = regroup(after(w_whole, (w_payload, *m_near)))
     *w_own, w_scales = pack_weight(USUAL[1], kept_w, w_payload)
-    w_parts = along_z_down(*w_own)
-    written_moment = unpack(replica, kept_m, m_parts)
-    written_weight = unpack(replica, kept_w, w_parts, w_whole)
+    w_parts = along_z_in_turn(*w_own)
+    written_moment = unpack(kept_m, m_parts)
+    written_weight = unpack(kept_w, w_parts, w_whole)
 
     over = jnp.any(totals[:2, :WRITERS] >= jnp.array([[sum(USUAL[1])], [sum(USUAL[0])]], jnp.float32)).astype(jnp.int32)
     _, written_weight, written_moment = lax.while_loop(
         lambda carry: carry[0] < over,
-        lambda carry: (carry[0] + 1, *exchange_again(carry[0].reshape(1), replica, m_payload, w_payload, w_whole)),
+        lambda carry: (carry[0] + 1, *exchange_again(carry[0].reshape(1), m_payload, w_payload, w_whole)),
         (jnp.int32(0), written_weight, written_moment),
     )
     written_scales = jnp.stack([w_scales[:, :CAP], m_scales[:, :CAP]], axis=0).astype(jnp.bfloat16)

time: 129 us -> 126 us (0.977)
  Pallas kernels: 42.5 us -> 39.6 us
  starting transfers between devices: 39.2 us -> 40.5 us
  waiting for transfers between devices: 42 us -> 40.7 us
    ppermute x5 -> x6, waiting for transfers between devices: 20.7 us -> 5.21 us  [downward(): return lax.ppermute(values, 'replica', [(i, (i - 1) % 4) for i in range(4)])]
    ppermute x4 -> x6, waiting for transfers between devices: 10.6 us -> 24.8 us  [upward(): return lax.ppermute(values, 'replica', [(i, (i + 1) % 4) for i in range(4)])]
    pallas_call x5, Pallas kernels: 25.1 us -> 22.1 us  [the longest x2 11.1 us: unpack(): pl.pallas_call(functools.partial(unpack_kernel, n_whole, sizes), in_specs...]
    ppermute x5 -> x6, starting transfers between devices: 12.5 us -> 13.7 us  [downward(): return lax.ppermute(values, 'replica', [(i, (i - 1) % 4) for i in range(4)])]
    ppermute x4 -> x6, starting transfers between devices: 3.97 us -> 4.05 us  [upward(): return lax.ppermute(values, 'replica', [(i, (i + 1) % 4) for i in range(4)])]
  transfers between devices with their start and end apart: 12 -> 15, of which waited for: 6 -> 8; matrix products, arithmetic and copies ran while one was open for 2% -> 2% of each run, Pallas kernels for 24% -> 23%
where the time goes in v6:
time: 126 us; the launch traced here: 125 us
  waiting for transfers between devices  40.7 us (32%)
  starting transfers between devices  40.5 us (32%)
  Pallas kernels  39.6 us (31%)
  other arithmetic  2.08 us (2%)
  between operations  1.63 us (1%)
    ppermute x6, waiting for transfers between devices, upward(): return lax.ppermute(values, 'replica', [(i, (i + 1) % 4) for i in range(4)])  24.8 us
    all_to_all x3, starting transfers between devices, regroup(): lax.all_to_all(values, 'fsdp', split_axis=0, concat_axis=0, tiled=True)  22.8 us
    pallas_call x1, Pallas kernels, weight_call(): pl.pallas_call(functools.partial(weight_kernel, blocks), grid_spec=pltpu....  17.4 us
    ppermute x6, starting transfers between devices, downward(): return lax.ppermute(values, 'replica', [(i, (i - 1) % 4) for i in range(4)])  13.7 us
    pallas_call x2, Pallas kernels, unpack(): pl.pallas_call(functools.partial(unpack_kernel, n_whole, sizes), in_specs...  11.1 us
    all_to_all x3, waiting for transfers between devices, regroup(): lax.all_to_all(values, 'fsdp', split_axis=0, concat_axis=0, tiled=True)  10.6 us
    ppermute x6, waiting for transfers between devices, downward(): return lax.ppermute(values, 'replica', [(i, (i - 1) % 4) for i in range(4)])  5.21 us
    pallas_call x1, Pallas kernels, moment_call(): pl.pallas_call(moment_kernel, in_specs=[HBM] * 4, out_shape=jax.ShapeDtyp...  5.11 us
  transfers between devices with their start and end apart: 15, of which 8 were waited for; matrix products, arithmetic and copies ran while one was open for 2% of the time, Pallas kernels for 23%

profile of v6, /device:TPU:2, one launch (start us, length us, event | category | flops | bytes accessed | tf_op | source)
XLA Modules:
  0.0 125.4 jit_solution(5814669485498659665)
XLA Ops:
  0.6 5.1 %shard_map.111 = bf16[8704,128]{1,0:T(8,128)(2,1)} custom-call(s32[128]{0:T(128)} %bitcast.27, s32[128]{0:T(128)} %weight_mask.1, s32[128]{0:T(128)} %moment_mask_in.1, f32[128,128,128]{2,1,0:T(8,128)} %moment.1), custom_call_target="tpu_custom_call" | custom-call | flops 10485760 | bytes 12582912 | tf_op jit(solution)/shard_map/pallas_call | solution.py:175
  5.7 7.6 %all-to-all-start = ((bf16[32,272,128]{2,1,0:T(8,128)(2,1)}), bf16[32,272,128]{2,1,0:T(8,128)(2,1)S(1)}, u32[]{:S(2)}, u32[]{:S(2)}) async-start(bf16[32,272,128]{2,1,0:T(8,128)(2,1)} %bitcast.23), calls=%async_computation | async-start | bytes 4456448 | tf_op jit(solution)/shard_map/all_to_all | solution.py:462
  13.4 17.4 %shard_map.113 = (bf16[5632,128]{1,0:T(8,128)(2,1)}, bf16[96,128,128]{2,1,0:T(8,128)(2,1)}, bf16[128,128,128]{2,1,0:T(8,128)(2,1)}) custom-call(s32[128]{0:T(128)} %bitcast.28, s32[128]{0:T(128)} %weight_mask.1, f32[128]{0:T(128)} %base_scale.1, f32[128,128,128]{2,1,0:T(8,128)} %weight.1, s32[128,128,128]{2,1,0:T(8,128)} %codes.1), custom_call_target="tpu_custom_call" | custom-call | flops 20971520 | bytes 29360128 | tf_op jit(solution)/shard_map/pallas_call | solution.py:200
  30.8 9.9 %all-to-all-done.payload = bf16[32,272,128]{2,1,0:T(8,128)(2,1)S(1)} async-done(((bf16[32,272,128]{2,1,0:T(8,128)(2,1)}), bf16[32,272,128]{2,1,0:T(8,128)(2,1)S(1)}, u32[]{:S(2)}, u32[]{:S(2)}) %all-to-all-start) | async-done | bytes 2228256 | tf_op jit(solution)/shard_map/all_to_all | solution.py:462
  40.8 7.6 %all-to-all-start.1 = ((bf16[32,176,128]{2,1,0:T(8,128)(2,1)}), bf16[32,176,128]{2,1,0:T(8,128)(2,1)}, u32[]{:S(2)}, u32[]{:S(2)}) async-start(bf16[32,176,128]{2,1,0:T(8,128)(2,1)} %bitcast.26), calls=%async_computation.1 | async-start | bytes 2883584 | tf_op jit(solution)/shard_map/all_to_all | solution.py:462
  48.3 3.3 %shard_map.112 = (bf16[54,32,128]{2,1,0:T(8,128)(2,1)}, bf16[54,32,128]{2,1,0:T(8,128)(2,1)}, s32[32,128]{1,0:T(8,128)}, s32[32,128]{1,0:T(8,128)}, f32[8,128]{1,0:T(8,128)}, /*index=5*/f32[32,128]{1,0:T(8,128)}) custom-call(s32[1]{0:T(128)} %constant.3.clone.1.ticket, bf16[32,272,128]{2,1,0:T(8,128)(2,1)S(1)} %all-to-all-done.payload), custom_call_target="tpu_custom_call" | custom-call | tf_op jit(solution)/shard_map/pallas_call | solution.py:296
  51.6 2.0 %collective-permute-start.18 = (bf16[54,32,128]{2,1,0:T(8,128)(2,1)}, bf16[54,32,128]{2,1,0:T(8,128)(2,1)S(1)}, u32[]{:S(2)}, u32[]{:S(2)}) collective-permute-start(bf16[54,32,128]{2,1,0:T(8,128)(2,1)} %get-tuple-element.64.refs_0_), channel_id=1, source_target_pairs={{0,32},{32,64},{64,96},{96,0},{1,33},{33,65},{65,97},{97,1},{2,34}... | collective-permute-start | bytes 1327112 | tf_op jit(solution)/shard_map/ppermute | solution.py:466
  53.6 2.2 %collective-permute-start.19 = (bf16[54,32,128]{2,1,0:T(8,128)(2,1)}, bf16[54,32,128]{2,1,0:T(8,128)(2,1)S(1)}, u32[]{:S(2)}, u32[]{:S(2)}) collective-permute-start(bf16[54,32,128]{2,1,0:T(8,128)(2,1)} %get-tuple-element.65.refs_1_), channel_id=1, source_target_pairs={{0,96},{32,0},{64,32},{96,64},{1,97},{33,1},{65,33},{97,65},{2,98}... | collective-permute-start | bytes 1327112 | tf_op jit(solution)/shard_map/ppermute | solution.py:470
  55.8 10.6 %collective-permute-done.18.refs_2_.refs_6_ = bf16[54,32,128]{2,1,0:T(8,128)(2,1)S(1)} collective-permute-done((bf16[54,32,128]{2,1,0:T(8,128)(2,1)}, bf16[54,32,128]{2,1,0:T(8,128)(2,1)S(1)}, u32[]{:S(2)}, u32[]{:S(2)}) %collective-permute-start.18) | collective-permute-done | bytes 442400 | tf_op jit(solution)/shard_map/ppermute | solution.py:466
  66.4 0.7 all-to-all-done.1.payload
  67.2 0.1 copy-done.7
  67.3 7.6 %all-to-all-start.2 = ((bf16[96,128,128]{2,1,0:T(8,128)(2,1)}), bf16[96,128,128]{2,1,0:T(8,128)(2,1)S(1)}, u32[]{:S(2)}, u32[]{:S(2)}) async-start(bf16[96,128,128]{2,1,0:T(8,128)(2,1)} %shard_map.118), calls=%async_computation.2 | async-start | bytes 6291456 | tf_op jit(solution)/shard_map/all_to_all | solution.py:462
  74.9 3.3 %collective-permute-start.20 = (bf16[54,32,128]{2,1,0:T(8,128)(2,1)}, bf16[54,32,128]{2,1,0:T(8,128)(2,1)}, u32[]{:S(2)}, u32[]{:S(2)}) collective-permute-start(bf16[54,32,128]{2,1,0:T(8,128)(2,1)} %get-tuple-element.64.refs_0_), channel_id=1, source_target_pairs={{0,96},{32,0},{64,32},{96,64},{1,97},{33,1},{65,33},{97,65},{2,98}... | collective-permute-start | bytes 1327112 | tf_op jit(solution)/shard_map/ppermute | solution.py:470
  78.2 3.3 %collective-permute-start.22 = (bf16[54,32,128]{2,1,0:T(8,128)(2,1)}, bf16[54,32,128]{2,1,0:T(8,128)(2,1)}, u32[]{:S(2)}, u32[]{:S(2)}) collective-permute-start(bf16[54,32,128]{2,1,0:T(8,128)(2,1)} %copy-done.7), channel_id=1, source_target_pairs={{0,96},{32,0},{64,32},{96,64},{1,97},{33,1},{65,33},{97,65},{2,98}... | collective-permute-start | bytes 1327112 | tf_op jit(solution)/shard_map/ppermute | solution.py:470
  81.5 2.7 %shard_map.115 = (bf16[28,32,128]{2,1,0:T(8,128)(2,1)}, bf16[28,32,128]{2,1,0:T(8,128)(2,1)}, f32[32,128]{1,0:T(8,128)}) custom-call(s32[32,128]{1,0:T(8,128)} %get-tuple-element.59.kept_in, bf16[32,176,128]{2,1,0:T(8,128)(2,1)} %all-to-all-done.1.payload), custom_call_target="tpu_custom_call" | custom-call | tf_op jit(solution)/shard_map/pallas_call | solution.py:340
  84.2 0.1 collective-permute-start.15
  84.3 4.8 %collective-permute-done.20.refs_2_ = bf16[54,32,128]{2,1,0:T(8,128)(2,1)} collective-permute-done((bf16[54,32,128]{2,1,0:T(8,128)(2,1)}, bf16[54,32,128]{2,1,0:T(8,128)(2,1)}, u32[]{:S(2)}, u32[]{:S(2)}) %collective-permute-start.20) | collective-permute-done | bytes 442400 | tf_op jit(solution)/shard_map/ppermute | solution.py:470
  89.1 3.7 %collective-permute-start.12 = (bf16[28,32,128]{2,1,0:T(8,128)(2,1)}, bf16[28,32,128]{2,1,0:T(8,128)(2,1)S(1)}, u32[]{:S(2)}, u32[]{:S(2)}) collective-permute-start(bf16[28,32,128]{2,1,0:T(8,128)(2,1)} %get-tuple-element.61.refs_0_), channel_id=1, source_target_pairs={{0,96},{32,0},{64,32},{96,64},{1,97},{33,1},{65,33},{97,65},{2,98}... | collective-permute-start | bytes 688136 | tf_op jit(solution)/shard_map/ppermute | solution.py:470
  92.8 9.5 %collective-permute-done.21.refs_4_ = bf16[54,32,128]{2,1,0:T(8,128)(2,1)} collective-permute-done((bf16[54,32,128]{2,1,0:T(8,128)(2,1)}, bf16[54,32,128]{2,1,0:T(8,128)(2,1)}, u32[]{:S(2)}, u32[]{:S(2)}) %collective-permute-start.21) | collective-permute-done | bytes 442400 | tf_op jit(solution)/shard_map/ppermute | solution.py:466
  102.3 1.5 %compare_reduce_fusion = pred[]{:T(512)} fusion(f32[8,128]{1,0:T(8,128)} %get-tuple-element.67, f32[2]{0:T(128)S(1)} %copy-done.11), kind=kLoop, calls=%fused_computation.5 | loop fusion | flops 127 | bytes 265 | tf_op jit(solution)/shard_map/reduce_or | solution.py:507
  104.5 0.1 copy.18
  104.6 5.7 %shard_map.120 = bf16[256,128,128]{2,1,0:T(8,128)(2,1)} custom-call(s32[32,128]{1,0:T(8,128)} %get-tuple-element.66.kept_in, bf16[54,32,128]{2,1,0:T(8,128)(2,1)} %get-tuple-element.64.refs_0_, bf16[54,32,128]{2,1,0:T(8,128)(2,1)} %get-tuple-element.65.refs_1_, bf16[54,32,128]{2,1,0:T(8,128)(2,1)} %collective-permute-done.20.refs_2_, ...), custom_call_target="tpu_custom_call" | custom-call | tf_op jit(solution)/shard_map/pallas_call | solution.py:443
  110.3 0.7 collective-permute-done.14.refs_2_.refs_7_
  111.0 2.0 %collective-permute-start.16 = (bf16[28,32,128]{2,1,0:T(8,128)(2,1)}, bf16[28,32,128]{2,1,0:T(8,128)(2,1)S(1)}, u32[]{:S(2)}, u32[]{:S(2)}) collective-permute-start(bf16[28,32,128]{2,1,0:T(8,128)(2,1)} %shard_map.117.refs_6_), channel_id=1, source_target_pairs={{0,32},{32,64},{64,96},{96,0},{1,33},{33,65},{65,97},{97,1},{2,34}... | collective-permute-start | bytes 688136 | tf_op jit(solution)/shard_map/ppermute | solution.py:466
  113.0 1.3 collective-permute-start.17
  114.3 0.1 copy.17
  114.3 0.6 pad_maximum_fusion
  114.9 4.0 %collective-permute-done.16.refs_4_ = bf16[28,32,128]{2,1,0:T(8,128)(2,1)S(1)} collective-permute-done((bf16[28,32,128]{2,1,0:T(8,128)(2,1)}, bf16[28,32,128]{2,1,0:T(8,128)(2,1)S(1)}, u32[]{:S(2)}, u32[]{:S(2)}) %collective-permute-start.16) | collective-permute-done | bytes 229408 | tf_op jit(solution)/shard_map/ppermute | solution.py:466
  118.9 0.4 collective-permute-done.17.refs_5_
  119.3 0.3 copy-done.8
  119.6 5.4 %shard_map.119 = bf16[256,128,128]{2,1,0:T(8,128)(2,1)} custom-call(s32[32,128]{1,0:T(8,128)} %get-tuple-element.59.kept_in, bf16[28,32,128]{2,1,0:T(8,128)(2,1)} %get-tuple-element.61.refs_0_, bf16[28,32,128]{2,1,0:T(8,128)(2,1)} %get-tuple-element.62.refs_1_, bf16[28,32,128]{2,1,0:T(8,128)(2,1)} %copy-done.5, bf16[28,32,128]{2,1,0:T(8,128)(2,1)} %shard_map.116.refs_3_, ...), custom_call_target="tpu_custom_call" | custom-call | tf_op jit(solution)/shard_map/pallas_call | solution.py:443
  125.0 0.2 while.12
  (31 shorter events, 0.1 us)
Async XLA Ops:
  5.7 35.0 %all-to-all-start = ((bf16[32,272,128]{2,1,0:T(8,128)(2,1)}), bf16[32,272,128]{2,1,0:T(8,128)(2,1)S(1)}, u32[]{:S(2)}, u32[]{:S(2)}) async-start(bf16[32,272,128]{2,1,0:T(8,128)(2,1)} %bitcast.23), calls=%async_computation | async-start | bytes 4456448 | tf_op jit(solution)/shard_map/all_to_all | solution.py:462
  40.8 7.6 %copy-start = (bf16[32,272,128]{2,1,0:T(8,128)(2,1)}, bf16[32,272,128]{2,1,0:T(8,128)(2,1)S(1)}, u32[]{:S(2)}) copy-start(bf16[32,272,128]{2,1,0:T(8,128)(2,1)S(1)} %all-to-all-done.payload) | copy-start | bytes 6684676
  40.8 26.4 %all-to-all-start.1 = ((bf16[32,176,128]{2,1,0:T(8,128)(2,1)}), bf16[32,176,128]{2,1,0:T(8,128)(2,1)}, u32[]{:S(2)}, u32[]{:S(2)}) async-start(bf16[32,176,128]{2,1,0:T(8,128)(2,1)} %bitcast.26), calls=%async_computation.1 | async-start | bytes 2883584 | tf_op jit(solution)/shard_map/all_to_all | solution.py:462
  51.6 14.8 %collective-permute-start.18 = (bf16[54,32,128]{2,1,0:T(8,128)(2,1)}, bf16[54,32,128]{2,1,0:T(8,128)(2,1)S(1)}, u32[]{:S(2)}, u32[]{:S(2)}) collective-permute-start(bf16[54,32,128]{2,1,0:T(8,128)(2,1)} %get-tuple-element.64.refs_0_), channel_id=1, source_target_pairs={{0,32},{32,64},{64,96},{96,0},{1,33},{33,65},{65,97},{97,1},{2,34}... | collective-permute-start | bytes 1327112 | tf_op jit(solution)/shard_map/ppermute | solution.py:466
  53.6 12.8 %collective-permute-start.19 = (bf16[54,32,128]{2,1,0:T(8,128)(2,1)}, bf16[54,32,128]{2,1,0:T(8,128)(2,1)S(1)}, u32[]{:S(2)}, u32[]{:S(2)}) collective-permute-start(bf16[54,32,128]{2,1,0:T(8,128)(2,1)} %get-tuple-element.65.refs_1_), channel_id=1, source_target_pairs={{0,96},{32,0},{64,32},{96,64},{1,97},{33,1},{65,33},{97,65},{2,98}... | collective-permute-start | bytes 1327112 | tf_op jit(solution)/shard_map/ppermute | solution.py:470
  66.4 0.8 copy-start.6
  66.4 0.9 copy-start.7
  67.3 35.0 %copy-start.11 = (f32[2]{0:T(128)S(1)}, f32[2]{0:T(128)}, u32[]{:S(2)}) copy-start(f32[2]{0:T(128)} %constant.11) | copy-start | bytes 28
  67.3 37.1 %copy-start.9 = (f32[32,128]{1,0:T(8,128)S(1)}, f32[32,128]{1,0:T(8,128)}, u32[]{:S(2)}) copy-start(f32[32,128]{1,0:T(8,128)} %get-tuple-element.71) | copy-start | bytes 49156
  67.3 52.0 %all-to-all-start.2 = ((bf16[96,128,128]{2,1,0:T(8,128)(2,1)}), bf16[96,128,128]{2,1,0:T(8,128)(2,1)S(1)}, u32[]{:S(2)}, u32[]{:S(2)}) async-start(bf16[96,128,128]{2,1,0:T(8,128)(2,1)} %shard_map.118), calls=%async_computation.2 | async-start | bytes 6291456 | tf_op jit(solution)/shard_map/all_to_all | solution.py:462
  74.9 14.1 %collective-permute-start.20 = (bf16[54,32,128]{2,1,0:T(8,128)(2,1)}, bf16[54,32,128]{2,1,0:T(8,128)(2,1)}, u32[]{:S(2)}, u32[]{:S(2)}) collective-permute-start(bf16[54,32,128]{2,1,0:T(8,128)(2,1)} %get-tuple-element.64.refs_0_), channel_id=1, source_target_pairs={{0,96},{32,0},{64,32},{96,64},{1,97},{33,1},{65,33},{97,65},{2,98}... | collective-permute-start | bytes 1327112 | tf_op jit(solution)/shard_map/ppermute | solution.py:470
  78.2 14.6 %collective-permute-start.23 = (bf16[54,32,128]{2,1,0:T(8,128)(2,1)}, bf16[54,32,128]{2,1,0:T(8,128)(2,1)}, u32[]{:S(2)}, u32[]{:S(2)}) collective-permute-start(bf16[54,32,128]{2,1,0:T(8,128)(2,1)} %get-tuple-element.65.refs_1_), channel_id=1, source_target_pairs={{0,32},{32,64},{64,96},{96,0},{1,33},{33,65},{65,97},{97,1},{2,34}... | collective-permute-start | bytes 1327112 | tf_op jit(solution)/shard_map/ppermute | solution.py:466
  78.2 24.1 %collective-permute-start.21 = (bf16[54,32,128]{2,1,0:T(8,128)(2,1)}, bf16[54,32,128]{2,1,0:T(8,128)(2,1)}, u32[]{:S(2)}, u32[]{:S(2)}) collective-permute-start(bf16[54,32,128]{2,1,0:T(8,128)(2,1)} %copy-done.6), channel_id=1, source_target_pairs={{0,32},{32,64},{64,96},{96,0},{1,33},{33,65},{65,97},{97,1},{2,34}... | collective-permute-start | bytes 1327112 | tf_op jit(solution)/shard_map/ppermute | solution.py:466
  78.2 26.3 %collective-permute-start.22 = (bf16[54,32,128]{2,1,0:T(8,128)(2,1)}, bf16[54,32,128]{2,1,0:T(8,128)(2,1)}, u32[]{:S(2)}, u32[]{:S(2)}) collective-permute-start(bf16[54,32,128]{2,1,0:T(8,128)(2,1)} %copy-done.7), channel_id=1, source_target_pairs={{0,96},{32,0},{64,32},{96,64},{1,97},{33,1},{65,33},{97,65},{2,98}... | collective-permute-start | bytes 1327112 | tf_op jit(solution)/shard_map/ppermute | solution.py:470
  84.2 26.1 %collective-permute-start.15 = (bf16[28,32,128]{2,1,0:T(8,128)(2,1)}, bf16[28,32,128]{2,1,0:T(8,128)(2,1)}, u32[]{:S(2)}, u32[]{:S(2)}) collective-permute-start(bf16[28,32,128]{2,1,0:T(8,128)(2,1)} %get-tuple-element.61.refs_0_), channel_id=1, source_target_pairs={{0,32},{32,64},{64,96},{96,0},{1,33},{33,65},{65,97},{97,1},{2,34}... | collective-permute-start | bytes 688136 | tf_op jit(solution)/shard_map/ppermute | solution.py:466
  89.1 21.2 %collective-permute-start.12 = (bf16[28,32,128]{2,1,0:T(8,128)(2,1)}, bf16[28,32,128]{2,1,0:T(8,128)(2,1)S(1)}, u32[]{:S(2)}, u32[]{:S(2)}) collective-permute-start(bf16[28,32,128]{2,1,0:T(8,128)(2,1)} %get-tuple-element.61.refs_0_), channel_id=1, source_target_pairs={{0,96},{32,0},{64,32},{96,64},{1,97},{33,1},{65,33},{97,65},{2,98}... | collective-permute-start | bytes 688136 | tf_op jit(solution)/shard_map/ppermute | solution.py:470
  92.8 18.2 %collective-permute-start.14 = (bf16[28,32,128]{2,1,0:T(8,128)(2,1)}, bf16[28,32,128]{2,1,0:T(8,128)(2,1)}, u32[]{:S(2)}, u32[]{:S(2)}) collective-permute-start(bf16[28,32,128]{2,1,0:T(8,128)(2,1)} %get-tuple-element.62.refs_1_), channel_id=1, source_target_pairs={{0,32},{32,64},{64,96},{96,0},{1,33},{33,65},{65,97},{97,1},{2,34}... | collective-permute-start | bytes 688136 | tf_op jit(solution)/shard_map/ppermute | solution.py:466
  102.3 10.7 %collective-permute-start.13 = (bf16[28,32,128]{2,1,0:T(8,128)(2,1)}, bf16[28,32,128]{2,1,0:T(8,128)(2,1)}, u32[]{:S(2)}, u32[]{:S(2)}) collective-permute-start(bf16[28,32,128]{2,1,0:T(8,128)(2,1)} %get-tuple-element.62.refs_1_), channel_id=1, source_target_pairs={{0,96},{32,0},{64,32},{96,64},{1,97},{33,1},{65,33},{97,65},{2,98}... | collective-permute-start | bytes 688136 | tf_op jit(solution)/shard_map/ppermute | solution.py:470
  104.6 9.7 %copy-start.10 = (f32[32,128]{1,0:T(8,128)S(1)}, f32[32,128]{1,0:T(8,128)}, u32[]{:S(2)}) copy-start(f32[32,128]{1,0:T(8,128)} %get-tuple-element.70) | copy-start | bytes 49156
  110.3 0.7 copy-start.5
  111.0 7.9 %collective-permute-start.16 = (bf16[28,32,128]{2,1,0:T(8,128)(2,1)}, bf16[28,32,128]{2,1,0:T(8,128)(2,1)S(1)}, u32[]{:S(2)}, u32[]{:S(2)}) collective-permute-start(bf16[28,32,128]{2,1,0:T(8,128)(2,1)} %shard_map.117.refs_6_), channel_id=1, source_target_pairs={{0,32},{32,64},{64,96},{96,0},{1,33},{33,65},{65,97},{97,1},{2,34}... | collective-permute-start | bytes 688136 | tf_op jit(solution)/shard_map/ppermute | solution.py:466
  113.0 6.3 %collective-permute-start.17 = (bf16[28,32,128]{2,1,0:T(8,128)(2,1)}, bf16[28,32,128]{2,1,0:T(8,128)(2,1)}, u32[]{:S(2)}, u32[]{:S(2)}) collective-permute-start(bf16[28,32,128]{2,1,0:T(8,128)(2,1)} %shard_map.116.refs_3_), channel_id=1, source_target_pairs={{0,96},{32,0},{64,32},{96,64},{1,97},{33,1},{65,33},{97,65},{2,98}... | collective-permute-start | bytes 688136 | tf_op jit(solution)/shard_map/ppermute | solution.py:470
  118.9 0.7 copy-start.8

commit v7 on v6

--- a/solution.py
+++ b/solution.py
@@ -476,12 +476,6 @@
     return (first_up, second_down), ((first, second), (first_down, second_down), (upward(first_up), downward(second_down)), (first_up, second_up))
 
 
-def along_z_in_turn(first, second):
-    near = (upward(first), downward(second), downward(first), upward(second))
-    first_up, second_down = after(near[0], near[2:]), after(near[1], near[2:])
-    return ((first, second), (near[2], second_down), (upward(first_up), downward(second_down)), (first_up, near[3]))
-
-
 def exchange_again(ticket, m_payload, w_payload, w_whole):
     *m_own, kept_w, kept_m, _, _ = pack_moment(FULL[0], ticket, m_payload)
     written_moment = unpack(kept_m, along_z(*m_own)[1])
@@ -500,7 +494,7 @@
     m_near, m_parts = along_z(*m_own)
     w_whole = regroup(after(w_whole, (w_payload, *m_near)))
     *w_own, w_scales = pack_weight(USUAL[1], kept_w, w_payload)
-    w_parts = along_z_in_turn(*w_own)
+    w_parts = along_z(*w_own)[1]
     written_moment = unpack(kept_m, m_parts)
     written_weight = unpack(kept_w, w_parts, w_whole)
 

time: 126 us -> 127 us (level)
  starting transfers between devices: 40.5 us -> 42.6 us
    ppermute x6, waiting for transfers between devices: 24.8 us -> 22.2 us  [upward(): return lax.ppermute(values, 'replica', [(i, (i + 1) % 4) for i in range(4)])]
    ppermute x6, starting transfers between devices: 13.7 us -> 15.7 us  [downward(): return lax.ppermute(values, 'replica', [(i, (i - 1) % 4) for i in range(4)])]
    ppermute x6, waiting for transfers between devices: 5.21 us -> 6.85 us  [downward(): return lax.ppermute(values, 'replica', [(i, (i - 1) % 4) for i in range(4)])]
where the time goes in v7:
time: 127 us; the launch traced here: 126 us
  starting transfers between devices  42.6 us (34%)
  waiting for transfers between devices  39.7 us (31%)
  Pallas kernels  39.6 us (31%)
  other arithmetic  2.03 us (2%)
  between operations  1.54 us (1%)
    all_to_all x3, starting transfers between devices, regroup(): lax.all_to_all(values, 'fsdp', split_axis=0, concat_axis=0, tiled=True)  22.8 us
    ppermute x6, waiting for transfers between devices, upward(): return lax.ppermute(values, 'replica', [(i, (i + 1) % 4) for i in range(4)])  22.2 us
    pallas_call x1, Pallas kernels, weight_call(): pl.pallas_call(functools.partial(weight_kernel, blocks), grid_spec=pltpu....  17.4 us
    ppermute x6, starting transfers between devices, downward(): return lax.ppermute(values, 'replica', [(i, (i - 1) % 4) for i in range(4)])  15.7 us
    pallas_call x2, Pallas kernels, unpack(): pl.pallas_call(functools.partial(unpack_kernel, n_whole, sizes), in_specs...  11.1 us
    all_to_all x3, waiting for transfers between devices, regroup(): lax.all_to_all(values, 'fsdp', split_axis=0, concat_axis=0, tiled=True)  10.6 us
    ppermute x6, waiting for transfers between devices, downward(): return lax.ppermute(values, 'replica', [(i, (i - 1) % 4) for i in range(4)])  6.85 us
    pallas_call x1, Pallas kernels, moment_call(): pl.pallas_call(moment_kernel, in_specs=[HBM] * 4, out_shape=jax.ShapeDtyp...  5.11 us
  transfers between devices with their start and end apart: 15, of which 8 were waited for; matrix products, arithmetic and copies ran while one was open for 2% of the time, Pallas kernels for 23%

profile of v7, /device:TPU:2, one launch (start us, length us, event | category | flops | bytes accessed | tf_op | source)
XLA Modules:
  0.0 126.0 jit_solution(5102822371269200676)
XLA Ops:
  0.6 5.1 %shard_map.111 = bf16[8704,128]{1,0:T(8,128)(2,1)} custom-call(s32[128]{0:T(128)} %bitcast.27, s32[128]{0:T(128)} %weight_mask.1, s32[128]{0:T(128)} %moment_mask_in.1, f32[128,128,128]{2,1,0:T(8,128)} %moment.1), custom_call_target="tpu_custom_call" | custom-call | flops 10485760 | bytes 12582912 | tf_op jit(solution)/shard_map/pallas_call | solution.py:175
  5.7 7.6 %all-to-all-start = ((bf16[32,272,128]{2,1,0:T(8,128)(2,1)}), bf16[32,272,128]{2,1,0:T(8,128)(2,1)S(1)}, u32[]{:S(2)}, u32[]{:S(2)}) async-start(bf16[32,272,128]{2,1,0:T(8,128)(2,1)} %bitcast.23), calls=%async_computation | async-start | bytes 4456448 | tf_op jit(solution)/shard_map/all_to_all | solution.py:462
  13.4 17.4 %shard_map.113 = (bf16[5632,128]{1,0:T(8,128)(2,1)}, bf16[96,128,128]{2,1,0:T(8,128)(2,1)}, bf16[128,128,128]{2,1,0:T(8,128)(2,1)}) custom-call(s32[128]{0:T(128)} %bitcast.28, s32[128]{0:T(128)} %weight_mask.1, f32[128]{0:T(128)} %base_scale.1, f32[128,128,128]{2,1,0:T(8,128)} %weight.1, s32[128,128,128]{2,1,0:T(8,128)} %codes.1), custom_call_target="tpu_custom_call" | custom-call | flops 20971520 | bytes 29360128 | tf_op jit(solution)/shard_map/pallas_call | solution.py:200
  30.8 9.9 %all-to-all-done.payload = bf16[32,272,128]{2,1,0:T(8,128)(2,1)S(1)} async-done(((bf16[32,272,128]{2,1,0:T(8,128)(2,1)}), bf16[32,272,128]{2,1,0:T(8,128)(2,1)S(1)}, u32[]{:S(2)}, u32[]{:S(2)}) %all-to-all-start) | async-done | bytes 2228256 | tf_op jit(solution)/shard_map/all_to_all | solution.py:462
  40.8 7.6 %all-to-all-start.1 = ((bf16[32,176,128]{2,1,0:T(8,128)(2,1)}), bf16[32,176,128]{2,1,0:T(8,128)(2,1)}, u32[]{:S(2)}, u32[]{:S(2)}) async-start(bf16[32,176,128]{2,1,0:T(8,128)(2,1)} %bitcast.26), calls=%async_computation.1 | async-start | bytes 2883584 | tf_op jit(solution)/shard_map/all_to_all | solution.py:462
  48.3 3.3 %shard_map.112 = (bf16[54,32,128]{2,1,0:T(8,128)(2,1)}, bf16[54,32,128]{2,1,0:T(8,128)(2,1)}, s32[32,128]{1,0:T(8,128)}, s32[32,128]{1,0:T(8,128)}, f32[8,128]{1,0:T(8,128)}, /*index=5*/f32[32,128]{1,0:T(8,128)}) custom-call(s32[1]{0:T(128)} %constant.3.clone.1.ticket, bf16[32,272,128]{2,1,0:T(8,128)(2,1)S(1)} %all-to-all-done.payload), custom_call_target="tpu_custom_call" | custom-call | tf_op jit(solution)/shard_map/pallas_call | solution.py:296
  51.6 2.0 %collective-permute-start.18 = (bf16[54,32,128]{2,1,0:T(8,128)(2,1)}, bf16[54,32,128]{2,1,0:T(8,128)(2,1)S(1)}, u32[]{:S(2)}, u32[]{:S(2)}) collective-permute-start(bf16[54,32,128]{2,1,0:T(8,128)(2,1)} %get-tuple-element.64.refs_0_), channel_id=1, source_target_pairs={{0,32},{32,64},{64,96},{96,0},{1,33},{33,65},{65,97},{97,1},{2,34}... | collective-permute-start | bytes 1327112 | tf_op jit(solution)/shard_map/ppermute | solution.py:466
  53.6 2.2 %collective-permute-start.19 = (bf16[54,32,128]{2,1,0:T(8,128)(2,1)}, bf16[54,32,128]{2,1,0:T(8,128)(2,1)S(1)}, u32[]{:S(2)}, u32[]{:S(2)}) collective-permute-start(bf16[54,32,128]{2,1,0:T(8,128)(2,1)} %get-tuple-element.65.refs_1_), channel_id=1, source_target_pairs={{0,96},{32,0},{64,32},{96,64},{1,97},{33,1},{65,33},{97,65},{2,98}... | collective-permute-start | bytes 1327112 | tf_op jit(solution)/shard_map/ppermute | solution.py:470
  55.8 10.6 %collective-permute-done.18.refs_2_.refs_6_ = bf16[54,32,128]{2,1,0:T(8,128)(2,1)S(1)} collective-permute-done((bf16[54,32,128]{2,1,0:T(8,128)(2,1)}, bf16[54,32,128]{2,1,0:T(8,128)(2,1)S(1)}, u32[]{:S(2)}, u32[]{:S(2)}) %collective-permute-start.18) | collective-permute-done | bytes 442400 | tf_op jit(solution)/shard_map/ppermute | solution.py:466
  66.4 0.7 all-to-all-done.1.payload
  67.2 0.2 copy-done.6
  67.4 7.6 %all-to-all-start.2 = ((bf16[96,128,128]{2,1,0:T(8,128)(2,1)}), bf16[96,128,128]{2,1,0:T(8,128)(2,1)S(1)}, u32[]{:S(2)}, u32[]{:S(2)}) async-start(bf16[96,128,128]{2,1,0:T(8,128)(2,1)} %shard_map.116), calls=%async_computation.2 | async-start | bytes 6291456 | tf_op jit(solution)/shard_map/all_to_all | solution.py:462
  75.0 3.3 %collective-permute-start.20 = (bf16[54,32,128]{2,1,0:T(8,128)(2,1)}, bf16[54,32,128]{2,1,0:T(8,128)(2,1)}, u32[]{:S(2)}, u32[]{:S(2)}) collective-permute-start(bf16[54,32,128]{2,1,0:T(8,128)(2,1)} %get-tuple-element.64.refs_0_), channel_id=1, source_target_pairs={{0,96},{32,0},{64,32},{96,64},{1,97},{33,1},{65,33},{97,65},{2,98}... | collective-permute-start | bytes 1327112 | tf_op jit(solution)/shard_map/ppermute | solution.py:470
  78.2 3.3 %collective-permute-start.22 = (bf16[54,32,128]{2,1,0:T(8,128)(2,1)}, bf16[54,32,128]{2,1,0:T(8,128)(2,1)}, u32[]{:S(2)}, u32[]{:S(2)}) collective-permute-start(bf16[54,32,128]{2,1,0:T(8,128)(2,1)} %copy-done.6), channel_id=1, source_target_pairs={{0,96},{32,0},{64,32},{96,64},{1,97},{33,1},{65,33},{97,65},{2,98}... | collective-permute-start | bytes 1327112 | tf_op jit(solution)/shard_map/ppermute | solution.py:470
  81.5 2.6 %shard_map.115 = (bf16[28,32,128]{2,1,0:T(8,128)(2,1)}, bf16[28,32,128]{2,1,0:T(8,128)(2,1)}, f32[32,128]{1,0:T(8,128)}) custom-call(s32[32,128]{1,0:T(8,128)} %get-tuple-element.59.kept_in, bf16[32,176,128]{2,1,0:T(8,128)(2,1)} %all-to-all-done.1.payload), custom_call_target="tpu_custom_call" | custom-call | tf_op jit(solution)/shard_map/pallas_call | solution.py:340
  84.2 0.1 collective-permute-start.14
  84.2 4.8 %collective-permute-done.20.refs_2_ = bf16[54,32,128]{2,1,0:T(8,128)(2,1)} collective-permute-done((bf16[54,32,128]{2,1,0:T(8,128)(2,1)}, bf16[54,32,128]{2,1,0:T(8,128)(2,1)}, u32[]{:S(2)}, u32[]{:S(2)}) %collective-permute-start.20) | collective-permute-done | bytes 442400 | tf_op jit(solution)/shard_map/ppermute | solution.py:470
  89.1 3.7 %collective-permute-start.13 = (bf16[28,32,128]{2,1,0:T(8,128)(2,1)}, bf16[28,32,128]{2,1,0:T(8,128)(2,1)}, u32[]{:S(2)}, u32[]{:S(2)}) collective-permute-start(bf16[28,32,128]{2,1,0:T(8,128)(2,1)} %get-tuple-element.62.refs_1_), channel_id=1, source_target_pairs={{0,96},{32,0},{64,32},{96,64},{1,97},{33,1},{65,33},{97,65},{2,98}... | collective-permute-start | bytes 688136 | tf_op jit(solution)/shard_map/ppermute | solution.py:470
  92.8 1.4 %compare_reduce_fusion = pred[]{:T(512)} fusion(f32[8,128]{1,0:T(8,128)} %get-tuple-element.67, f32[2]{0:T(128)S(1)} %copy-done.10), kind=kLoop, calls=%fused_computation.5 | loop fusion | flops 127 | bytes 265 | tf_op jit(solution)/shard_map/reduce_or | solution.py:501
  94.8 0.1 copy.16
  94.9 7.4 %collective-permute-done.21.refs_4_ = bf16[54,32,128]{2,1,0:T(8,128)(2,1)} collective-permute-done((bf16[54,32,128]{2,1,0:T(8,128)(2,1)}, bf16[54,32,128]{2,1,0:T(8,128)(2,1)}, u32[]{:S(2)}, u32[]{:S(2)}) %collective-permute-start.21) | collective-permute-done | bytes 442400 | tf_op jit(solution)/shard_map/ppermute | solution.py:466
  102.3 5.7 %shard_map.118 = bf16[256,128,128]{2,1,0:T(8,128)(2,1)} custom-call(s32[32,128]{1,0:T(8,128)} %get-tuple-element.66.kept_in, bf16[54,32,128]{2,1,0:T(8,128)(2,1)} %get-tuple-element.64.refs_0_, bf16[54,32,128]{2,1,0:T(8,128)(2,1)} %get-tuple-element.65.refs_1_, bf16[54,32,128]{2,1,0:T(8,128)(2,1)} %collective-permute-done.20.refs_2_, ...), custom_call_target="tpu_custom_call" | custom-call | tf_op jit(solution)/shard_map/pallas_call | solution.py:443
  108.0 0.1 collective-permute-start.12
  108.1 2.0 %collective-permute-start.17 = (bf16[28,32,128]{2,1,0:T(8,128)(2,1)}, bf16[28,32,128]{2,1,0:T(8,128)(2,1)}, u32[]{:S(2)}, u32[]{:S(2)}) collective-permute-start(bf16[28,32,128]{2,1,0:T(8,128)(2,1)} %get-tuple-element.62.refs_1_), channel_id=1, source_target_pairs={{0,32},{32,64},{64,96},{96,0},{1,33},{33,65},{65,97},{97,1},{2,34}... | collective-permute-start | bytes 688136 | tf_op jit(solution)/shard_map/ppermute | solution.py:466
  110.2 3.2 %collective-permute-start.16 = (bf16[28,32,128]{2,1,0:T(8,128)(2,1)}, bf16[28,32,128]{2,1,0:T(8,128)(2,1)}, u32[]{:S(2)}, u32[]{:S(2)}) collective-permute-start(bf16[28,32,128]{2,1,0:T(8,128)(2,1)} %collective-permute-done.13.refs_3_), channel_id=1, source_target_pairs={{0,96},{32,0},{64,32},{96,64},{1,97},{33,1},{65,33},{97,65},{2,98}... | collective-permute-start | bytes 688136 | tf_op jit(solution)/shard_map/ppermute | solution.py:470
  113.4 0.1 copy.15
  113.5 0.6 pad_maximum_fusion
  114.1 2.0 %collective-permute-done.12.refs_2_ = bf16[28,32,128]{2,1,0:T(8,128)(2,1)} collective-permute-done((bf16[28,32,128]{2,1,0:T(8,128)(2,1)S(1)}, bf16[28,32,128]{2,1,0:T(8,128)(2,1)}, u32[]{:S(2)}, u32[]{:S(2)}) %collective-permute-start.12) | collective-permute-done | bytes 229408 | tf_op jit(solution)/shard_map/ppermute | solution.py:470
  116.1 1.7 %collective-permute-done.17.refs_7_ = bf16[28,32,128]{2,1,0:T(8,128)(2,1)} collective-permute-done((bf16[28,32,128]{2,1,0:T(8,128)(2,1)}, bf16[28,32,128]{2,1,0:T(8,128)(2,1)}, u32[]{:S(2)}, u32[]{:S(2)}) %collective-permute-start.17) | collective-permute-done | bytes 229408 | tf_op jit(solution)/shard_map/ppermute | solution.py:466
  117.8 2.5 %collective-permute-done.15.refs_4_ = bf16[28,32,128]{2,1,0:T(8,128)(2,1)} collective-permute-done((bf16[28,32,128]{2,1,0:T(8,128)(2,1)}, bf16[28,32,128]{2,1,0:T(8,128)(2,1)}, u32[]{:S(2)}, u32[]{:S(2)}) %collective-permute-start.15) | collective-permute-done | bytes 229408 | tf_op jit(solution)/shard_map/ppermute | solution.py:466
  120.3 5.4 %shard_map.117 = bf16[256,128,128]{2,1,0:T(8,128)(2,1)} custom-call(s32[32,128]{1,0:T(8,128)} %get-tuple-element.59.kept_in, bf16[28,32,128]{2,1,0:T(8,128)(2,1)} %get-tuple-element.61.refs_0_, bf16[28,32,128]{2,1,0:T(8,128)(2,1)} %get-tuple-element.62.refs_1_, bf16[28,32,128]{2,1,0:T(8,128)(2,1)} %collective-permute-done.12.refs_2_, ...), custom_call_target="tpu_custom_call" | custom-call | tf_op jit(solution)/shard_map/pallas_call | solution.py:443
  125.6 0.2 while.12
  (27 shorter events, 0.1 us)
Async XLA Ops:
  5.7 35.0 %all-to-all-start = ((bf16[32,272,128]{2,1,0:T(8,128)(2,1)}), bf16[32,272,128]{2,1,0:T(8,128)(2,1)S(1)}, u32[]{:S(2)}, u32[]{:S(2)}) async-start(bf16[32,272,128]{2,1,0:T(8,128)(2,1)} %bitcast.23), calls=%async_computation | async-start | bytes 4456448 | tf_op jit(solution)/shard_map/all_to_all | solution.py:462
  40.8 7.6 %copy-start = (bf16[32,272,128]{2,1,0:T(8,128)(2,1)}, bf16[32,272,128]{2,1,0:T(8,128)(2,1)S(1)}, u32[]{:S(2)}) copy-start(bf16[32,272,128]{2,1,0:T(8,128)(2,1)S(1)} %all-to-all-done.payload) | copy-start | bytes 6684676
  40.8 26.4 %all-to-all-start.1 = ((bf16[32,176,128]{2,1,0:T(8,128)(2,1)}), bf16[32,176,128]{2,1,0:T(8,128)(2,1)}, u32[]{:S(2)}, u32[]{:S(2)}) async-start(bf16[32,176,128]{2,1,0:T(8,128)(2,1)} %bitcast.26), calls=%async_computation.1 | async-start | bytes 2883584 | tf_op jit(solution)/shard_map/all_to_all | solution.py:462
  51.6 14.8 %collective-permute-start.18 = (bf16[54,32,128]{2,1,0:T(8,128)(2,1)}, bf16[54,32,128]{2,1,0:T(8,128)(2,1)S(1)}, u32[]{:S(2)}, u32[]{:S(2)}) collective-permute-start(bf16[54,32,128]{2,1,0:T(8,128)(2,1)} %get-tuple-element.64.refs_0_), channel_id=1, source_target_pairs={{0,32},{32,64},{64,96},{96,0},{1,33},{33,65},{65,97},{97,1},{2,34}... | collective-permute-start | bytes 1327112 | tf_op jit(solution)/shard_map/ppermute | solution.py:466
  53.6 12.8 %collective-permute-start.19 = (bf16[54,32,128]{2,1,0:T(8,128)(2,1)}, bf16[54,32,128]{2,1,0:T(8,128)(2,1)S(1)}, u32[]{:S(2)}, u32[]{:S(2)}) collective-permute-start(bf16[54,32,128]{2,1,0:T(8,128)(2,1)} %get-tuple-element.65.refs_1_), channel_id=1, source_target_pairs={{0,96},{32,0},{64,32},{96,64},{1,97},{33,1},{65,33},{97,65},{2,98}... | collective-permute-start | bytes 1327112 | tf_op jit(solution)/shard_map/ppermute | solution.py:470
  66.4 0.8 copy-start.5
  66.4 0.9 copy-start.6
  67.4 25.4 %copy-start.10 = (f32[2]{0:T(128)S(1)}, f32[2]{0:T(128)}, u32[]{:S(2)}) copy-start(f32[2]{0:T(128)} %constant.11) | copy-start | bytes 28
  67.4 27.4 %copy-start.8 = (f32[32,128]{1,0:T(8,128)S(1)}, f32[32,128]{1,0:T(8,128)}, u32[]{:S(2)}) copy-start(f32[32,128]{1,0:T(8,128)} %get-tuple-element.71) | copy-start | bytes 49156
  67.4 52.9 %all-to-all-start.2 = ((bf16[96,128,128]{2,1,0:T(8,128)(2,1)}), bf16[96,128,128]{2,1,0:T(8,128)(2,1)S(1)}, u32[]{:S(2)}, u32[]{:S(2)}) async-start(bf16[96,128,128]{2,1,0:T(8,128)(2,1)} %shard_map.116), calls=%async_computation.2 | async-start | bytes 6291456 | tf_op jit(solution)/shard_map/all_to_all | solution.py:462
  75.0 14.1 %collective-permute-start.20 = (bf16[54,32,128]{2,1,0:T(8,128)(2,1)}, bf16[54,32,128]{2,1,0:T(8,128)(2,1)}, u32[]{:S(2)}, u32[]{:S(2)}) collective-permute-start(bf16[54,32,128]{2,1,0:T(8,128)(2,1)} %get-tuple-element.64.refs_0_), channel_id=1, source_target_pairs={{0,96},{32,0},{64,32},{96,64},{1,97},{33,1},{65,33},{97,65},{2,98}... | collective-permute-start | bytes 1327112 | tf_op jit(solution)/shard_map/ppermute | solution.py:470
  78.2 16.7 %collective-permute-start.23 = (bf16[54,32,128]{2,1,0:T(8,128)(2,1)}, bf16[54,32,128]{2,1,0:T(8,128)(2,1)}, u32[]{:S(2)}, u32[]{:S(2)}) collective-permute-start(bf16[54,32,128]{2,1,0:T(8,128)(2,1)} %get-tuple-element.65.refs_1_), channel_id=1, source_target_pairs={{0,32},{32,64},{64,96},{96,0},{1,33},{33,65},{65,97},{97,1},{2,34}... | collective-permute-start | bytes 1327112 | tf_op jit(solution)/shard_map/ppermute | solution.py:466
  78.2 24.1 %collective-permute-start.21 = (bf16[54,32,128]{2,1,0:T(8,128)(2,1)}, bf16[54,32,128]{2,1,0:T(8,128)(2,1)}, u32[]{:S(2)}, u32[]{:S(2)}) collective-permute-start(bf16[54,32,128]{2,1,0:T(8,128)(2,1)} %copy-done.5), channel_id=1, source_target_pairs={{0,32},{32,64},{64,96},{96,0},{1,33},{33,65},{65,97},{97,1},{2,34}... | collective-permute-start | bytes 1327112 | tf_op jit(solution)/shard_map/ppermute | solution.py:466
  78.2 24.1 %collective-permute-start.22 = (bf16[54,32,128]{2,1,0:T(8,128)(2,1)}, bf16[54,32,128]{2,1,0:T(8,128)(2,1)}, u32[]{:S(2)}, u32[]{:S(2)}) collective-permute-start(bf16[54,32,128]{2,1,0:T(8,128)(2,1)} %copy-done.6), channel_id=1, source_target_pairs={{0,96},{32,0},{64,32},{96,64},{1,97},{33,1},{65,33},{97,65},{2,98}... | collective-permute-start | bytes 1327112 | tf_op jit(solution)/shard_map/ppermute | solution.py:470
  84.2 26.0 %collective-permute-start.14 = (bf16[28,32,128]{2,1,0:T(8,128)(2,1)}, bf16[28,32,128]{2,1,0:T(8,128)(2,1)}, u32[]{:S(2)}, u32[]{:S(2)}) collective-permute-start(bf16[28,32,128]{2,1,0:T(8,128)(2,1)} %get-tuple-element.61.refs_0_), channel_id=1, source_target_pairs={{0,32},{32,64},{64,96},{96,0},{1,33},{33,65},{65,97},{97,1},{2,34}... | collective-permute-start | bytes 688136 | tf_op jit(solution)/shard_map/ppermute | solution.py:466
  89.1 21.1 %collective-permute-start.13 = (bf16[28,32,128]{2,1,0:T(8,128)(2,1)}, bf16[28,32,128]{2,1,0:T(8,128)(2,1)}, u32[]{:S(2)}, u32[]{:S(2)}) collective-permute-start(bf16[28,32,128]{2,1,0:T(8,128)(2,1)} %get-tuple-element.62.refs_1_), channel_id=1, source_target_pairs={{0,96},{32,0},{64,32},{96,64},{1,97},{33,1},{65,33},{97,65},{2,98}... | collective-permute-start | bytes 688136 | tf_op jit(solution)/shard_map/ppermute | solution.py:470
  102.3 5.7 %copy-start.7 = (bf16[28,32,128]{2,1,0:T(8,128)(2,1)S(1)}, bf16[28,32,128]{2,1,0:T(8,128)(2,1)}, u32[]{:S(2)}) copy-start(bf16[28,32,128]{2,1,0:T(8,128)(2,1)} %get-tuple-element.61.refs_0_) | copy-start | bytes 688132
  102.3 11.1 %copy-start.9 = (f32[32,128]{1,0:T(8,128)S(1)}, f32[32,128]{1,0:T(8,128)}, u32[]{:S(2)}) copy-start(f32[32,128]{1,0:T(8,128)} %get-tuple-element.70) | copy-start | bytes 49156
  108.0 8.0 %collective-permute-start.12 = (bf16[28,32,128]{2,1,0:T(8,128)(2,1)S(1)}, bf16[28,32,128]{2,1,0:T(8,128)(2,1)}, u32[]{:S(2)}, u32[]{:S(2)}) collective-permute-start(bf16[28,32,128]{2,1,0:T(8,128)(2,1)S(1)} %copy-done.7), channel_id=1, source_target_pairs={{0,96},{32,0},{64,32},{96,64},{1,97},{33,1},{65,33},{97,65},{2,98}... | collective-permute-start | bytes 688136 | tf_op jit(solution)/shard_map/ppermute | solution.py:470
  108.1 9.7 %collective-permute-start.17 = (bf16[28,32,128]{2,1,0:T(8,128)(2,1)}, bf16[28,32,128]{2,1,0:T(8,128)(2,1)}, u32[]{:S(2)}, u32[]{:S(2)}) collective-permute-start(bf16[28,32,128]{2,1,0:T(8,128)(2,1)} %get-tuple-element.62.refs_1_), channel_id=1, source_target_pairs={{0,32},{32,64},{64,96},{96,0},{1,33},{33,65},{65,97},{97,1},{2,34}... | collective-permute-start | bytes 688136 | tf_op jit(solution)/shard_map/ppermute | solution.py:466
  110.1 10.1 %collective-permute-start.15 = (bf16[28,32,128]{2,1,0:T(8,128)(2,1)}, bf16[28,32,128]{2,1,0:T(8,128)(2,1)}, u32[]{:S(2)}, u32[]{:S(2)}) collective-permute-start(bf16[28,32,128]{2,1,0:T(8,128)(2,1)} %collective-permute-done.14.refs_6_), channel_id=1, source_target_pairs={{0,32},{32,64},{64,96},{96,0},{1,33},{33,65},{65,97},{97,1},{2,34}... | collective-permute-start | bytes 688136 | tf_op jit(solution)/shard_map/ppermute | solution.py:466
  110.2 10.1 %collective-permute-start.16 = (bf16[28,32,128]{2,1,0:T(8,128)(2,1)}, bf16[28,32,128]{2,1,0:T(8,128)(2,1)}, u32[]{:S(2)}, u32[]{:S(2)}) collective-permute-start(bf16[28,32,128]{2,1,0:T(8,128)(2,1)} %collective-permute-done.13.refs_3_), channel_id=1, source_target_pairs={{0,96},{32,0},{64,32},{96,64},{1,97},{33,1},{65,33},{97,65},{2,98}... | collective-permute-start | bytes 688136 | tf_op jit(solution)/shard_map/ppermute | solution.py:470
